TPU v7x, 32 devices: a whole 2x2x4 slice. The times are simulated.
32 devices in a mesh: tm: 2 (over x), row: 16 (over z, y, core).
Axes of the slice: x: 2, y: 2, z: 4, core: 2. Of those that a mesh axis runs over, the one named last changes fastest.
Arguments:
- snapshots: float32 [16384, 256], P('row', 'tm'), may hold values from -6 to 6
- sketches: float32 [1, 256, 128], replicated, may hold values from -0.375 to 0.375
Outputs:
- coefficients: float32 [128, 256], P(None, 'tm')
- deflated: float32 [16384, 256], P('row', 'tm')
All inputs are finite; a program needn't handle non-finite values.
Results may differ from a plain program's by a relative error of at most 0.00024.
Values sent between devices are 32-bit elements; how exact they have to be, the bound alone decides.
No kernel may reach another device: no remote copies, remote signals or barrier semaphores. Data moves between devices by JAX's collectives and lax.ppermute only.
A program may use at most 64 MiB of HBM per device.

v0:
```python
import jax
import jax.numpy as jnp
from jax import lax
from jax.sharding import PartitionSpec as P

NS_STEPS = 5


HIGH = lax.Precision.HIGHEST


def passed_along(block, axis, distance):
    devices = range(lax.axis_size(axis))
    route = [((i - distance) % len(devices), i) for i in devices]
    return lax.ppermute(block, axis, route)


def product_t(left, right):
    return jnp.dot(left.T, right, precision=HIGH, preferred_element_type=jnp.float32)


def product(left, right):
    return jnp.dot(left, right, precision=HIGH, preferred_element_type=jnp.float32)


def inverse_root(matrix):
    frob_scale = jnp.sqrt(jnp.sum(matrix * matrix) + 1e-06)
    ident = jnp.eye(matrix.shape[0], dtype=matrix.dtype)
    y_iter = matrix / frob_scale
    z_iter = ident
    for repeat in range(NS_STEPS):
        middle = 1.5 * ident - 0.5 * product(z_iter, y_iter)
        y_iter = product(y_iter, middle)
        z_iter = product(middle, z_iter)
    return z_iter / jnp.sqrt(frob_scale)


def body(snapshots, sketches):
    leaf_sum = lax.psum(product_t(snapshots, snapshots), "row")
    leaf_root = inverse_root(leaf_sum)
    mode_block = product(snapshots, leaf_root)
    own_gram = product_t(leaf_root, product(leaf_sum, leaf_root))
    group_count = lax.axis_size("tm")
    tree_depth = group_count.bit_length() - 1
    for tree_level in range(tree_depth):
        sketch = sketches[tree_level]
        lower_block, lower_gram = passed_along((mode_block, own_gram), "tm", 1 << tree_level)
        cross_sum = lax.psum(product_t(lower_block, mode_block), "row")
        top_rows = jnp.concatenate([lower_gram, cross_sum], axis=1)
        bottom_rows = jnp.concatenate([cross_sum.T, own_gram], axis=1)
        gram_sum = jnp.concatenate([top_rows, bottom_rows], axis=0)
        joined = jnp.concatenate([lower_block, mode_block], axis=1)
        reduced = product(gram_sum, sketch)
        small = product_t(reduced, product(gram_sum, reduced))
        mixing = product(reduced, inverse_root(small))
        mode_block = product(joined, mixing)
        own_gram = product_t(mixing, product(gram_sum, mixing))
    coefficients = lax.psum(product_t(mode_block, snapshots), "row")
    deflated = snapshots - product(mode_block, coefficients)
    return (coefficients, deflated)


def solution(mesh):
    placed = (P("row", "tm"), P())
    return jax.shard_map(
        body, mesh=mesh, in_specs=placed, out_specs=(P(None, "tm"), P("row", "tm")), check_vma=False
    )
```

profile of v0, /device:TPU:0, one launch (start us, length us, event | category | flops | bytes accessed | tf_op | source)
XLA Modules:
  0.0 311.3 jit_solution(16994604468315279436)
XLA Ops:
  7.2 3.0 fusion.24
  10.2 89.0 %all-reduce.4.cloned.1.call-done = f32[128,128]{1,0:T(8,128)} async-done(((f32[128,128]{1,0:T(8,128)}), f32[128,128]{1,0:T(8,128)}) %all-reduce.4.cloned.1.call-update) | async-done | bytes 65552 | tf_op jit(solution)/shard_map/psum | solution.py:39
  99.3 1.5 multiply_reduce_fusion.1
  102.1 0.2 fusion.8
  102.8 0.2 fusion.7
  104.5 0.7 fusion.31
  105.1 1.5 collective-permute-start
  106.9 0.3 fusion.33
  107.2 0.6 collective-permute-start.1
  107.8 12.2 %collective-permute-done = f32[1024,128]{0,1:T(8,128)S(1)} collective-permute-done((f32[1024,128]{0,1:T(8,128)S(1)}, f32[1024,128]{0,1:T(8,128)S(1)}, u32[]{:S(2)}, u32[]{:S(2)}) %collective-permute-start) | collective-permute-done | bytes 524320 | tf_op jit(solution)/shard_map/ppermute | solution.py:15
  120.0 1.2 fusion.34
  121.2 83.8 %all-reduce.6.cloned.1.call-done = f32[128,128]{0,1:T(8,128)} async-done(((f32[128,128]{0,1:T(8,128)}), f32[128,128]{0,1:T(8,128)}) %all-reduce.6.cloned.1.call-update) | async-done | bytes 65552 | tf_op jit(solution)/shard_map/psum | solution.py:48
  205.0 1.0 copy.5
  206.0 0.6 fusion.15
  206.6 0.6 fusion.14
  207.2 1.0 multiply_reduce_fusion
  209.6 0.2 fusion.3
  210.8 0.2 fusion.1
  211.9 0.3 fusion.41
  212.2 1.8 fusion.10
  214.0 1.6 fusion.42
  215.6 86.2 %all-reduce.8.cloned.1.call-done = f32[128,128]{1,0:T(8,128)} async-done(((f32[128,128]{1,0:T(8,128)}), f32[128,128]{1,0:T(8,128)}) %all-reduce.8.cloned.1.call-update) | async-done | bytes 65552 | tf_op jit(solution)/shard_map/psum | solution.py:58
  301.8 2.3 convolution_subtract_fusion
  304.1 0.6 copy.10
  (42 shorter events, 5.2 us)
Async XLA Ops:
  7.2 198.9 %copy-start = (f32[1,256,128]{2,1,0:T(8,128)S(1)}, f32[1,256,128]{2,1,0:T(8,128)}, u32[]{:S(2)}) copy-start(f32[1,256,128]{2,1,0:T(8,128)} %param.3) | copy-start | bytes 393220
  7.2 92.1 %all-reduce.4.cloned.1.call-start = ((), (), s32[]{:S(2)}) async-start(), calls=%async_computation | async-start | bytes 131072 | tf_op jit(solution)/shard_map/psum | solution.py:39
  10.2 194.8 %all-reduce.6.cloned.1.call-start = ((), (), s32[]{:S(2)}) async-start(), calls=%async_computation.1 | async-start | bytes 131072 | tf_op jit(solution)/shard_map/psum | solution.py:48
  99.3 2.3 copy-start.3
  103.4 1.1 copy-start.1
  105.1 14.8 %collective-permute-start = (f32[1024,128]{0,1:T(8,128)S(1)}, f32[1024,128]{0,1:T(8,128)S(1)}, u32[]{:S(2)}, u32[]{:S(2)}) collective-permute-start(f32[1024,128]{0,1:T(8,128)S(1)} %bitcast.73), channel_id=1, source_target_pairs={{16,0},{0,16},{17,1},{1,17},{18,2},{2,18},{19,3},{3,19},{20,4},{4,... | collective-permute-start | bytes 1572872 | tf_op jit(solution)/shard_map/ppermute | solution.py:15
  107.2 98.8 %collective-permute-start.1 = (f32[128,128]{0,1:T(8,128)S(1)}, f32[128,128]{0,1:T(8,128)S(1)}, u32[]{:S(2)}, u32[]{:S(2)}) collective-permute-start(f32[128,128]{0,1:T(8,128)S(1)} %fusion.33), channel_id=1, source_target_pairs={{16,0},{0,16},{17,1},{1,17},{18,2},{2,18},{19,3},{3,19},{20,4},{4,... | collective-permute-start | bytes 196616 | tf_op jit(solution)/shard_map/ppermute | solution.py:15
  121.2 180.6 %all-reduce.8.cloned.1.call-start = ((), (), s32[]{:S(2)}) async-start(), calls=%async_computation.2 | async-start | bytes 131072 | tf_op jit(solution)/shard_map/psum | solution.py:58
  205.0 1.0 copy-start.2
  301.8 2.3 copy-start.4
Sparse Core Ops, SparseCore 0:
  12.1 87.1 all-reduce.3
  121.3 83.6 all-reduce.5
  215.7 86.0 all-reduce.7
where the time goes:
time: 313 us; the launch traced here: 311 us
  waiting for transfers between devices  271 us (87%)
  matrix products  19.1 us (6%)
  between operations  15.5 us (5%)
    psum x1, waiting for transfers between devices, body(): leaf_sum = lax.psum(product_t(snapshots, snapshots), 'row')  89 us
    psum x1, waiting for transfers between devices, body(): coefficients = lax.psum(product_t(mode_block, snapshots), 'row')  86.2 us
    psum x1, waiting for transfers between devices, body(): cross_sum = lax.psum(product_t(lower_block, mode_block), 'row')  83.8 us
    ppermute x2, waiting for transfers between devices, passed_along(): return lax.ppermute(block, axis, route)  12.2 us
    dot_general x35, matrix products, product(): jnp.dot(left, right, precision=HIGH, preferred_element_type=jnp.float32)  12 us
    dot_general x5, matrix products, product_t(): jnp.dot(left.T, right, precision=HIGH, preferred_element_type=jnp.float32)  7.07 us
  transfers between devices with their start and end apart: 5, of which 4 were waited for; matrix products, arithmetic and copies ran while one was open for 1% of the time, Pallas kernels for 0%

commit v1 on v0

v1 whole, which is shorter than its diff:
```python
import jax
import jax.numpy as jnp
from jax import lax
from jax.sharding import PartitionSpec as P

NS_STEPS = 5


HIGH = lax.Precision.HIGH
HIGHEST = lax.Precision.HIGHEST


def passed_along(block, axis, distance):
    devices = range(lax.axis_size(axis))
    route = [((i - distance) % len(devices), i) for i in devices]
    return lax.ppermute(block, axis, route)


def product_t(left, right, precision=HIGHEST):
    return jnp.dot(left.T, right, precision=precision, preferred_element_type=jnp.float32)


def product(left, right, precision=HIGHEST):
    return jnp.dot(left, right, precision=precision, preferred_element_type=jnp.float32)


def stages_of(size):
    bits = [1 << b for b in range(size.bit_length() - 1)]
    stages = [(bits[0],)] if bits else []
    rest = bits[1:]
    while rest:
        stages.append(tuple(rest[:2]) if len(rest) >= 2 else tuple(rest))
        rest = rest[2:]
    return stages


def row_sum(part, axis="row"):
    size = lax.axis_size(axis)
    if size & (size - 1):
        return lax.psum(part, axis)
    for bits in stages_of(size):
        flips = [bits[0]] if len(bits) == 1 else [bits[0], bits[1], bits[0] | bits[1]]
        others = [lax.ppermute(part, axis, [(i, i ^ flip) for i in range(size)]) for flip in flips]
        if len(others) == 1:
            part = part + others[0]
        else:
            part = (part + others[0]) + (others[1] + others[2])
    return part


def inverse_root(matrix):
    frob_scale = jnp.sqrt(jnp.sum(matrix * matrix) + 1e-06)
    ident = jnp.eye(matrix.shape[0], dtype=matrix.dtype)
    y_iter = matrix / frob_scale
    z_iter = ident
    for repeat in range(NS_STEPS):
        if repeat == 0:
            middle = 1.5 * ident - 0.5 * y_iter
            z_iter = middle
        else:
            middle = 1.5 * ident - 0.5 * product(z_iter, y_iter)
            z_iter = product(middle, z_iter)
        y_iter = product(y_iter, middle)
    return z_iter / jnp.sqrt(frob_scale)


def one_merge(snapshots, sketch):
    modes = snapshots.shape[1]
    lower = passed_along(snapshots, "tm", 1)
    own_gram = row_sum(product_t(snapshots, snapshots, HIGH))
    own_root = inverse_root(own_gram)
    lower_gram, lower_root = passed_along((own_gram, own_root), "tm", 1)
    cross = row_sum(product_t(lower, snapshots, HIGH))
    top, bottom = sketch[:modes], sketch[modes:]
    lower_e, own_e = product(lower_root, top), product(own_root, bottom)
    whole = jnp.concatenate(
        [jnp.concatenate([lower_gram, cross], axis=1), jnp.concatenate([cross.T, own_gram], axis=1)], axis=0
    )
    f = product(whole, jnp.concatenate([lower_e, own_e], axis=0))
    v = jnp.concatenate(
        [
            product(lower_root, product_t(lower_root, f[:modes])),
            product(own_root, product_t(own_root, f[modes:])),
        ],
        axis=0,
    )
    p = product(whole, v)
    root = inverse_root(product_t(v, p))
    coefficients = product_t(root, p[modes:].T)
    mixed = product(v, product(root, coefficients))
    deflated = snapshots - product(lower, mixed[:modes], HIGH) - product(snapshots, mixed[modes:], HIGH)
    return coefficients, deflated


def many_merges(snapshots, sketches, tree_depth):
    leaf_sum = row_sum(product_t(snapshots, snapshots))
    leaf_root = inverse_root(leaf_sum)
    mode_block = product(snapshots, leaf_root)
    own_gram = product_t(leaf_root, product(leaf_sum, leaf_root))
    for tree_level in range(tree_depth):
        sketch = sketches[tree_level]
        lower_block, lower_gram = passed_along((mode_block, own_gram), "tm", 1 << tree_level)
        cross_sum = row_sum(product_t(lower_block, mode_block))
        top_rows = jnp.concatenate([lower_gram, cross_sum], axis=1)
        bottom_rows = jnp.concatenate([cross_sum.T, own_gram], axis=1)
        gram_sum = jnp.concatenate([top_rows, bottom_rows], axis=0)
        joined = jnp.concatenate([lower_block, mode_block], axis=1)
        reduced = product(gram_sum, sketch)
        small = product_t(reduced, product(gram_sum, reduced))
        mixing = product(reduced, inverse_root(small))
        mode_block = product(joined, mixing)
        own_gram = product_t(mixing, product(gram_sum, mixing))
    coefficients = row_sum(product_t(mode_block, snapshots))
    deflated = snapshots - product(mode_block, coefficients)
    return coefficients, deflated


def body(snapshots, sketches):
    tree_depth = lax.axis_size("tm").bit_length() - 1
    if tree_depth == 1:
        return one_merge(snapshots, sketches[0])
    return many_merges(snapshots, sketches, tree_depth)


def solution(mesh):
    placed = (P("row", "tm"), P())
    return jax.shard_map(
        body, mesh=mesh, in_specs=placed, out_specs=(P(None, "tm"), P("row", "tm")), check_vma=False
    )
```

time: 313 us -> 54.3 us (0.17)
  waiting for transfers between devices: 271 us -> 18.3 us
  starting transfers between devices: 2.28 us -> 16.5 us
  between operations: 15.5 us -> 2.44 us
  matrix products: 19.1 us -> 14.4 us
    psum x3 -> x0, waiting for transfers between devices: 259 us -> none  [the longest x1 89 us: body(): leaf_sum = lax.psum(product_t(snapshots, snapshots), 'row')]
    ppermute x0 -> x10, waiting for transfers between devices: none -> 14.1 us  [row_sum(): lax.ppermute(part, axis, [(i, i ^ flip) for i in range(size)])]
    ppermute x0 -> x10, starting transfers between devices: none -> 11.9 us  [row_sum(): lax.ppermute(part, axis, [(i, i ^ flip) for i in range(size)])]
    ppermute x2 -> x3, waiting for transfers between devices: 12.2 us -> 4.2 us  [passed_along(): return lax.ppermute(block, axis, route)]
    dot_general x40, matrix products: 19.1 us -> 14.4 us  [the longest x34 10.1 us: product(): jnp.dot(left, right, precision=precision, preferred_element_type=jnp.floa...]
  transfers between devices with their start and end apart: 5 -> 13, of which waited for: 4 -> 10; matrix products, arithmetic and copies ran while one was open for 1% -> 10% of each run, Pallas kernels for 0% -> 0%
where the time goes in v1:
time: 54.3 us; the launch traced here: 54.1 us
  waiting for transfers between devices  18.3 us (34%)
  starting transfers between devices  16.5 us (30%)
  matrix products  14.4 us (27%)
  between operations  2.44 us (4%)
  local copies, waits for them, and re-layouts  1.79 us (3%)
  other arithmetic  0.68 us (1%)
    ppermute x10, waiting for transfers between devices, row_sum(): lax.ppermute(part, axis, [(i, i ^ flip) for i in range(size)])  14.1 us
    ppermute x10, starting transfers between devices, row_sum(): lax.ppermute(part, axis, [(i, i ^ flip) for i in range(size)])  11.9 us
    dot_general x34, matrix products, product(): jnp.dot(left, right, precision=precision, preferred_element_type=jnp.floa...  10.1 us
    ppermute x3, starting transfers between devices, passed_along(): return lax.ppermute(block, axis, route)  4.6 us
    dot_general x6, matrix products, product_t(): jnp.dot(left.T, right, precision=precision, preferred_element_type=jnp.fl...  4.31 us
    ppermute x3, waiting for transfers between devices, passed_along(): return lax.ppermute(block, axis, route)  4.2 us
    unnamed x8, local copies, waits for them, and re-layouts  1.61 us
  transfers between devices with their start and end apart: 13, of which 10 were waited for; matrix products, arithmetic and copies ran while one was open for 10% of the time, Pallas kernels for 0%

profile of v1, /device:TPU:0, one launch (start us, length us, event | category | flops | bytes accessed | tf_op | source)
XLA Modules:
  0.0 54.1 jit_solution(6113461305160793061)
XLA Ops:
  0.6 1.9 %fusion.75 = f32[128,128]{0,1:T(8,128)S(1)} fusion(f32[1024,128]{1,0:T(8,128)} %param.2), kind=kOutput, calls=%fused_computation.98 | convolution fusion | flops 100663296 | bytes 589824 | tf_op jit(solution)/shard_map/dot_general | solution.py:20
  2.5 0.5 collective-permute-start
  3.0 0.9 %collective-permute-done = f32[128,128]{0,1:T(8,128)S(1)} collective-permute-done((f32[128,128]{0,1:T(8,128)S(1)}, f32[128,128]{0,1:T(8,128)S(1)}, u32[]{:S(2)}, u32[]{:S(2)}) %collective-permute-start) | collective-permute-done | bytes 65568 | tf_op jit(solution)/shard_map/ppermute | solution.py:43
  4.0 3.9 %collective-permute-start.3 = (f32[128,128]{0,1:T(8,128)S(1)}, f32[128,128]{0,1:T(8,128)S(1)}, u32[]{:S(2)}, u32[]{:S(2)}) collective-permute-start(f32[128,128]{0,1:T(8,128)S(1)} %add.36), channel_id=1, source_target_pairs={{0,6},{1,7},{2,4},{3,5},{4,2},{5,3},{6,0},{7,1},{8,14},{9,15},{10,... | collective-permute-start | bytes 196616 | tf_op jit(solution)/shard_map/ppermute | solution.py:43
  8.5 1.8 %collective-permute-done.3 = f32[128,128]{0,1:T(8,128)S(1)} collective-permute-done((f32[128,128]{0,1:T(8,128)S(1)}, f32[128,128]{0,1:T(8,128)S(1)}, u32[]{:S(2)}, u32[]{:S(2)}) %collective-permute-start.3) | collective-permute-done | bytes 65568 | tf_op jit(solution)/shard_map/ppermute | solution.py:43
  10.3 1.9 %collective-permute-done.2 = f32[128,128]{0,1:T(8,128)S(1)} collective-permute-done((f32[128,128]{0,1:T(8,128)S(1)}, f32[128,128]{0,1:T(8,128)S(1)}, u32[]{:S(2)}, u32[]{:S(2)}) %collective-permute-start.2) | collective-permute-done | bytes 65568 | tf_op jit(solution)/shard_map/ppermute | solution.py:43
  12.6 2.7 %collective-permute-start.4 = (f32[128,128]{0,1:T(8,128)S(1)}, f32[128,128]{0,1:T(8,128)S(1)}, u32[]{:S(2)}, u32[]{:S(2)}) collective-permute-start(f32[128,128]{0,1:T(8,128)S(1)} %add_add_fusion.1), channel_id=1, source_target_pairs={{0,8},{1,9},{2,10},{3,11},{4,12},{5,13},{6,14},{7,15},{8,0},{9,1},... | collective-permute-start | bytes 196616 | tf_op jit(solution)/shard_map/ppermute | solution.py:43
  15.3 1.5 %collective-permute-start.7 = (f32[1024,128]{1,0:T(8,128)S(1)}, f32[1024,128]{1,0:T(8,128)S(1)}, u32[]{:S(2)}, u32[]{:S(2)}) collective-permute-start(f32[1024,128]{1,0:T(8,128)S(1)} %copy-done), channel_id=1, source_target_pairs={{16,0},{0,16},{17,1},{1,17},{18,2},{2,18},{19,3},{3,19},{20,4},{4,... | collective-permute-start | bytes 1572872 | tf_op jit(solution)/shard_map/ppermute | solution.py:16
  17.0 0.9 %collective-permute-done.4 = f32[128,128]{0,1:T(8,128)S(1)} collective-permute-done((f32[128,128]{0,1:T(8,128)S(1)}, f32[128,128]{0,1:T(8,128)S(1)}, u32[]{:S(2)}, u32[]{:S(2)}) %collective-permute-start.4) | collective-permute-done | bytes 65568 | tf_op jit(solution)/shard_map/ppermute | solution.py:43
  17.9 0.6 %multiply_reduce_fusion.1 = (f32[]{:T(128)}, f32[128,128]{0,1:T(8,128)S(1)}) fusion(f32[128,128]{0,1:T(8,128)S(1)} %add_add_fusion.1, f32[128,128]{0,1:T(8,128)S(1)} %collective-permute-done.4), kind=kLoop, calls=%fused_computation.53 | loop fusion | flops 49151 | bytes 196612 | tf_op jit(solution)/shard_map/reduce_sum | solution.py:52
  21.2 1.6 %collective-permute-start.6 = (f32[128,128]{0,1:T(8,128)S(1)}, f32[128,128]{0,1:T(8,128)S(1)}, u32[]{:S(2)}, u32[]{:S(2)}) collective-permute-start(f32[128,128]{0,1:T(8,128)S(1)} %get-tuple-element.5), channel_id=1, source_target_pairs={{16,0},{0,16},{17,1},{1,17},{18,2},{2,18},{19,3},{3,19},{20,4},{4,... | collective-permute-start | bytes 196616 | tf_op jit(solution)/shard_map/ppermute | solution.py:16
  23.9 4.2 %collective-permute-done.7 = f32[1024,128]{1,0:T(8,128)S(1)} collective-permute-done((f32[1024,128]{1,0:T(8,128)S(1)}, f32[1024,128]{1,0:T(8,128)S(1)}, u32[]{:S(2)}, u32[]{:S(2)}) %collective-permute-start.7) | collective-permute-done | bytes 524320 | tf_op jit(solution)/shard_map/ppermute | solution.py:16
  28.1 0.6 %fusion.81 = f32[128,128]{0,1:T(8,128)S(1)} fusion(f32[1024,128]{1,0:T(8,128)S(1)} %collective-permute-done.7, f32[1024,128]{1,0:T(8,128)S(1)} %copy-done), kind=kOutput, calls=%fused_computation.104 | convolution fusion | flops 100663296 | bytes 1114112 | tf_op jit(solution)/shard_map/dot_general | solution.py:20
  29.1 1.6 %collective-permute-start.5 = (f32[128,128]{1,0:T(8,128)S(1)}, f32[128,128]{1,0:T(8,128)S(1)}, u32[]{:S(2)}, u32[]{:S(2)}) collective-permute-start(f32[128,128]{1,0:T(8,128)S(1)} %convolution_divide_fusion.1), channel_id=1, source_target_pairs={{16,0},{0,16},{17,1},{1,17},{18,2},{2,18},{19,3},{3,19},{20,4},{4,... | collective-permute-start | bytes 196616 | tf_op jit(solution)/shard_map/ppermute | solution.py:16
  30.7 2.6 %collective-permute-start.11 = (f32[128,128]{0,1:T(8,128)S(1)}, f32[128,128]{0,1:T(8,128)S(1)}, u32[]{:S(2)}, u32[]{:S(2)}) collective-permute-start(f32[128,128]{0,1:T(8,128)S(1)} %add.42), channel_id=1, source_target_pairs={{0,6},{1,7},{2,4},{3,5},{4,2},{5,3},{6,0},{7,1},{8,14},{9,15},{10,... | collective-permute-start | bytes 196616 | tf_op jit(solution)/shard_map/ppermute | solution.py:43
  33.3 0.6 %collective-permute-start.10 = (f32[128,128]{0,1:T(8,128)S(1)}, f32[128,128]{0,1:T(8,128)S(1)}, u32[]{:S(2)}, u32[]{:S(2)}) collective-permute-start(f32[128,128]{0,1:T(8,128)S(1)} %add.42), channel_id=1, source_target_pairs={{0,4},{1,5},{2,6},{3,7},{4,0},{5,1},{6,2},{7,3},{8,12},{9,13},{10,... | collective-permute-start | bytes 196616 | tf_op jit(solution)/shard_map/ppermute | solution.py:43
  34.5 1.4 %collective-permute-done.11 = f32[128,128]{0,1:T(8,128)S(1)} collective-permute-done((f32[128,128]{0,1:T(8,128)S(1)}, f32[128,128]{0,1:T(8,128)S(1)}, u32[]{:S(2)}, u32[]{:S(2)}) %collective-permute-start.11) | collective-permute-done | bytes 65568 | tf_op jit(solution)/shard_map/ppermute | solution.py:43
  35.9 1.7 %collective-permute-done.10 = f32[128,128]{0,1:T(8,128)S(1)} collective-permute-done((f32[128,128]{0,1:T(8,128)S(1)}, f32[128,128]{0,1:T(8,128)S(1)}, u32[]{:S(2)}, u32[]{:S(2)}) %collective-permute-start.10) | collective-permute-done | bytes 65568 | tf_op jit(solution)/shard_map/ppermute | solution.py:43
  37.6 0.6 %collective-permute-done.9 = f32[128,128]{0,1:T(8,128)S(1)} collective-permute-done((f32[128,128]{0,1:T(8,128)S(1)}, f32[128,128]{0,1:T(8,128)S(1)}, u32[]{:S(2)}, u32[]{:S(2)}) %collective-permute-start.9) | collective-permute-done | bytes 65568 | tf_op jit(solution)/shard_map/ppermute | solution.py:43
  38.9 4.6 %collective-permute-done.12 = f32[128,128]{0,1:T(8,128)S(1)} collective-permute-done((f32[128,128]{0,1:T(8,128)S(1)}, f32[128,128]{0,1:T(8,128)S(1)}, u32[]{:S(2)}, u32[]{:S(2)}) %collective-permute-start.12) | collective-permute-done | bytes 65568 | tf_op jit(solution)/shard_map/ppermute | solution.py:43
  43.6 0.6 %fusion.11 = f32[256,128]{1,0:T(8,128)S(1)} fusion(f32[128,128]{0,1:T(8,128)S(1)} %get-tuple-element.5, f32[128,128]{0,1:T(8,128)S(1)} %copy.9, f32[128,128]{0,1:T(8,128)S(1)} %add.46, f32[128,128]{0,1:T(8,128)S(1)} %collective-permute-done.6, f32[128,128]{1,0:T(8,128)S(1)} %fusion.25, f32[128,128]{1,0:T(8,128)S(1)} %fusion.27), kind=kOutput, calls=%fused_computation.26 | convolution fusion | flops 100892672 | bytes 524288 | tf_op jit(solution)/shard_map/dot_general | solution.py:24
  45.2 0.6 %fusion.10 = f32[256,128]{1,0:T(8,128)S(1)} fusion(f32[128,128]{0,1:T(8,128)S(1)} %get-tuple-element.5, f32[128,128]{0,1:T(8,128)S(1)} %copy.9, f32[128,128]{0,1:T(8,128)S(1)} %add.46, f32[128,128]{0,1:T(8,128)S(1)} %collective-permute-done.6, f32[128,128]{1,0:T(8,128)S(1)} %fusion.83, f32[128,128]{1,0:T(8,128)S(1)} %fusion.82), kind=kOutput, calls=%fused_computation.25 | convolution fusion | flops 100892672 | bytes 524288 | tf_op jit(solution)/shard_map/dot_general | solution.py:24
  45.8 1.0 %multiply_reduce_fusion = (f32[]{:T(128)}, f32[128,128]{1,0:T(8,128)S(1)}) fusion(f32[256,128]{1,0:T(8,128)S(1)} %fusion.10, f32[128,128]{1,0:T(8,128)S(1)} %fusion.83, f32[128,128]{1,0:T(8,128)S(1)} %fusion.82), kind=kOutput, calls=%fused_computation.47 | convolution fusion | flops 50397184 | bytes 327684 | tf_op jit(solution)/shard_map/dot_general | solution.py:20
  53.1 1.0 %copy.15 = f32[1024,128]{1,0:T(8,128)} copy(f32[1024,128]{0,1:T(8,128)S(1)} %fusion.1) | data formatting | bytes 1048576
  (58 shorter events, 12.6 us)
Async XLA Ops:
  0.6 14.7 %copy-start = (f32[1024,128]{1,0:T(8,128)S(1)}, f32[1024,128]{1,0:T(8,128)}, u32[]{:S(2)}) copy-start(f32[1024,128]{1,0:T(8,128)} %param.2) | copy-start | bytes 1572868
  2.5 1.4 %collective-permute-start = (f32[128,128]{0,1:T(8,128)S(1)}, f32[128,128]{0,1:T(8,128)S(1)}, u32[]{:S(2)}, u32[]{:S(2)}) collective-permute-start(f32[128,128]{0,1:T(8,128)S(1)} %fusion.75), channel_id=1, source_target_pairs={{0,1},{1,0},{2,3},{3,2},{4,5},{5,4},{6,7},{7,6},{8,9},{9,8},{10,11... | collective-permute-start | bytes 196616 | tf_op jit(solution)/shard_map/ppermute | solution.py:43
  4.0 6.4 %collective-permute-start.3 = (f32[128,128]{0,1:T(8,128)S(1)}, f32[128,128]{0,1:T(8,128)S(1)}, u32[]{:S(2)}, u32[]{:S(2)}) collective-permute-start(f32[128,128]{0,1:T(8,128)S(1)} %add.36), channel_id=1, source_target_pairs={{0,6},{1,7},{2,4},{3,5},{4,2},{5,3},{6,0},{7,1},{8,14},{9,15},{10,... | collective-permute-start | bytes 196616 | tf_op jit(solution)/shard_map/ppermute | solution.py:43
  7.9 4.3 %collective-permute-start.2 = (f32[128,128]{0,1:T(8,128)S(1)}, f32[128,128]{0,1:T(8,128)S(1)}, u32[]{:S(2)}, u32[]{:S(2)}) collective-permute-start(f32[128,128]{0,1:T(8,128)S(1)} %add.36), channel_id=1, source_target_pairs={{0,4},{1,5},{2,6},{3,7},{4,0},{5,1},{6,2},{7,3},{8,12},{9,13},{10,... | collective-permute-start | bytes 196616 | tf_op jit(solution)/shard_map/ppermute | solution.py:43
  8.3 4.3 %collective-permute-start.1 = (f32[128,128]{0,1:T(8,128)S(1)}, f32[128,128]{0,1:T(8,128)S(1)}, u32[]{:S(2)}, u32[]{:S(2)}) collective-permute-start(f32[128,128]{0,1:T(8,128)S(1)} %add.36), channel_id=1, source_target_pairs={{0,2},{1,3},{2,0},{3,1},{4,6},{5,7},{6,4},{7,5},{8,10},{9,11},{10,... | collective-permute-start | bytes 196616 | tf_op jit(solution)/shard_map/ppermute | solution.py:43
  12.6 5.2 %collective-permute-start.4 = (f32[128,128]{0,1:T(8,128)S(1)}, f32[128,128]{0,1:T(8,128)S(1)}, u32[]{:S(2)}, u32[]{:S(2)}) collective-permute-start(f32[128,128]{0,1:T(8,128)S(1)} %add_add_fusion.1), channel_id=1, source_target_pairs={{0,8},{1,9},{2,10},{3,11},{4,12},{5,13},{6,14},{7,15},{8,0},{9,1},... | collective-permute-start | bytes 196616 | tf_op jit(solution)/shard_map/ppermute | solution.py:43
  15.3 12.8 %collective-permute-start.7 = (f32[1024,128]{1,0:T(8,128)S(1)}, f32[1024,128]{1,0:T(8,128)S(1)}, u32[]{:S(2)}, u32[]{:S(2)}) collective-permute-start(f32[1024,128]{1,0:T(8,128)S(1)} %copy-done), channel_id=1, source_target_pairs={{16,0},{0,16},{17,1},{1,17},{18,2},{2,18},{19,3},{3,19},{20,4},{4,... | collective-permute-start | bytes 1572872 | tf_op jit(solution)/shard_map/ppermute | solution.py:16
  21.2 22.3 %collective-permute-start.6 = (f32[128,128]{0,1:T(8,128)S(1)}, f32[128,128]{0,1:T(8,128)S(1)}, u32[]{:S(2)}, u32[]{:S(2)}) collective-permute-start(f32[128,128]{0,1:T(8,128)S(1)} %get-tuple-element.5), channel_id=1, source_target_pairs={{16,0},{0,16},{17,1},{1,17},{18,2},{2,18},{19,3},{3,19},{20,4},{4,... | collective-permute-start | bytes 196616 | tf_op jit(solution)/shard_map/ppermute | solution.py:16
  28.7 1.9 %collective-permute-start.8 = (f32[128,128]{0,1:T(8,128)S(1)}, f32[128,128]{0,1:T(8,128)S(1)}, u32[]{:S(2)}, u32[]{:S(2)}) collective-permute-start(f32[128,128]{0,1:T(8,128)S(1)} %fusion.81), channel_id=1, source_target_pairs={{0,1},{1,0},{2,3},{3,2},{4,5},{5,4},{6,7},{7,6},{8,9},{9,8},{10,11... | collective-permute-start | bytes 196616 | tf_op jit(solution)/shard_map/ppermute | solution.py:43
  29.1 5.2 %copy-start.2 = (f32[1,256,128]{2,1,0:T(8,128)S(1)}, f32[1,256,128]{2,1,0:T(8,128)}, u32[]{:S(2)}) copy-start(f32[1,256,128]{2,1,0:T(8,128)} %param.3) | copy-start | bytes 393220
  29.1 9.5 %collective-permute-start.5 = (f32[128,128]{1,0:T(8,128)S(1)}, f32[128,128]{1,0:T(8,128)S(1)}, u32[]{:S(2)}, u32[]{:S(2)}) collective-permute-start(f32[128,128]{1,0:T(8,128)S(1)} %convolution_divide_fusion.1), channel_id=1, source_target_pairs={{16,0},{0,16},{17,1},{1,17},{18,2},{2,18},{19,3},{3,19},{20,4},{4,... | collective-permute-start | bytes 196616 | tf_op jit(solution)/shard_map/ppermute | solution.py:16
  30.7 5.2 %collective-permute-start.11 = (f32[128,128]{0,1:T(8,128)S(1)}, f32[128,128]{0,1:T(8,128)S(1)}, u32[]{:S(2)}, u32[]{:S(2)}) collective-permute-start(f32[128,128]{0,1:T(8,128)S(1)} %add.42), channel_id=1, source_target_pairs={{0,6},{1,7},{2,4},{3,5},{4,2},{5,3},{6,0},{7,1},{8,14},{9,15},{10,... | collective-permute-start | bytes 196616 | tf_op jit(solution)/shard_map/ppermute | solution.py:43
  33.3 4.3 %collective-permute-start.10 = (f32[128,128]{0,1:T(8,128)S(1)}, f32[128,128]{0,1:T(8,128)S(1)}, u32[]{:S(2)}, u32[]{:S(2)}) collective-permute-start(f32[128,128]{0,1:T(8,128)S(1)} %add.42), channel_id=1, source_target_pairs={{0,4},{1,5},{2,6},{3,7},{4,0},{5,1},{6,2},{7,3},{8,12},{9,13},{10,... | collective-permute-start | bytes 196616 | tf_op jit(solution)/shard_map/ppermute | solution.py:43
  33.9 4.3 %collective-permute-start.9 = (f32[128,128]{0,1:T(8,128)S(1)}, f32[128,128]{0,1:T(8,128)S(1)}, u32[]{:S(2)}, u32[]{:S(2)}) collective-permute-start(f32[128,128]{0,1:T(8,128)S(1)} %add.42), channel_id=1, source_target_pairs={{0,2},{1,3},{2,0},{3,1},{4,6},{5,7},{6,4},{7,5},{8,10},{9,11},{10,... | collective-permute-start | bytes 196616 | tf_op jit(solution)/shard_map/ppermute | solution.py:43
  38.2 5.2 %collective-permute-start.12 = (f32[128,128]{0,1:T(8,128)S(1)}, f32[128,128]{0,1:T(8,128)S(1)}, u32[]{:S(2)}, u32[]{:S(2)}) collective-permute-start(f32[128,128]{0,1:T(8,128)S(1)} %add_add_fusion), channel_id=1, source_target_pairs={{0,8},{1,9},{2,10},{3,11},{4,12},{5,13},{6,14},{7,15},{8,0},{9,1},... | collective-permute-start | bytes 196616 | tf_op jit(solution)/shard_map/ppermute | solution.py:43
  51.4 0.6 %copy-start.1 = (f32[128,128]{1,0:T(8,128)}, f32[128,128]{1,0:T(8,128)S(1)}, u32[]{:S(2)}) copy-start(f32[128,128]{1,0:T(8,128)S(1)} %fusion.19) | copy-start | bytes 196612

commit v2 on v0

v2 whole, which is shorter than its diff:
```python
import jax
import jax.numpy as jnp
from jax import lax
from jax.experimental import pallas as pl
from jax.experimental.pallas import tpu as pltpu
from jax.sharding import PartitionSpec as P

NS_STEPS = 5
HIGHEST = lax.Precision.HIGHEST
F32 = jnp.float32
BF16 = jnp.bfloat16
IN_VMEM = pl.BlockSpec(memory_space=pltpu.VMEM)
LIMITED = pltpu.CompilerParams(vmem_limit_bytes=12 << 20)
ANYWHERE = pl.BlockSpec(memory_space=pl.ANY)


def split(x):
    high = x.astype(BF16)
    rest = x - high.astype(F32)
    middle = rest.astype(BF16)
    low = (rest - middle.astype(F32)).astype(BF16)
    return high, middle, low


def dot(left, right):
    return jnp.dot(left, right, preferred_element_type=F32)


def dot_t(left, right):
    return lax.dot_general(left, right, (((0,), (0,)), ((), ())), preferred_element_type=F32)


def mul(left, right):
    lh, lm, ll = left
    rh, rm, rl = right
    n = rh.shape[1]
    both = jnp.concatenate([jnp.concatenate([rh, rm], 1), jnp.concatenate([rm, rh], 1)], 0)
    wide = dot(jnp.concatenate([lh, lm], 1), both)
    small = dot(jnp.concatenate([ll, lh], 1), jnp.concatenate([rh, rl], 0))
    return wide[:, :n] + (wide[:, n:] + small)


def mul_t(left, right):
    lh, lm, ll = left
    rh, rm, rl = right
    k, n = lh.shape[1], rh.shape[1]
    wide = dot_t(jnp.concatenate([lh, lm, ll], 1), jnp.concatenate([rh, rm], 1))
    small = dot_t(lh, rl)
    return wide[:k, :n] + ((wide[:k, n:] + wide[k : 2 * k, :n]) + (wide[k : 2 * k, n:] + (wide[2 * k :, :n] + small)))


def mul_long(left, right):
    lh, lm, ll = left
    rh, rm, rl = right
    n = rh.shape[1]
    both = jnp.concatenate([rh, rm], 1)
    first, second = dot(lh, both), dot(lm, both)
    return first[:, :n] + ((first[:, n:] + second[:, :n]) + (second[:, n:] + (dot(ll, rh) + dot(lh, rl))))


def identity(size):
    return (
        lax.broadcasted_iota(jnp.int32, (size, size), 0) == lax.broadcasted_iota(jnp.int32, (size, size), 1)
    ).astype(F32)


def root_iteration(matrices):
    eye = identity(matrices[0].shape[0])
    squares = []
    for a in matrices:
        parts = split(a)
        squares.append(mul(parts, parts))
    scales = [jnp.sqrt(jnp.sum(a * a, keepdims=True) + 1e-06) for a in matrices]
    ys, zs = [], []
    for a, square, scale in zip(matrices, squares, scales):
        inverse = 1.0 / scale
        y = a * inverse
        ys.append(1.5 * y - (0.5 * inverse * inverse) * square)
        zs.append(1.5 * eye - 0.5 * y)
    for repeat in range(1, NS_STEPS):
        y_parts, z_parts = [split(y) for y in ys], [split(z) for z in zs]
        middles = [1.5 * eye - 0.5 * mul(z, y) for z, y in zip(z_parts, y_parts)]
        if repeat == NS_STEPS - 1:
            return zs, middles, scales
        m_parts = [split(m) for m in middles]
        ys = [mul(y, m) for y, m in zip(y_parts, m_parts)]
        zs = [mul(m, z) for z, m in zip(z_parts, m_parts)]


def gram_kernel(x_ref, out_ref):
    parts = split(x_ref[...])
    k = x_ref.shape[1]
    h, m, l = parts
    wide = dot_t(jnp.concatenate([h, m, l], 1), jnp.concatenate([h, m], 1))
    cross = wide[:k, k:] + wide[2 * k :, :k]
    out_ref[...] = (wide[:k, :k] + wide[k : 2 * k, k:]) + (cross + cross.T)


def cross_kernel(left_ref, right_ref, out_ref):
    out_ref[...] = mul_t(split(left_ref[...]), split(right_ref[...]))


def leaf_kernel(lower_ref, own_ref, sketch_ref, e_ref, m_ref, f_ref, hm_ref):
    n = own_ref.shape[0]
    grams = [lower_ref[...], own_ref[...]]
    zs, middles, scales = root_iteration(grams)
    roots = [mul(split(m), split(z)) * lax.rsqrt(c) for z, m, c in zip(zs, middles, scales)]
    for at, (gram, root) in enumerate(zip(grams, roots)):
        rows = slice(at * n, (at + 1) * n)
        root_parts, gram_parts = split(root), split(gram)
        e = mul(root_parts, split(sketch_ref[rows, :]))
        m = mul(root_parts, split(root.T))
        e_ref[rows, :] = e
        m_ref[rows, :] = m
        f_ref[rows, :] = mul(gram_parts, split(e))
        hm_ref[rows, :] = mul(gram_parts, split(m))


def merge_kernel(cross_ref, e_ref, m_ref, f_ref, hm_ref, lower_ref, own_ref, coef_ref, out_ref, stage_ref, sems):
    n = cross_ref.shape[0]
    low, own = slice(0, n), slice(n, 2 * n)
    cross = cross_ref[...]
    cross_parts, cross_t_parts = split(cross), split(cross.T)
    e_low, e_own = split(e_ref[low, :]), split(e_ref[own, :])
    m_low, m_own = split(m_ref[low, :]), split(m_ref[own, :])
    right = mul(cross_parts, [jnp.concatenate([a, b], 1) for a, b in zip(e_own, m_own)])
    left = mul(cross_t_parts, [jnp.concatenate([a, b], 1) for a, b in zip(e_low, m_low)])
    f = jnp.concatenate([f_ref[low, :] + right[:, :n], f_ref[own, :] + left[:, :n]], 0)
    f_parts = split(f)
    hm = jnp.concatenate(
        [jnp.concatenate([hm_ref[low, :], right[:, n:]], 1), jnp.concatenate([left[:, n:], hm_ref[own, :]], 1)], 0
    )
    p = mul_long(split(hm), f_parts)
    v = jnp.concatenate([mul(m_low, [q[:n] for q in f_parts]), mul(m_own, [q[n:] for q in f_parts])], 0)
    small = mul_t(split(v), split(p))
    (z,), (middle,), (scale,) = root_iteration([small])
    both = mul(split(jnp.concatenate([v, p[n:]], 0)), split(z))
    both = mul(split(both), split(middle)) * lax.rsqrt(scale)
    coefficients = both[2 * n :].T
    coef_ref[...] = coefficients
    mixed = split(mul(split(both[: 2 * n]), split(coefficients)))
    rows, chunks = own_ref.shape[0], sems.shape[0]
    step = rows // chunks
    copies = []
    for at in range(chunks):
        here = slice(at * step, (at + 1) * step)
        x = own_ref[here, :]
        joined = split(jnp.concatenate([lower_ref[here, :], x], 1))
        stage_ref[here, :] = x - mul_long(joined, mixed)
        copy = pltpu.make_async_copy(stage_ref.at[here], out_ref.at[here], sems.at[at])
        copy.start()
        copies.append(copy)
    for copy in copies:
        copy.wait()


def shape(*dims):
    return jax.ShapeDtypeStruct(dims, F32)


def cost(flops, count):
    return pl.CostEstimate(flops=flops, bytes_accessed=count, transcendentals=0)


def passed_along(block, axis, distance):
    devices = range(lax.axis_size(axis))
    route = [((i - distance) % len(devices), i) for i in devices]
    return lax.ppermute(block, axis, route)


def stages_of(size):
    bits = [1 << b for b in range(size.bit_length() - 1)]
    stages, rest = [(b,) for b in bits[:1]], bits[1:]
    while rest:
        stages.append(tuple(rest[:2]))
        rest = rest[2:]
    return stages


def summed_over(part, axis, bits):
    size = lax.axis_size(axis)
    flips = [bits[0]] if len(bits) == 1 else [bits[0], bits[1], bits[0] | bits[1]]
    others = [lax.ppermute(part, axis, [(i, i ^ flip) for i in range(size)]) for flip in flips]
    if len(others) == 1:
        return part + others[0]
    return (part + others[0]) + (others[1] + others[2])


def row_sum(part, axis="row"):
    size = lax.axis_size(axis)
    if size & (size - 1):
        return lax.psum(part, axis)
    for bits in stages_of(size):
        part = summed_over(part, axis, bits)
    return part


def one_merge(snapshots, sketch):
    rows, n = snapshots.shape
    lower = passed_along(snapshots, "tm", 1)
    gram = pl.pallas_call(
        gram_kernel, out_shape=shape(n, n), in_specs=[IN_VMEM], out_specs=IN_VMEM, name="own_gram",
        compiler_params=LIMITED,
    )(snapshots)
    own_gram = row_sum(gram)
    own_gram, lower = lax.optimization_barrier((own_gram, lower))
    cross = pl.pallas_call(
        cross_kernel, out_shape=shape(n, n), in_specs=[IN_VMEM] * 2, out_specs=IN_VMEM, name="cross_gram",
        compiler_params=LIMITED,
    )(lower, snapshots)
    lower_gram = passed_along(own_gram, "tm", 1)
    leaf = pl.pallas_call(
        leaf_kernel,
        out_shape=[shape(2 * n, n)] * 4,
        in_specs=[IN_VMEM] * 3,
        out_specs=[IN_VMEM] * 4,
        compiler_params=LIMITED,
        name="leaf_roots",
    )(lower_gram, own_gram, sketch)
    cross = row_sum(cross)
    chunks = 4
    coefficients, deflated = pl.pallas_call(
        merge_kernel,
        out_shape=[shape(n, n), shape(rows, n)],
        in_specs=[IN_VMEM] * 7,
        out_specs=[IN_VMEM, ANYWHERE],
        scratch_shapes=[pltpu.VMEM((rows, n), F32), pltpu.SemaphoreType.DMA((chunks,))],
        compiler_params=LIMITED,
        name="merge",
    )(cross, *leaf, lower, snapshots)
    return coefficients, deflated


def product_t(left, right):
    return jnp.dot(left.T, right, precision=HIGHEST, preferred_element_type=F32)


def product(left, right):
    return jnp.dot(left, right, precision=HIGHEST, preferred_element_type=F32)


def inverse_root(matrix):
    frob_scale = jnp.sqrt(jnp.sum(matrix * matrix) + 1e-06)
    ident = jnp.eye(matrix.shape[0], dtype=matrix.dtype)
    y_iter = matrix / frob_scale
    z_iter = ident
    for repeat in range(NS_STEPS):
        middle = 1.5 * ident - 0.5 * product(z_iter, y_iter)
        y_iter = product(y_iter, middle)
        z_iter = product(middle, z_iter)
    return z_iter / jnp.sqrt(frob_scale)


def many_merges(snapshots, sketches, tree_depth):
    leaf_sum = row_sum(product_t(snapshots, snapshots))
    leaf_root = inverse_root(leaf_sum)
    mode_block = product(snapshots, leaf_root)
    own_gram = product_t(leaf_root, product(leaf_sum, leaf_root))
    for tree_level in range(tree_depth):
        sketch = sketches[tree_level]
        lower_block, lower_gram = passed_along((mode_block, own_gram), "tm", 1 << tree_level)
        cross_sum = row_sum(product_t(lower_block, mode_block))
        top_rows = jnp.concatenate([lower_gram, cross_sum], axis=1)
        bottom_rows = jnp.concatenate([cross_sum.T, own_gram], axis=1)
        gram_sum = jnp.concatenate([top_rows, bottom_rows], axis=0)
        joined = jnp.concatenate([lower_block, mode_block], axis=1)
        reduced = product(gram_sum, sketch)
        small = product_t(reduced, product(gram_sum, reduced))
        mixing = product(reduced, inverse_root(small))
        mode_block = product(joined, mixing)
        own_gram = product_t(mixing, product(gram_sum, mixing))
    coefficients = row_sum(product_t(mode_block, snapshots))
    deflated = snapshots - product(mode_block, coefficients)
    return coefficients, deflated


def body(snapshots, sketches):
    tree_depth = lax.axis_size("tm").bit_length() - 1
    if tree_depth == 1:
        return one_merge(snapshots, sketches[0])
    return many_merges(snapshots, sketches, tree_depth)


def solution(mesh):
    placed = (P("row", "tm"), P())
    return jax.shard_map(
        body, mesh=mesh, in_specs=placed, out_specs=(P(None, "tm"), P("row", "tm")), check_vma=False
    )
```

time: 313 us -> 38.6 us (0.12)
  waiting for transfers between devices: 271 us -> 12.1 us
  matrix products: 19.1 us -> 0 us
  between operations: 15.5 us -> 0.72 us
  starting transfers between devices: 2.28 us -> 16.1 us
  Pallas kernels: 0 us -> 8.37 us
    psum x3 -> x0, waiting for transfers between devices: 259 us -> none  [the longest x1 89 us: body(): leaf_sum = lax.psum(product_t(snapshots, snapshots), 'row')]
    dot_general x40 -> x0, matrix products: 19.1 us -> none  [the longest x35 12 us: product(): jnp.dot(left, right, precision=HIGH, preferred_element_type=jnp.float32)]
    ppermute x0 -> x10, starting transfers between devices: none -> 12.5 us  [summed_over(): lax.ppermute(part, axis, [(i, i ^ flip) for i in range(size)])]
    ppermute x2, waiting for transfers between devices: 12.2 us -> 0.01 us  [passed_along(): return lax.ppermute(block, axis, route)]
    ppermute x0 -> x10, waiting for transfers between devices: none -> 12.1 us  [summed_over(): lax.ppermute(part, axis, [(i, i ^ flip) for i in range(size)])]
    pallas_call x0 -> x4, Pallas kernels: none -> 8.37 us  [the longest x1 4.96 us: one_merge(): pl.pallas_call(merge_kernel, out_shape=[shape(n, n), shape(rows, n)], in_...]
  transfers between devices with their start and end apart: 5 -> 12, of which waited for: 4 -> 10; matrix products, arithmetic and copies ran while one was open for 1% -> 0% of each run, Pallas kernels for 0% -> 8%
where the time goes in v2:
time: 38.6 us; the launch traced here: 38.4 us
  starting transfers between devices  16.1 us (42%)
  waiting for transfers between devices  12.1 us (31%)
  Pallas kernels  8.37 us (22%)
  local copies, waits for them, and re-layouts  1.08 us (3%)
  between operations  0.72 us (2%)
    ppermute x10, starting transfers between devices, summed_over(): lax.ppermute(part, axis, [(i, i ^ flip) for i in range(size)])  12.5 us
    ppermute x10, waiting for transfers between devices, summed_over(): lax.ppermute(part, axis, [(i, i ^ flip) for i in range(size)])  12.1 us
    pallas_call x1, Pallas kernels, one_merge(): pl.pallas_call(merge_kernel, out_shape=[shape(n, n), shape(rows, n)], in_...  4.96 us
    ppermute x2, starting transfers between devices, passed_along(): return lax.ppermute(block, axis, route)  3.54 us
    pallas_call x1, Pallas kernels, one_merge(): pl.pallas_call(leaf_kernel, out_shape=[shape(2 * n, n)] * 4, in_specs=[IN...  2.44 us
    unnamed x6, local copies, waits for them, and re-layouts  1.08 us
  transfers between devices with their start and end apart: 12, of which 10 were waited for; matrix products, arithmetic and copies ran while one was open for 0% of the time, Pallas kernels for 8%

profile of v2, /device:TPU:0, one launch (start us, length us, event | category | flops | bytes accessed | tf_op | source)
XLA Modules:
  0.0 38.4 jit_solution(14373787956999233008)
XLA Ops:
  0.6 3.0 %collective-permute-start.5 = (f32[1024,128]{1,0:T(8,128)}, f32[1024,128]{1,0:T(8,128)S(1)}, u32[]{:S(2)}, u32[]{:S(2)}) collective-permute-start(f32[1024,128]{1,0:T(8,128)} %own_ref.1), channel_id=1, source_target_pairs={{16,0},{0,16},{17,1},{1,17},{18,2},{2,18},{19,3},{3,19},{20,4},{4,... | collective-permute-start | bytes 1572872 | tf_op jit(solution)/shard_map/ppermute | solution.py:168
  3.6 1.1 %copy-done = f32[1024,128]{1,0:T(8,128)S(1)} copy-done((f32[1024,128]{1,0:T(8,128)S(1)}, f32[1024,128]{1,0:T(8,128)}, u32[]{:S(2)}) %copy-start) | copy-done | bytes 524312
  4.7 0.5 %own_gram.1 = f32[128,128]{1,0:T(8,128)S(1)} custom-call(f32[1024,128]{1,0:T(8,128)S(1)} %copy-done), custom_call_target="tpu_custom_call" | custom-call | tf_op jit(solution)/shard_map/own_gram/pallas_call | solution.py:201
  5.3 1.2 %collective-permute-done = f32[128,128]{1,0:T(8,128)S(1)} collective-permute-done((f32[128,128]{1,0:T(8,128)S(1)}, f32[128,128]{1,0:T(8,128)S(1)}, u32[]{:S(2)}, u32[]{:S(2)}) %collective-permute-start) | collective-permute-done | bytes 65568 | tf_op jit(solution)/shard_map/ppermute | solution.py:183
  6.5 2.6 %collective-permute-start.3 = (f32[128,128]{1,0:T(8,128)S(1)}, f32[128,128]{1,0:T(8,128)S(1)}, u32[]{:S(2)}, u32[]{:S(2)}) collective-permute-start(f32[128,128]{1,0:T(8,128)S(1)} %add.30), channel_id=1, source_target_pairs={{0,6},{1,7},{2,4},{3,5},{4,2},{5,3},{6,0},{7,1},{8,14},{9,15},{10,... | collective-permute-start | bytes 196616 | tf_op jit(solution)/shard_map/ppermute | solution.py:183
  9.1 0.4 %collective-permute-start.2 = (f32[128,128]{1,0:T(8,128)S(1)}, f32[128,128]{1,0:T(8,128)S(1)}, u32[]{:S(2)}, u32[]{:S(2)}) collective-permute-start(f32[128,128]{1,0:T(8,128)S(1)} %add.30), channel_id=1, source_target_pairs={{0,4},{1,5},{2,6},{3,7},{4,0},{5,1},{6,2},{7,3},{8,12},{9,13},{10,... | collective-permute-start | bytes 196616 | tf_op jit(solution)/shard_map/ppermute | solution.py:183
  9.6 0.5 %collective-permute-start.1 = (f32[128,128]{1,0:T(8,128)S(1)}, f32[128,128]{1,0:T(8,128)S(1)}, u32[]{:S(2)}, u32[]{:S(2)}) collective-permute-start(f32[128,128]{1,0:T(8,128)S(1)} %add.30), channel_id=1, source_target_pairs={{0,2},{1,3},{2,0},{3,1},{4,6},{5,7},{6,4},{7,5},{8,10},{9,11},{10,... | collective-permute-start | bytes 196616 | tf_op jit(solution)/shard_map/ppermute | solution.py:183
  10.1 2.0 %collective-permute-done.3 = f32[128,128]{1,0:T(8,128)S(1)} collective-permute-done((f32[128,128]{1,0:T(8,128)S(1)}, f32[128,128]{1,0:T(8,128)S(1)}, u32[]{:S(2)}, u32[]{:S(2)}) %collective-permute-start.3) | collective-permute-done | bytes 65568 | tf_op jit(solution)/shard_map/ppermute | solution.py:183
  12.1 1.3 %collective-permute-done.2 = f32[128,128]{1,0:T(8,128)S(1)} collective-permute-done((f32[128,128]{1,0:T(8,128)S(1)}, f32[128,128]{1,0:T(8,128)S(1)}, u32[]{:S(2)}, u32[]{:S(2)}) %collective-permute-start.2) | collective-permute-done | bytes 65568 | tf_op jit(solution)/shard_map/ppermute | solution.py:183
  13.9 2.7 %collective-permute-start.4 = (f32[128,128]{1,0:T(8,128)S(1)}, f32[128,128]{1,0:T(8,128)S(1)}, u32[]{:S(2)}, u32[]{:S(2)}) collective-permute-start(f32[128,128]{1,0:T(8,128)S(1)} %add_add_fusion.1), channel_id=1, source_target_pairs={{0,8},{1,9},{2,10},{3,11},{4,12},{5,13},{6,14},{7,15},{8,0},{9,1},... | collective-permute-start | bytes 196616 | tf_op jit(solution)/shard_map/ppermute | solution.py:183
  16.5 2.6 %collective-permute-done.4 = f32[128,128]{1,0:T(8,128)S(1)} collective-permute-done((f32[128,128]{1,0:T(8,128)S(1)}, f32[128,128]{1,0:T(8,128)S(1)}, u32[]{:S(2)}, u32[]{:S(2)}) %collective-permute-start.4) | collective-permute-done | bytes 65568 | tf_op jit(solution)/shard_map/ppermute | solution.py:183
  19.1 0.5 %cross_gram.1 = f32[128,128]{1,0:T(8,128)S(1)} custom-call(f32[1024,128]{1,0:T(8,128)S(1)} %collective-permute-done.5.left_ref.lower_ref, f32[1024,128]{1,0:T(8,128)S(1)} %copy-done.1), custom_call_target="tpu_custom_call" | custom-call | tf_op jit(solution)/shard_map/cross_gram/pallas_call | solution.py:207
  19.7 1.2 %collective-permute-done.6 = f32[128,128]{1,0:T(8,128)S(1)} collective-permute-done((f32[128,128]{1,0:T(8,128)S(1)}, f32[128,128]{1,0:T(8,128)S(1)}, u32[]{:S(2)}, u32[]{:S(2)}) %collective-permute-start.6) | collective-permute-done | bytes 65568 | tf_op jit(solution)/shard_map/ppermute | solution.py:183
  21.0 1.8 %collective-permute-start.9 = (f32[128,128]{1,0:T(8,128)S(1)}, f32[128,128]{1,0:T(8,128)S(1)}, u32[]{:S(2)}, u32[]{:S(2)}) collective-permute-start(f32[128,128]{1,0:T(8,128)S(1)} %add.35), channel_id=1, source_target_pairs={{0,6},{1,7},{2,4},{3,5},{4,2},{5,3},{6,0},{7,1},{8,14},{9,15},{10,... | collective-permute-start | bytes 196616 | tf_op jit(solution)/shard_map/ppermute | solution.py:183
  22.8 0.6 %collective-permute-start.8 = (f32[128,128]{1,0:T(8,128)S(1)}, f32[128,128]{1,0:T(8,128)S(1)}, u32[]{:S(2)}, u32[]{:S(2)}) collective-permute-start(f32[128,128]{1,0:T(8,128)S(1)} %add.35), channel_id=1, source_target_pairs={{0,4},{1,5},{2,6},{3,7},{4,0},{5,1},{6,2},{7,3},{8,12},{9,13},{10,... | collective-permute-start | bytes 196616 | tf_op jit(solution)/shard_map/ppermute | solution.py:183
  23.4 1.1 %collective-permute-start.7 = (f32[128,128]{1,0:T(8,128)S(1)}, f32[128,128]{1,0:T(8,128)S(1)}, u32[]{:S(2)}, u32[]{:S(2)}) collective-permute-start(f32[128,128]{1,0:T(8,128)S(1)} %add.35), channel_id=1, source_target_pairs={{0,2},{1,3},{2,0},{3,1},{4,6},{5,7},{6,4},{7,5},{8,10},{9,11},{10,... | collective-permute-start | bytes 196616 | tf_op jit(solution)/shard_map/ppermute | solution.py:183
  24.5 0.5 %collective-permute-start.11 = (f32[128,128]{1,0:T(8,128)S(1)}, f32[128,128]{1,0:T(8,128)S(1)}, u32[]{:S(2)}, u32[]{:S(2)}) collective-permute-start(f32[128,128]{1,0:T(8,128)S(1)} %add.34.own_ref), channel_id=1, source_target_pairs={{16,0},{0,16},{17,1},{1,17},{18,2},{2,18},{19,3},{3,19},{20,4},{4,... | collective-permute-start | bytes 196616 | tf_op jit(solution)/shard_map/ppermute | solution.py:168
  25.1 1.4 %collective-permute-done.9 = f32[128,128]{1,0:T(8,128)S(1)} collective-permute-done((f32[128,128]{1,0:T(8,128)S(1)}, f32[128,128]{1,0:T(8,128)S(1)}, u32[]{:S(2)}, u32[]{:S(2)}) %collective-permute-start.9) | collective-permute-done | bytes 65568 | tf_op jit(solution)/shard_map/ppermute | solution.py:183
  26.5 0.6 %collective-permute-done.8 = f32[128,128]{1,0:T(8,128)S(1)} collective-permute-done((f32[128,128]{1,0:T(8,128)S(1)}, f32[128,128]{1,0:T(8,128)S(1)}, u32[]{:S(2)}, u32[]{:S(2)}) %collective-permute-start.8) | collective-permute-done | bytes 65568 | tf_op jit(solution)/shard_map/ppermute | solution.py:183
  27.0 0.6 %collective-permute-done.7 = f32[128,128]{1,0:T(8,128)S(1)} collective-permute-done((f32[128,128]{1,0:T(8,128)S(1)}, f32[128,128]{1,0:T(8,128)S(1)}, u32[]{:S(2)}, u32[]{:S(2)}) %collective-permute-start.7) | collective-permute-done | bytes 65568 | tf_op jit(solution)/shard_map/ppermute | solution.py:183
  27.7 2.6 %collective-permute-start.10 = (f32[128,128]{1,0:T(8,128)S(1)}, f32[128,128]{1,0:T(8,128)S(1)}, u32[]{:S(2)}, u32[]{:S(2)}) collective-permute-start(f32[128,128]{1,0:T(8,128)S(1)} %add_add_fusion), channel_id=1, source_target_pairs={{0,8},{1,9},{2,10},{3,11},{4,12},{5,13},{6,14},{7,15},{8,0},{9,1},... | collective-permute-start | bytes 196616 | tf_op jit(solution)/shard_map/ppermute | solution.py:183
  30.3 2.4 %leaf_roots.1 = (f32[256,128]{1,0:T(8,128)S(1)}, f32[256,128]{1,0:T(8,128)S(1)}, f32[256,128]{1,0:T(8,128)S(1)}, f32[256,128]{1,0:T(8,128)S(1)}) custom-call(f32[128,128]{1,0:T(8,128)S(1)} %collective-permute-done.11.lower_ref, f32[128,128]{1,0:T(8,128)S(1)} %add.34.own_ref, f32[256,128]{1,0:T(8,128)S(1)} %bitcast.1), custom_call_target="tpu_custom_call" | custom-call | tf_op jit(solution)/shard_map/leaf_roots/pallas_call | solution.py:212
  32.8 0.7 %collective-permute-done.10 = f32[128,128]{1,0:T(8,128)S(1)} collective-permute-done((f32[128,128]{1,0:T(8,128)S(1)}, f32[128,128]{1,0:T(8,128)S(1)}, u32[]{:S(2)}, u32[]{:S(2)}) %collective-permute-start.10) | collective-permute-done | bytes 65568 | tf_op jit(solution)/shard_map/ppermute | solution.py:183
  33.5 5.0 %merge.1 = (f32[128,128]{1,0:T(8,128)}, f32[1024,128]{1,0:T(8,128)}) custom-call(f32[128,128]{1,0:T(8,128)S(1)} %add.39.cross_ref, f32[256,128]{1,0:T(8,128)S(1)} %get-tuple-element.10.e_ref, f32[256,128]{1,0:T(8,128)S(1)} %get-tuple-element.11.m_ref, f32[256,128]{1,0:T(8,128)S(1)} %get-tuple-element.12.f_ref, f32[256,128]{1,0:T(8,128)S(1)} %get-tuple-element.13.hm_ref, ...), custom_call_target="tpu_custom_call" | custom-call | tf_op jit(solution)/shard_map/merge/pallas_call | solution.py:222
  (16 shorter events, 0.7 us)
Async XLA Ops:
  0.6 18.5 %collective-permute-start.5 = (f32[1024,128]{1,0:T(8,128)}, f32[1024,128]{1,0:T(8,128)S(1)}, u32[]{:S(2)}, u32[]{:S(2)}) collective-permute-start(f32[1024,128]{1,0:T(8,128)} %own_ref.1), channel_id=1, source_target_pairs={{16,0},{0,16},{17,1},{1,17},{18,2},{2,18},{19,3},{3,19},{20,4},{4,... | collective-permute-start | bytes 1572872 | tf_op jit(solution)/shard_map/ppermute | solution.py:168
  3.6 1.1 %copy-start = (f32[1024,128]{1,0:T(8,128)S(1)}, f32[1024,128]{1,0:T(8,128)}, u32[]{:S(2)}) copy-start(f32[1024,128]{1,0:T(8,128)} %own_ref.1) | copy-start | bytes 1572868
  4.7 14.4 %copy-start.1 = (f32[1024,128]{1,0:T(8,128)S(1)}, f32[1024,128]{1,0:T(8,128)}, u32[]{:S(2)}) copy-start(f32[1024,128]{1,0:T(8,128)} %own_ref.1) | copy-start | bytes 1572868
  5.2 1.3 %collective-permute-start = (f32[128,128]{1,0:T(8,128)S(1)}, f32[128,128]{1,0:T(8,128)S(1)}, u32[]{:S(2)}, u32[]{:S(2)}) collective-permute-start(f32[128,128]{1,0:T(8,128)S(1)} %own_gram.1), channel_id=1, source_target_pairs={{0,1},{1,0},{2,3},{3,2},{4,5},{5,4},{6,7},{7,6},{8,9},{9,8},{10,11... | collective-permute-start | bytes 196616 | tf_op jit(solution)/shard_map/ppermute | solution.py:183
  6.5 5.5 %collective-permute-start.3 = (f32[128,128]{1,0:T(8,128)S(1)}, f32[128,128]{1,0:T(8,128)S(1)}, u32[]{:S(2)}, u32[]{:S(2)}) collective-permute-start(f32[128,128]{1,0:T(8,128)S(1)} %add.30), channel_id=1, source_target_pairs={{0,6},{1,7},{2,4},{3,5},{4,2},{5,3},{6,0},{7,1},{8,14},{9,15},{10,... | collective-permute-start | bytes 196616 | tf_op jit(solution)/shard_map/ppermute | solution.py:183
  9.1 4.3 %collective-permute-start.2 = (f32[128,128]{1,0:T(8,128)S(1)}, f32[128,128]{1,0:T(8,128)S(1)}, u32[]{:S(2)}, u32[]{:S(2)}) collective-permute-start(f32[128,128]{1,0:T(8,128)S(1)} %add.30), channel_id=1, source_target_pairs={{0,4},{1,5},{2,6},{3,7},{4,0},{5,1},{6,2},{7,3},{8,12},{9,13},{10,... | collective-permute-start | bytes 196616 | tf_op jit(solution)/shard_map/ppermute | solution.py:183
  9.6 4.3 %collective-permute-start.1 = (f32[128,128]{1,0:T(8,128)S(1)}, f32[128,128]{1,0:T(8,128)S(1)}, u32[]{:S(2)}, u32[]{:S(2)}) collective-permute-start(f32[128,128]{1,0:T(8,128)S(1)} %add.30), channel_id=1, source_target_pairs={{0,2},{1,3},{2,0},{3,1},{4,6},{5,7},{6,4},{7,5},{8,10},{9,11},{10,... | collective-permute-start | bytes 196616 | tf_op jit(solution)/shard_map/ppermute | solution.py:183
  13.9 5.2 %collective-permute-start.4 = (f32[128,128]{1,0:T(8,128)S(1)}, f32[128,128]{1,0:T(8,128)S(1)}, u32[]{:S(2)}, u32[]{:S(2)}) collective-permute-start(f32[128,128]{1,0:T(8,128)S(1)} %add_add_fusion.1), channel_id=1, source_target_pairs={{0,8},{1,9},{2,10},{3,11},{4,12},{5,13},{6,14},{7,15},{8,0},{9,1},... | collective-permute-start | bytes 196616 | tf_op jit(solution)/shard_map/ppermute | solution.py:183
  19.6 1.3 %collective-permute-start.6 = (f32[128,128]{1,0:T(8,128)S(1)}, f32[128,128]{1,0:T(8,128)S(1)}, u32[]{:S(2)}, u32[]{:S(2)}) collective-permute-start(f32[128,128]{1,0:T(8,128)S(1)} %cross_gram.1), channel_id=1, source_target_pairs={{0,1},{1,0},{2,3},{3,2},{4,5},{5,4},{6,7},{7,6},{8,9},{9,8},{10,11... | collective-permute-start | bytes 196616 | tf_op jit(solution)/shard_map/ppermute | solution.py:183
  20.9 9.4 %copy-start.2 = (f32[1,256,128]{2,1,0:T(8,128)S(1)}, f32[1,256,128]{2,1,0:T(8,128)}, u32[]{:S(2)}) copy-start(f32[1,256,128]{2,1,0:T(8,128)} %param.3) | copy-start | bytes 393220
  21.0 5.5 %collective-permute-start.9 = (f32[128,128]{1,0:T(8,128)S(1)}, f32[128,128]{1,0:T(8,128)S(1)}, u32[]{:S(2)}, u32[]{:S(2)}) collective-permute-start(f32[128,128]{1,0:T(8,128)S(1)} %add.35), channel_id=1, source_target_pairs={{0,6},{1,7},{2,4},{3,5},{4,2},{5,3},{6,0},{7,1},{8,14},{9,15},{10,... | collective-permute-start | bytes 196616 | tf_op jit(solution)/shard_map/ppermute | solution.py:183
  22.8 4.3 %collective-permute-start.8 = (f32[128,128]{1,0:T(8,128)S(1)}, f32[128,128]{1,0:T(8,128)S(1)}, u32[]{:S(2)}, u32[]{:S(2)}) collective-permute-start(f32[128,128]{1,0:T(8,128)S(1)} %add.35), channel_id=1, source_target_pairs={{0,4},{1,5},{2,6},{3,7},{4,0},{5,1},{6,2},{7,3},{8,12},{9,13},{10,... | collective-permute-start | bytes 196616 | tf_op jit(solution)/shard_map/ppermute | solution.py:183
  23.4 4.3 %collective-permute-start.7 = (f32[128,128]{1,0:T(8,128)S(1)}, f32[128,128]{1,0:T(8,128)S(1)}, u32[]{:S(2)}, u32[]{:S(2)}) collective-permute-start(f32[128,128]{1,0:T(8,128)S(1)} %add.35), channel_id=1, source_target_pairs={{0,2},{1,3},{2,0},{3,1},{4,6},{5,7},{6,4},{7,5},{8,10},{9,11},{10,... | collective-permute-start | bytes 196616 | tf_op jit(solution)/shard_map/ppermute | solution.py:183
  24.5 5.8 %collective-permute-start.11 = (f32[128,128]{1,0:T(8,128)S(1)}, f32[128,128]{1,0:T(8,128)S(1)}, u32[]{:S(2)}, u32[]{:S(2)}) collective-permute-start(f32[128,128]{1,0:T(8,128)S(1)} %add.34.own_ref), channel_id=1, source_target_pairs={{16,0},{0,16},{17,1},{1,17},{18,2},{2,18},{19,3},{3,19},{20,4},{4,... | collective-permute-start | bytes 196616 | tf_op jit(solution)/shard_map/ppermute | solution.py:168
  27.7 5.8 %collective-permute-start.10 = (f32[128,128]{1,0:T(8,128)S(1)}, f32[128,128]{1,0:T(8,128)S(1)}, u32[]{:S(2)}, u32[]{:S(2)}) collective-permute-start(f32[128,128]{1,0:T(8,128)S(1)} %add_add_fusion), channel_id=1, source_target_pairs={{0,8},{1,9},{2,10},{3,11},{4,12},{5,13},{6,14},{7,15},{8,0},{9,1},... | collective-permute-start | bytes 196616 | tf_op jit(solution)/shard_map/ppermute | solution.py:183

commit v3 on v2

--- a/solution.py
+++ b/solution.py
@@ -177,13 +177,20 @@
     return stages
 
 
-def summed_over(part, axis, bits):
+def received(part, axis, bits):
+    flips = [bits[0]] if len(bits) == 1 else [bits[0], bits[1], bits[0] | bits[1]]
     size = lax.axis_size(axis)
-    flips = [bits[0]] if len(bits) == 1 else [bits[0], bits[1], bits[0] | bits[1]]
-    others = [lax.ppermute(part, axis, [(i, i ^ flip) for i in range(size)]) for flip in flips]
+    return [lax.ppermute(part, axis, [(i, i ^ flip) for i in range(size)]) for flip in flips]
+
+
+def total(part, others):
     if len(others) == 1:
         return part + others[0]
     return (part + others[0]) + (others[1] + others[2])
+
+
+def summed_over(part, axis, bits):
+    return total(part, received(part, axis, bits))
 
 
 def row_sum(part, axis="row"):
@@ -202,12 +209,16 @@
         gram_kernel, out_shape=shape(n, n), in_specs=[IN_VMEM], out_specs=IN_VMEM, name="own_gram",
         compiler_params=LIMITED,
     )(snapshots)
-    own_gram = row_sum(gram)
-    own_gram, lower = lax.optimization_barrier((own_gram, lower))
+    stages = stages_of(lax.axis_size("row"))
+    for bits in stages[1:-1]:
+        gram = summed_over(gram, "row", bits)
+    gram = summed_over(gram, "row", stages[-1])
+    own_gram = summed_over(gram, "row", stages[0])
     cross = pl.pallas_call(
         cross_kernel, out_shape=shape(n, n), in_specs=[IN_VMEM] * 2, out_specs=IN_VMEM, name="cross_gram",
         compiler_params=LIMITED,
     )(lower, snapshots)
+    cross = summed_over(cross, "row", stages[0])
     lower_gram = passed_along(own_gram, "tm", 1)
     leaf = pl.pallas_call(
         leaf_kernel,
@@ -217,7 +228,8 @@
         compiler_params=LIMITED,
         name="leaf_roots",
     )(lower_gram, own_gram, sketch)
-    cross = row_sum(cross)
+    for bits in stages[1:]:
+        cross = summed_over(cross, "row", bits)
     chunks = 4
     coefficients, deflated = pl.pallas_call(
         merge_kernel,

time: 38.6 us -> 36.7 us (0.951)
  waiting for transfers between devices: 12.1 us -> 9.21 us
  starting transfers between devices: 16.1 us -> 17.1 us
    ppermute x10, waiting for transfers between devices: 12.1 us -> 8.63 us  [received(): lax.ppermute(part, axis, [(i, i ^ flip) for i in range(size)])]
    ppermute x2, starting transfers between devices: 3.54 us -> 4.5 us  [passed_along(): return lax.ppermute(block, axis, route)]
    ppermute x2, waiting for transfers between devices: 0.01 us -> 0.58 us  [passed_along(): return lax.ppermute(block, axis, route)]
  transfers between devices with their start and end apart: 12 -> 12, of which waited for: 10 -> 9; matrix products, arithmetic and copies ran while one was open for 0% -> 0% of each run, Pallas kernels for 8% -> 9%
where the time goes in v3:
time: 36.7 us; the launch traced here: 36.5 us
  starting transfers between devices  17.1 us (47%)
  waiting for transfers between devices  9.21 us (25%)
  Pallas kernels  8.36 us (23%)
  local copies, waits for them, and re-layouts  1.08 us (3%)
  between operations  0.72 us (2%)
    ppermute x10, starting transfers between devices, received(): lax.ppermute(part, axis, [(i, i ^ flip) for i in range(size)])  12.6 us
    ppermute x10, waiting for transfers between devices, received(): lax.ppermute(part, axis, [(i, i ^ flip) for i in range(size)])  8.63 us
    pallas_call x1, Pallas kernels, one_merge(): pl.pallas_call(merge_kernel, out_shape=[shape(n, n), shape(rows, n)], in_...  4.96 us
    ppermute x2, starting transfers between devices, passed_along(): return lax.ppermute(block, axis, route)  4.5 us
    pallas_call x1, Pallas kernels, one_merge(): pl.pallas_call(leaf_kernel, out_shape=[shape(2 * n, n)] * 4, in_specs=[IN...  2.44 us
    unnamed x6, local copies, waits for them, and re-layouts  1.08 us
  transfers between devices with their start and end apart: 12, of which 9 were waited for; matrix products, arithmetic and copies ran while one was open for 0% of the time, Pallas kernels for 9%

profile of v3, /device:TPU:0, one launch (start us, length us, event | category | flops | bytes accessed | tf_op | source)
XLA Modules:
  0.0 36.5 jit_solution(7777497860212932903)
XLA Ops:
  0.6 3.0 %collective-permute-start = (f32[1024,128]{1,0:T(8,128)}, f32[1024,128]{1,0:T(8,128)S(1)}, u32[]{:S(2)}, u32[]{:S(2)}) collective-permute-start(f32[1024,128]{1,0:T(8,128)} %own_ref.1), channel_id=1, source_target_pairs={{16,0},{0,16},{17,1},{1,17},{18,2},{2,18},{19,3},{3,19},{20,4},{4,... | collective-permute-start | bytes 1572872 | tf_op jit(solution)/shard_map/ppermute | solution.py:168
  3.6 1.1 %copy-done = f32[1024,128]{1,0:T(8,128)S(1)} copy-done((f32[1024,128]{1,0:T(8,128)S(1)}, f32[1024,128]{1,0:T(8,128)}, u32[]{:S(2)}) %copy-start) | copy-done | bytes 524312
  4.7 0.5 %own_gram.1 = f32[128,128]{1,0:T(8,128)S(1)} custom-call(f32[1024,128]{1,0:T(8,128)S(1)} %copy-done), custom_call_target="tpu_custom_call" | custom-call | tf_op jit(solution)/shard_map/own_gram/pallas_call | solution.py:208
  5.2 2.6 %collective-permute-start.8 = (f32[128,128]{1,0:T(8,128)S(1)}, f32[128,128]{1,0:T(8,128)S(1)}, u32[]{:S(2)}, u32[]{:S(2)}) collective-permute-start(f32[128,128]{1,0:T(8,128)S(1)} %own_gram.1), channel_id=1, source_target_pairs={{0,6},{1,7},{2,4},{3,5},{4,2},{5,3},{6,0},{7,1},{8,14},{9,15},{10,... | collective-permute-start | bytes 196616 | tf_op jit(solution)/shard_map/ppermute | solution.py:183
  7.8 0.4 %collective-permute-start.7 = (f32[128,128]{1,0:T(8,128)S(1)}, f32[128,128]{1,0:T(8,128)S(1)}, u32[]{:S(2)}, u32[]{:S(2)}) collective-permute-start(f32[128,128]{1,0:T(8,128)S(1)} %own_gram.1), channel_id=1, source_target_pairs={{0,4},{1,5},{2,6},{3,7},{4,0},{5,1},{6,2},{7,3},{8,12},{9,13},{10,... | collective-permute-start | bytes 196616 | tf_op jit(solution)/shard_map/ppermute | solution.py:183
  8.3 0.5 %collective-permute-start.6 = (f32[128,128]{1,0:T(8,128)S(1)}, f32[128,128]{1,0:T(8,128)S(1)}, u32[]{:S(2)}, u32[]{:S(2)}) collective-permute-start(f32[128,128]{1,0:T(8,128)S(1)} %own_gram.1), channel_id=1, source_target_pairs={{0,2},{1,3},{2,0},{3,1},{4,6},{5,7},{6,4},{7,5},{8,10},{9,11},{10,... | collective-permute-start | bytes 196616 | tf_op jit(solution)/shard_map/ppermute | solution.py:183
  8.8 2.4 %collective-permute-done.8 = f32[128,128]{1,0:T(8,128)S(1)} collective-permute-done((f32[128,128]{1,0:T(8,128)S(1)}, f32[128,128]{1,0:T(8,128)S(1)}, u32[]{:S(2)}, u32[]{:S(2)}) %collective-permute-start.8) | collective-permute-done | bytes 65568 | tf_op jit(solution)/shard_map/ppermute | solution.py:183
  11.1 0.9 %collective-permute-done.7 = f32[128,128]{1,0:T(8,128)S(1)} collective-permute-done((f32[128,128]{1,0:T(8,128)S(1)}, f32[128,128]{1,0:T(8,128)S(1)}, u32[]{:S(2)}, u32[]{:S(2)}) %collective-permute-start.7) | collective-permute-done | bytes 65568 | tf_op jit(solution)/shard_map/ppermute | solution.py:183
  12.1 0.4 %collective-permute-done.6 = f32[128,128]{1,0:T(8,128)S(1)} collective-permute-done((f32[128,128]{1,0:T(8,128)S(1)}, f32[128,128]{1,0:T(8,128)S(1)}, u32[]{:S(2)}, u32[]{:S(2)}) %collective-permute-start.6) | collective-permute-done | bytes 65568 | tf_op jit(solution)/shard_map/ppermute | solution.py:183
  12.5 2.7 %collective-permute-start.9 = (f32[128,128]{1,0:T(8,128)S(1)}, f32[128,128]{1,0:T(8,128)S(1)}, u32[]{:S(2)}, u32[]{:S(2)}) collective-permute-start(f32[128,128]{1,0:T(8,128)S(1)} %add_add_fusion), channel_id=1, source_target_pairs={{0,8},{1,9},{2,10},{3,11},{4,12},{5,13},{6,14},{7,15},{8,0},{9,1},... | collective-permute-start | bytes 196616 | tf_op jit(solution)/shard_map/ppermute | solution.py:183
  15.2 0.6 %collective-permute-done.left_ref.lower_ref = f32[1024,128]{1,0:T(8,128)S(1)} collective-permute-done((f32[1024,128]{1,0:T(8,128)}, f32[1024,128]{1,0:T(8,128)S(1)}, u32[]{:S(2)}, u32[]{:S(2)}) %collective-permute-start) | collective-permute-done | bytes 524320 | tf_op jit(solution)/shard_map/ppermute | solution.py:168
  15.8 0.5 %cross_gram.1 = f32[128,128]{1,0:T(8,128)S(1)} custom-call(f32[1024,128]{1,0:T(8,128)S(1)} %collective-permute-done.left_ref.lower_ref, f32[1024,128]{1,0:T(8,128)S(1)} %copy-done.1), custom_call_target="tpu_custom_call" | custom-call | tf_op jit(solution)/shard_map/cross_gram/pallas_call | solution.py:217
  16.3 1.4 %collective-permute-done.9 = f32[128,128]{1,0:T(8,128)S(1)} collective-permute-done((f32[128,128]{1,0:T(8,128)S(1)}, f32[128,128]{1,0:T(8,128)S(1)}, u32[]{:S(2)}, u32[]{:S(2)}) %collective-permute-start.9) | collective-permute-done | bytes 65568 | tf_op jit(solution)/shard_map/ppermute | solution.py:183
  17.9 2.5 %collective-permute-start.4 = (f32[128,128]{1,0:T(8,128)S(1)}, f32[128,128]{1,0:T(8,128)S(1)}, u32[]{:S(2)}, u32[]{:S(2)}) collective-permute-start(f32[128,128]{1,0:T(8,128)S(1)} %add.30), channel_id=1, source_target_pairs={{0,6},{1,7},{2,4},{3,5},{4,2},{5,3},{6,0},{7,1},{8,14},{9,15},{10,... | collective-permute-start | bytes 196616 | tf_op jit(solution)/shard_map/ppermute | solution.py:183
  20.4 0.4 %collective-permute-start.3 = (f32[128,128]{1,0:T(8,128)S(1)}, f32[128,128]{1,0:T(8,128)S(1)}, u32[]{:S(2)}, u32[]{:S(2)}) collective-permute-start(f32[128,128]{1,0:T(8,128)S(1)} %add.30), channel_id=1, source_target_pairs={{0,4},{1,5},{2,6},{3,7},{4,0},{5,1},{6,2},{7,3},{8,12},{9,13},{10,... | collective-permute-start | bytes 196616 | tf_op jit(solution)/shard_map/ppermute | solution.py:183
  20.9 0.6 %collective-permute-start.2 = (f32[128,128]{1,0:T(8,128)S(1)}, f32[128,128]{1,0:T(8,128)S(1)}, u32[]{:S(2)}, u32[]{:S(2)}) collective-permute-start(f32[128,128]{1,0:T(8,128)S(1)} %add.30), channel_id=1, source_target_pairs={{0,2},{1,3},{2,0},{3,1},{4,6},{5,7},{6,4},{7,5},{8,10},{9,11},{10,... | collective-permute-start | bytes 196616 | tf_op jit(solution)/shard_map/ppermute | solution.py:183
  21.5 1.5 %collective-permute-start.11 = (f32[128,128]{1,0:T(8,128)S(1)}, f32[128,128]{1,0:T(8,128)S(1)}, u32[]{:S(2)}, u32[]{:S(2)}) collective-permute-start(f32[128,128]{1,0:T(8,128)S(1)} %add.39.own_ref), channel_id=1, source_target_pairs={{16,0},{0,16},{17,1},{1,17},{18,2},{2,18},{19,3},{3,19},{20,4},{4,... | collective-permute-start | bytes 196616 | tf_op jit(solution)/shard_map/ppermute | solution.py:168
  23.0 0.5 %collective-permute-done.4 = f32[128,128]{1,0:T(8,128)S(1)} collective-permute-done((f32[128,128]{1,0:T(8,128)S(1)}, f32[128,128]{1,0:T(8,128)S(1)}, u32[]{:S(2)}, u32[]{:S(2)}) %collective-permute-start.4) | collective-permute-done | bytes 65568 | tf_op jit(solution)/shard_map/ppermute | solution.py:183
  23.5 1.2 %collective-permute-done.3 = f32[128,128]{1,0:T(8,128)S(1)} collective-permute-done((f32[128,128]{1,0:T(8,128)S(1)}, f32[128,128]{1,0:T(8,128)S(1)}, u32[]{:S(2)}, u32[]{:S(2)}) %collective-permute-start.3) | collective-permute-done | bytes 65568 | tf_op jit(solution)/shard_map/ppermute | solution.py:183
  24.7 0.4 %collective-permute-done.2 = f32[128,128]{1,0:T(8,128)S(1)} collective-permute-done((f32[128,128]{1,0:T(8,128)S(1)}, f32[128,128]{1,0:T(8,128)S(1)}, u32[]{:S(2)}, u32[]{:S(2)}) %collective-permute-start.2) | collective-permute-done | bytes 65568 | tf_op jit(solution)/shard_map/ppermute | solution.py:183
  25.2 2.7 %collective-permute-start.5 = (f32[128,128]{1,0:T(8,128)S(1)}, f32[128,128]{1,0:T(8,128)S(1)}, u32[]{:S(2)}, u32[]{:S(2)}) collective-permute-start(f32[128,128]{1,0:T(8,128)S(1)} %add_add_fusion.1), channel_id=1, source_target_pairs={{0,8},{1,9},{2,10},{3,11},{4,12},{5,13},{6,14},{7,15},{8,0},{9,1},... | collective-permute-start | bytes 196616 | tf_op jit(solution)/shard_map/ppermute | solution.py:183
  27.8 2.4 %leaf_roots.1 = (f32[256,128]{1,0:T(8,128)S(1)}, f32[256,128]{1,0:T(8,128)S(1)}, f32[256,128]{1,0:T(8,128)S(1)}, f32[256,128]{1,0:T(8,128)S(1)}) custom-call(f32[128,128]{1,0:T(8,128)S(1)} %collective-permute-done.11.lower_ref, f32[128,128]{1,0:T(8,128)S(1)} %add.39.own_ref, f32[256,128]{1,0:T(8,128)S(1)} %bitcast.1), custom_call_target="tpu_custom_call" | custom-call | tf_op jit(solution)/shard_map/leaf_roots/pallas_call | solution.py:223
  30.3 1.3 %collective-permute-done.5 = f32[128,128]{1,0:T(8,128)S(1)} collective-permute-done((f32[128,128]{1,0:T(8,128)S(1)}, f32[128,128]{1,0:T(8,128)S(1)}, u32[]{:S(2)}, u32[]{:S(2)}) %collective-permute-start.5) | collective-permute-done | bytes 65568 | tf_op jit(solution)/shard_map/ppermute | solution.py:183
  31.5 5.0 %merge.1 = (f32[128,128]{1,0:T(8,128)}, f32[1024,128]{1,0:T(8,128)}) custom-call(f32[128,128]{1,0:T(8,128)S(1)} %add.34.cross_ref, f32[256,128]{1,0:T(8,128)S(1)} %get-tuple-element.6.e_ref, f32[256,128]{1,0:T(8,128)S(1)} %get-tuple-element.7.m_ref, f32[256,128]{1,0:T(8,128)S(1)} %get-tuple-element.8.f_ref, f32[256,128]{1,0:T(8,128)S(1)} %get-tuple-element.9.hm_ref, ...), custom_call_target="tpu_custom_call" | custom-call | tf_op jit(solution)/shard_map/merge/pallas_call | solution.py:234
  (16 shorter events, 0.2 us)
Async XLA Ops:
  0.6 15.1 %collective-permute-start = (f32[1024,128]{1,0:T(8,128)}, f32[1024,128]{1,0:T(8,128)S(1)}, u32[]{:S(2)}, u32[]{:S(2)}) collective-permute-start(f32[1024,128]{1,0:T(8,128)} %own_ref.1), channel_id=1, source_target_pairs={{16,0},{0,16},{17,1},{1,17},{18,2},{2,18},{19,3},{3,19},{20,4},{4,... | collective-permute-start | bytes 1572872 | tf_op jit(solution)/shard_map/ppermute | solution.py:168
  3.6 1.1 %copy-start = (f32[1024,128]{1,0:T(8,128)S(1)}, f32[1024,128]{1,0:T(8,128)}, u32[]{:S(2)}) copy-start(f32[1024,128]{1,0:T(8,128)} %own_ref.1) | copy-start | bytes 1572868
  4.7 11.1 %copy-start.1 = (f32[1024,128]{1,0:T(8,128)S(1)}, f32[1024,128]{1,0:T(8,128)}, u32[]{:S(2)}) copy-start(f32[1024,128]{1,0:T(8,128)} %own_ref.1) | copy-start | bytes 1572868
  5.2 5.9 %collective-permute-start.8 = (f32[128,128]{1,0:T(8,128)S(1)}, f32[128,128]{1,0:T(8,128)S(1)}, u32[]{:S(2)}, u32[]{:S(2)}) collective-permute-start(f32[128,128]{1,0:T(8,128)S(1)} %own_gram.1), channel_id=1, source_target_pairs={{0,6},{1,7},{2,4},{3,5},{4,2},{5,3},{6,0},{7,1},{8,14},{9,15},{10,... | collective-permute-start | bytes 196616 | tf_op jit(solution)/shard_map/ppermute | solution.py:183
  7.8 4.3 %collective-permute-start.7 = (f32[128,128]{1,0:T(8,128)S(1)}, f32[128,128]{1,0:T(8,128)S(1)}, u32[]{:S(2)}, u32[]{:S(2)}) collective-permute-start(f32[128,128]{1,0:T(8,128)S(1)} %own_gram.1), channel_id=1, source_target_pairs={{0,4},{1,5},{2,6},{3,7},{4,0},{5,1},{6,2},{7,3},{8,12},{9,13},{10,... | collective-permute-start | bytes 196616 | tf_op jit(solution)/shard_map/ppermute | solution.py:183
  8.3 4.3 %collective-permute-start.6 = (f32[128,128]{1,0:T(8,128)S(1)}, f32[128,128]{1,0:T(8,128)S(1)}, u32[]{:S(2)}, u32[]{:S(2)}) collective-permute-start(f32[128,128]{1,0:T(8,128)S(1)} %own_gram.1), channel_id=1, source_target_pairs={{0,2},{1,3},{2,0},{3,1},{4,6},{5,7},{6,4},{7,5},{8,10},{9,11},{10,... | collective-permute-start | bytes 196616 | tf_op jit(solution)/shard_map/ppermute | solution.py:183
  12.5 5.2 %collective-permute-start.9 = (f32[128,128]{1,0:T(8,128)S(1)}, f32[128,128]{1,0:T(8,128)S(1)}, u32[]{:S(2)}, u32[]{:S(2)}) collective-permute-start(f32[128,128]{1,0:T(8,128)S(1)} %add_add_fusion), channel_id=1, source_target_pairs={{0,8},{1,9},{2,10},{3,11},{4,12},{5,13},{6,14},{7,15},{8,0},{9,1},... | collective-permute-start | bytes 196616 | tf_op jit(solution)/shard_map/ppermute | solution.py:183
  16.2 1.6 %collective-permute-start.1 = (f32[128,128]{1,0:T(8,128)S(1)}, f32[128,128]{1,0:T(8,128)S(1)}, u32[]{:S(2)}, u32[]{:S(2)}) collective-permute-start(f32[128,128]{1,0:T(8,128)S(1)} %cross_gram.1), channel_id=1, source_target_pairs={{0,1},{1,0},{2,3},{3,2},{4,5},{5,4},{6,7},{7,6},{8,9},{9,8},{10,11... | collective-permute-start | bytes 196616 | tf_op jit(solution)/shard_map/ppermute | solution.py:183
  17.8 3.7 %collective-permute-start.10 = (f32[128,128]{1,0:T(8,128)S(1)}, f32[128,128]{1,0:T(8,128)S(1)}, u32[]{:S(2)}, u32[]{:S(2)}) collective-permute-start(f32[128,128]{1,0:T(8,128)S(1)} %add.38), channel_id=1, source_target_pairs={{0,1},{1,0},{2,3},{3,2},{4,5},{5,4},{6,7},{7,6},{8,9},{9,8},{10,11... | collective-permute-start | bytes 196616 | tf_op jit(solution)/shard_map/ppermute | solution.py:183
  17.9 5.6 %collective-permute-start.4 = (f32[128,128]{1,0:T(8,128)S(1)}, f32[128,128]{1,0:T(8,128)S(1)}, u32[]{:S(2)}, u32[]{:S(2)}) collective-permute-start(f32[128,128]{1,0:T(8,128)S(1)} %add.30), channel_id=1, source_target_pairs={{0,6},{1,7},{2,4},{3,5},{4,2},{5,3},{6,0},{7,1},{8,14},{9,15},{10,... | collective-permute-start | bytes 196616 | tf_op jit(solution)/shard_map/ppermute | solution.py:183
  20.4 4.3 %collective-permute-start.3 = (f32[128,128]{1,0:T(8,128)S(1)}, f32[128,128]{1,0:T(8,128)S(1)}, u32[]{:S(2)}, u32[]{:S(2)}) collective-permute-start(f32[128,128]{1,0:T(8,128)S(1)} %add.30), channel_id=1, source_target_pairs={{0,4},{1,5},{2,6},{3,7},{4,0},{5,1},{6,2},{7,3},{8,12},{9,13},{10,... | collective-permute-start | bytes 196616 | tf_op jit(solution)/shard_map/ppermute | solution.py:183
  20.9 4.3 %collective-permute-start.2 = (f32[128,128]{1,0:T(8,128)S(1)}, f32[128,128]{1,0:T(8,128)S(1)}, u32[]{:S(2)}, u32[]{:S(2)}) collective-permute-start(f32[128,128]{1,0:T(8,128)S(1)} %add.30), channel_id=1, source_target_pairs={{0,2},{1,3},{2,0},{3,1},{4,6},{5,7},{6,4},{7,5},{8,10},{9,11},{10,... | collective-permute-start | bytes 196616 | tf_op jit(solution)/shard_map/ppermute | solution.py:183
  21.5 6.4 %copy-start.2 = (f32[1,256,128]{2,1,0:T(8,128)S(1)}, f32[1,256,128]{2,1,0:T(8,128)}, u32[]{:S(2)}) copy-start(f32[1,256,128]{2,1,0:T(8,128)} %param.3) | copy-start | bytes 393220
  21.5 6.4 %collective-permute-start.11 = (f32[128,128]{1,0:T(8,128)S(1)}, f32[128,128]{1,0:T(8,128)S(1)}, u32[]{:S(2)}, u32[]{:S(2)}) collective-permute-start(f32[128,128]{1,0:T(8,128)S(1)} %add.39.own_ref), channel_id=1, source_target_pairs={{16,0},{0,16},{17,1},{1,17},{18,2},{2,18},{19,3},{3,19},{20,4},{4,... | collective-permute-start | bytes 196616 | tf_op jit(solution)/shard_map/ppermute | solution.py:168
  25.2 6.4 %collective-permute-start.5 = (f32[128,128]{1,0:T(8,128)S(1)}, f32[128,128]{1,0:T(8,128)S(1)}, u32[]{:S(2)}, u32[]{:S(2)}) collective-permute-start(f32[128,128]{1,0:T(8,128)S(1)} %add_add_fusion.1), channel_id=1, source_target_pairs={{0,8},{1,9},{2,10},{3,11},{4,12},{5,13},{6,14},{7,15},{8,0},{9,1},... | collective-permute-start | bytes 196616 | tf_op jit(solution)/shard_map/ppermute | solution.py:183

commit v4 on v3

--- a/solution.py
+++ b/solution.py
@@ -47,15 +47,6 @@
     wide = dot_t(jnp.concatenate([lh, lm, ll], 1), jnp.concatenate([rh, rm], 1))
     small = dot_t(lh, rl)
     return wide[:k, :n] + ((wide[:k, n:] + wide[k : 2 * k, :n]) + (wide[k : 2 * k, n:] + (wide[2 * k :, :n] + small)))
-
-
-def mul_long(left, right):
-    lh, lm, ll = left
-    rh, rm, rl = right
-    n = rh.shape[1]
-    both = jnp.concatenate([rh, rm], 1)
-    first, second = dot(lh, both), dot(lm, both)
-    return first[:, :n] + ((first[:, n:] + second[:, :n]) + (second[:, n:] + (dot(ll, rh) + dot(lh, rl))))
 
 
 def identity(size):
@@ -87,20 +78,61 @@
         zs = [mul(m, z) for z, m in zip(z_parts, m_parts)]
 
 
-def gram_kernel(x_ref, out_ref):
-    parts = split(x_ref[...])
+def gram_kernel(x_ref, out_ref, buffer_ref, sems):
     k = x_ref.shape[1]
-    h, m, l = parts
-    wide = dot_t(jnp.concatenate([h, m, l], 1), jnp.concatenate([h, m], 1))
+    chunks = sems.shape[0]
+    step = x_ref.shape[0] // chunks
+    slices = [slice(at * step, (at + 1) * step) for at in range(chunks)]
+    copies = [pltpu.make_async_copy(x_ref.at[s], buffer_ref.at[s], sems.at[at]) for at, s in enumerate(slices)]
+    for copy in copies:
+        copy.start()
+    wide = None
+    for s, copy in zip(slices, copies):
+        copy.wait()
+        h, m, l = split(buffer_ref[s, :])
+        piece = dot_t(jnp.concatenate([h, m, l], 1), jnp.concatenate([h, m], 1))
+        wide = piece if wide is None else wide + piece
     cross = wide[:k, k:] + wide[2 * k :, :k]
     out_ref[...] = (wide[:k, :k] + wide[k : 2 * k, k:]) + (cross + cross.T)
 
 
-def cross_kernel(left_ref, right_ref, out_ref):
-    out_ref[...] = mul_t(split(left_ref[...]), split(right_ref[...]))
-
-
-def leaf_kernel(lower_ref, own_ref, sketch_ref, e_ref, m_ref, f_ref, hm_ref):
+def upper_half():
+    return lax.rem(lax.axis_index("row"), 2) == 1
+
+
+def cross_kernel(left_ref, right_ref, mine_ref, theirs_ref):
+    gram = mul_t(split(left_ref[...]), split(right_ref[...]))
+    half = gram.shape[0] // 2
+    upper = upper_half()
+    mine_ref[...] = jnp.where(upper, gram[half:], gram[:half])
+    theirs_ref[...] = jnp.where(upper, gram[:half], gram[half:])
+
+
+def packed(parts):
+    high, middle, low = parts
+    return jnp.concatenate([high, middle], 1), jnp.concatenate([low, high], 1)
+
+
+def weights(parts):
+    high, middle, low = parts
+    both = jnp.concatenate([jnp.concatenate([high, middle], 1), jnp.concatenate([middle, high], 1)], 0)
+    return both, jnp.concatenate([high, low], 0)
+
+
+def mul_packed(left, right):
+    n = right[1].shape[1]
+    wide = dot(left[0], right[0])
+    return wide[:, :n] + (wide[:, n:] + dot(left[1], right[1]))
+
+
+def split_kernel(lower_ref, own_ref, high_ref, middle_ref, low_ref):
+    n = own_ref.shape[1]
+    for at, ref in enumerate((lower_ref, own_ref)):
+        columns = slice(at * n, (at + 1) * n)
+        high_ref[:, columns], middle_ref[:, columns], low_ref[:, columns] = split(ref[...])
+
+
+def leaf_kernel(lower_ref, own_ref, sketch_ref, f_ref, wide_ref, small_ref, left_ref):
     n = own_ref.shape[0]
     grams = [lower_ref[...], own_ref[...]]
     zs, middles, scales = root_iteration(grams)
@@ -108,58 +140,63 @@
     for at, (gram, root) in enumerate(zip(grams, roots)):
         rows = slice(at * n, (at + 1) * n)
         root_parts, gram_parts = split(root), split(gram)
-        e = mul(root_parts, split(sketch_ref[rows, :]))
-        m = mul(root_parts, split(root.T))
-        e_ref[rows, :] = e
-        m_ref[rows, :] = m
-        f_ref[rows, :] = mul(gram_parts, split(e))
-        hm_ref[rows, :] = mul(gram_parts, split(m))
-
-
-def merge_kernel(cross_ref, e_ref, m_ref, f_ref, hm_ref, lower_ref, own_ref, coef_ref, out_ref, stage_ref, sems):
-    n = cross_ref.shape[0]
-    low, own = slice(0, n), slice(n, 2 * n)
-    cross = cross_ref[...]
-    cross_parts, cross_t_parts = split(cross), split(cross.T)
-    e_low, e_own = split(e_ref[low, :]), split(e_ref[own, :])
-    m_low, m_own = split(m_ref[low, :]), split(m_ref[own, :])
-    right = mul(cross_parts, [jnp.concatenate([a, b], 1) for a, b in zip(e_own, m_own)])
-    left = mul(cross_t_parts, [jnp.concatenate([a, b], 1) for a, b in zip(e_low, m_low)])
-    f = jnp.concatenate([f_ref[low, :] + right[:, :n], f_ref[own, :] + left[:, :n]], 0)
-    f_parts = split(f)
-    hm = jnp.concatenate(
-        [jnp.concatenate([hm_ref[low, :], right[:, n:]], 1), jnp.concatenate([left[:, n:], hm_ref[own, :]], 1)], 0
-    )
-    p = mul_long(split(hm), f_parts)
-    v = jnp.concatenate([mul(m_low, [q[:n] for q in f_parts]), mul(m_own, [q[n:] for q in f_parts])], 0)
-    small = mul_t(split(v), split(p))
-    (z,), (middle,), (scale,) = root_iteration([small])
+        e = split(mul(root_parts, split(sketch_ref[rows, :])))
+        m = split(mul(root_parts, split(root.T)))
+        wide_ref[at], small_ref[at] = weights([jnp.concatenate([a, b], 1) for a, b in zip(e, m)])
+        f_ref[rows, :] = mul(gram_parts, e)
+        left_ref[at, 0, :n], left_ref[at, 1, :n] = packed(m)
+        left_ref[at, 0, n:], left_ref[at, 1, n:] = packed(split(mul(gram_parts, m)))
+
+
+def merge_kernel(
+    mine_ref, theirs_ref, f_ref, wide_ref, small_ref, left_ref, high_ref, middle_ref, low_ref, own_ref,
+    coef_ref, out_ref, coef_stage_ref, stage_ref, coef_sem, sems,
+):
+    n = mine_ref.shape[1]
+    upper = upper_half()
+    mine, theirs = mine_ref[...], theirs_ref[...]
+    cross = jnp.concatenate([jnp.where(upper, theirs, mine), jnp.where(upper, mine, theirs)], 0)
+    right = mul_packed(packed(split(cross)), (wide_ref[1], small_ref[1]))
+    left = mul_packed(packed(split(cross.T)), (wide_ref[0], small_ref[0]))
+    results = []
+    for at, part, other in ((0, right, left), (1, left, right)):
+        f = weights(split(f_ref[at * n : (at + 1) * n, :] + part[:, :n]))
+        extra = packed(split(other[:, n:]))
+        lefts = [jnp.concatenate([left_ref[at, k], extra[k]], 0) for k in range(2)]
+        results.append(mul_packed(lefts, f))
+    lower, own = results
+    v = jnp.concatenate([lower[:n], own[:n]], 0)
+    p = jnp.concatenate([lower[n : 2 * n] + own[2 * n :], lower[2 * n :] + own[n : 2 * n]], 0)
+    (z,), (middle,), (scale,) = root_iteration([mul_t(split(v), split(p))])
     both = mul(split(jnp.concatenate([v, p[n:]], 0)), split(z))
     both = mul(split(both), split(middle)) * lax.rsqrt(scale)
     coefficients = both[2 * n :].T
-    coef_ref[...] = coefficients
+    coef_stage_ref[...] = coefficients
+    coef_copy = pltpu.make_async_copy(coef_stage_ref, coef_ref, coef_sem)
+    coef_copy.start()
     mixed = split(mul(split(both[: 2 * n]), split(coefficients)))
+    mixed_both = jnp.concatenate(mixed[:2], 1)
     rows, chunks = own_ref.shape[0], sems.shape[0]
     step = rows // chunks
     copies = []
     for at in range(chunks):
         here = slice(at * step, (at + 1) * step)
-        x = own_ref[here, :]
-        joined = split(jnp.concatenate([lower_ref[here, :], x], 1))
-        stage_ref[here, :] = x - mul_long(joined, mixed)
+        high = high_ref[here, :]
+        first, second = dot(high, mixed_both), dot(middle_ref[here, :], mixed_both)
+        third = dot(low_ref[here, :], mixed[0]) + dot(high, mixed[2])
+        stage_ref[here, :] = own_ref[here, :] - (
+            first[:, :n] + ((first[:, n:] + second[:, :n]) + (second[:, n:] + third))
+        )
         copy = pltpu.make_async_copy(stage_ref.at[here], out_ref.at[here], sems.at[at])
         copy.start()
         copies.append(copy)
     for copy in copies:
         copy.wait()
-
-
-def shape(*dims):
-    return jax.ShapeDtypeStruct(dims, F32)
-
-
-def cost(flops, count):
-    return pl.CostEstimate(flops=flops, bytes_accessed=count, transcendentals=0)
+    coef_copy.wait()
+
+
+def shape(*dims, kind=F32):
+    return jax.ShapeDtypeStruct(dims, kind)
 
 
 def passed_along(block, axis, distance):
@@ -202,45 +239,71 @@
     return part
 
 
+def call(kernel, name, outs, **more):
+    return pl.pallas_call(kernel, out_shape=outs, compiler_params=LIMITED, name=name, **more)
+
+
 def one_merge(snapshots, sketch):
     rows, n = snapshots.shape
     lower = passed_along(snapshots, "tm", 1)
-    gram = pl.pallas_call(
-        gram_kernel, out_shape=shape(n, n), in_specs=[IN_VMEM], out_specs=IN_VMEM, name="own_gram",
-        compiler_params=LIMITED,
-    )(snapshots)
     stages = stages_of(lax.axis_size("row"))
+    gram = call(
+        gram_kernel,
+        "own_gram",
+        shape(n, n),
+        in_specs=[pl.BlockSpec(memory_space=pltpu.HBM)],
+        out_specs=IN_VMEM,
+        scratch_shapes=[pltpu.VMEM((rows, n), F32), pltpu.SemaphoreType.DMA((2,))],
+    )(pltpu.with_memory_space_constraint(snapshots, pltpu.HBM))
     for bits in stages[1:-1]:
         gram = summed_over(gram, "row", bits)
-    gram = summed_over(gram, "row", stages[-1])
-    own_gram = summed_over(gram, "row", stages[0])
-    cross = pl.pallas_call(
-        cross_kernel, out_shape=shape(n, n), in_specs=[IN_VMEM] * 2, out_specs=IN_VMEM, name="cross_gram",
-        compiler_params=LIMITED,
+    mine, theirs = call(
+        cross_kernel, "cross_gram", [shape(n // 2, n)] * 2, in_specs=[IN_VMEM] * 2, out_specs=[IN_VMEM] * 2
     )(lower, snapshots)
-    cross = summed_over(cross, "row", stages[0])
+    parts = call(
+        split_kernel, "raw_parts", [shape(rows, 2 * n, kind=BF16)] * 3, in_specs=[IN_VMEM] * 2, out_specs=[IN_VMEM] * 3
+    )(lower, snapshots)
+    others = received(theirs, "row", stages[0])
+    others, parts = lax.optimization_barrier((others, parts))
+    mine = total(mine, others)
+    others, _ = lax.optimization_barrier((received(gram, "row", stages[-1]), mine))
+    own_gram = summed_over(total(gram, others), "row", stages[0])
     lower_gram = passed_along(own_gram, "tm", 1)
-    leaf = pl.pallas_call(
+    leaf = call(
         leaf_kernel,
-        out_shape=[shape(2 * n, n)] * 4,
+        "leaf_roots",
+        [
+            shape(2 * n, n),
+            shape(2, 2 * n, 4 * n, kind=BF16),
+            shape(2, 2 * n, 2 * n, kind=BF16),
+            shape(2, 2, 2 * n, 2 * n, kind=BF16),
+        ],
         in_specs=[IN_VMEM] * 3,
         out_specs=[IN_VMEM] * 4,
-        compiler_params=LIMITED,
-        name="leaf_roots",
     )(lower_gram, own_gram, sketch)
-    for bits in stages[1:]:
-        cross = summed_over(cross, "row", bits)
+    for bits in stages[:0:-1]:
+        beside = leaf if bits == stages[1] else own_gram
+        others, beside = lax.optimization_barrier((received(mine, "row", bits), beside))
+        mine = total(mine, others)
+        if bits == stages[1]:
+            leaf = beside
+    (theirs,) = received(mine, "row", stages[0])
     chunks = 4
-    coefficients, deflated = pl.pallas_call(
-        merge_kernel,
-        out_shape=[shape(n, n), shape(rows, n)],
-        in_specs=[IN_VMEM] * 7,
-        out_specs=[IN_VMEM, ANYWHERE],
-        scratch_shapes=[pltpu.VMEM((rows, n), F32), pltpu.SemaphoreType.DMA((chunks,))],
-        compiler_params=LIMITED,
-        name="merge",
-    )(cross, *leaf, lower, snapshots)
-    return coefficients, deflated
+    return tuple(
+        call(
+            merge_kernel,
+            "merge",
+            [shape(n, n), shape(rows, n)],
+            in_specs=[IN_VMEM] * 10,
+            out_specs=[ANYWHERE, ANYWHERE],
+            scratch_shapes=[
+                pltpu.VMEM((n, n), F32),
+                pltpu.VMEM((rows, n), F32),
+                pltpu.SemaphoreType.DMA,
+                pltpu.SemaphoreType.DMA((chunks,)),
+            ],
+        )(mine, theirs, *leaf, *parts, snapshots)
+    )
 
 
 def product_t(left, right):

time: 36.7 us -> 35.5 us (0.967)
  local copies, waits for them, and re-layouts: 1.08 us -> 0.01 us
  waiting for transfers between devices: 9.21 us -> 8.16 us
  Pallas kernels: 8.36 us -> 9.1 us
    unnamed x6 -> x4, local copies, waits for them, and re-layouts: 1.08 us -> 0.01 us
    ppermute x10 -> x11, waiting for transfers between devices: 8.63 us -> 7.57 us  [received(): lax.ppermute(part, axis, [(i, i ^ flip) for i in range(size)])]
    pallas_call x4 -> x5, Pallas kernels: 8.36 us -> 9.1 us  [the longest x1 4.26 us: one_merge(): call(merge_kernel, 'merge', [shape(n, n), shape(rows, n)], in_specs=[IN_V...]
    ppermute x10 -> x11, starting transfers between devices: 12.6 us -> 12.7 us  [received(): lax.ppermute(part, axis, [(i, i ^ flip) for i in range(size)])]
  transfers between devices with their start and end apart: 12 -> 13, of which waited for: 9 -> 10; matrix products, arithmetic and copies ran while one was open for 0% -> 0% of each run, Pallas kernels for 9% -> 14%
where the time goes in v4:
time: 35.5 us; the launch traced here: 35.3 us
  starting transfers between devices  17.3 us (49%)
  Pallas kernels  9.1 us (26%)
  waiting for transfers between devices  8.16 us (23%)
  between operations  0.73 us (2%)
    ppermute x11, starting transfers between devices, received(): lax.ppermute(part, axis, [(i, i ^ flip) for i in range(size)])  12.7 us
    ppermute x11, waiting for transfers between devices, received(): lax.ppermute(part, axis, [(i, i ^ flip) for i in range(size)])  7.57 us
    ppermute x2, starting transfers between devices, passed_along(): return lax.ppermute(block, axis, route)  4.55 us
    pallas_call x1, Pallas kernels, one_merge(): call(merge_kernel, 'merge', [shape(n, n), shape(rows, n)], in_specs=[IN_V...  4.26 us
    pallas_call x1, Pallas kernels, one_merge(): call(leaf_kernel, 'leaf_roots', [shape(2 * n, n), shape(2, 2 * n, 4 * n,...  2.45 us
    pallas_call x1, Pallas kernels, one_merge(): call(gram_kernel, 'own_gram', shape(n, n), in_specs=[pl.BlockSpec(memory_...  1.54 us
  transfers between devices with their start and end apart: 13, of which 10 were waited for; matrix products, arithmetic and copies ran while one was open for 0% of the time, Pallas kernels for 14%

profile of v4, /device:TPU:0, one launch (start us, length us, event | category | flops | bytes accessed | tf_op | source)
XLA Modules:
  0.0 35.3 jit_solution(13355033418454216779)
XLA Ops:
  0.6 3.0 %collective-permute-start = (f32[1024,128]{1,0:T(8,128)}, f32[1024,128]{1,0:T(8,128)S(1)}, u32[]{:S(2)}, u32[]{:S(2)}) collective-permute-start(f32[1024,128]{1,0:T(8,128)} %own_ref.3), channel_id=1, source_target_pairs={{16,0},{0,16},{17,1},{1,17},{18,2},{2,18},{19,3},{3,19},{20,4},{4,... | collective-permute-start | bytes 1572872 | tf_op jit(solution)/shard_map/ppermute | solution.py:205
  3.6 1.5 %own_gram.1 = f32[128,128]{1,0:T(8,128)S(1)} custom-call(f32[1024,128]{1,0:T(8,128)} %own_ref.3), custom_call_target="tpu_custom_call" | custom-call | tf_op jit(solution)/shard_map/own_gram/pallas_call | solution.py:250
  5.2 2.6 %collective-permute-start.5 = (f32[128,128]{1,0:T(8,128)S(1)}, f32[128,128]{1,0:T(8,128)S(1)}, u32[]{:S(2)}, u32[]{:S(2)}) collective-permute-start(f32[128,128]{1,0:T(8,128)S(1)} %own_gram.1), channel_id=1, source_target_pairs={{0,6},{1,7},{2,4},{3,5},{4,2},{5,3},{6,0},{7,1},{8,14},{9,15},{10,... | collective-permute-start | bytes 196616 | tf_op jit(solution)/shard_map/ppermute | solution.py:220
  7.8 0.4 %collective-permute-start.4 = (f32[128,128]{1,0:T(8,128)S(1)}, f32[128,128]{1,0:T(8,128)S(1)}, u32[]{:S(2)}, u32[]{:S(2)}) collective-permute-start(f32[128,128]{1,0:T(8,128)S(1)} %own_gram.1), channel_id=1, source_target_pairs={{0,4},{1,5},{2,6},{3,7},{4,0},{5,1},{6,2},{7,3},{8,12},{9,13},{10,... | collective-permute-start | bytes 196616 | tf_op jit(solution)/shard_map/ppermute | solution.py:220
  8.2 0.5 %collective-permute-start.3 = (f32[128,128]{1,0:T(8,128)S(1)}, f32[128,128]{1,0:T(8,128)S(1)}, u32[]{:S(2)}, u32[]{:S(2)}) collective-permute-start(f32[128,128]{1,0:T(8,128)S(1)} %own_gram.1), channel_id=1, source_target_pairs={{0,2},{1,3},{2,0},{3,1},{4,6},{5,7},{6,4},{7,5},{8,10},{9,11},{10,... | collective-permute-start | bytes 196616 | tf_op jit(solution)/shard_map/ppermute | solution.py:220
  8.7 2.4 %collective-permute-done.5 = f32[128,128]{1,0:T(8,128)S(1)} collective-permute-done((f32[128,128]{1,0:T(8,128)S(1)}, f32[128,128]{1,0:T(8,128)S(1)}, u32[]{:S(2)}, u32[]{:S(2)}) %collective-permute-start.5) | collective-permute-done | bytes 65568 | tf_op jit(solution)/shard_map/ppermute | solution.py:220
  11.1 0.9 %collective-permute-done.4 = f32[128,128]{1,0:T(8,128)S(1)} collective-permute-done((f32[128,128]{1,0:T(8,128)S(1)}, f32[128,128]{1,0:T(8,128)S(1)}, u32[]{:S(2)}, u32[]{:S(2)}) %collective-permute-start.4) | collective-permute-done | bytes 65568 | tf_op jit(solution)/shard_map/ppermute | solution.py:220
  12.1 0.4 %collective-permute-done.3 = f32[128,128]{1,0:T(8,128)S(1)} collective-permute-done((f32[128,128]{1,0:T(8,128)S(1)}, f32[128,128]{1,0:T(8,128)S(1)}, u32[]{:S(2)}, u32[]{:S(2)}) %collective-permute-start.3) | collective-permute-done | bytes 65568 | tf_op jit(solution)/shard_map/ppermute | solution.py:220
  12.5 2.7 %collective-permute-start.6 = (f32[128,128]{1,0:T(8,128)S(1)}, f32[128,128]{1,0:T(8,128)S(1)}, u32[]{:S(2)}, u32[]{:S(2)}) collective-permute-start(f32[128,128]{1,0:T(8,128)S(1)} %add_add_fusion), channel_id=1, source_target_pairs={{0,8},{1,9},{2,10},{3,11},{4,12},{5,13},{6,14},{7,15},{8,0},{9,1},... | collective-permute-start | bytes 196616 | tf_op jit(solution)/shard_map/ppermute | solution.py:220
  15.2 0.6 %collective-permute-done.left_ref.lower_ref = f32[1024,128]{1,0:T(8,128)S(1)} collective-permute-done((f32[1024,128]{1,0:T(8,128)}, f32[1024,128]{1,0:T(8,128)S(1)}, u32[]{:S(2)}, u32[]{:S(2)}) %collective-permute-start) | collective-permute-done | bytes 524320 | tf_op jit(solution)/shard_map/ppermute | solution.py:205
  15.8 0.5 %cross_gram.1 = (f32[64,128]{1,0:T(8,128)S(1)}, f32[64,128]{1,0:T(8,128)S(1)}) custom-call(f32[1024,128]{1,0:T(8,128)S(1)} %collective-permute-done.left_ref.lower_ref, f32[1024,128]{1,0:T(8,128)S(1)} %copy-done), custom_call_target="tpu_custom_call" | custom-call | tf_op jit(solution)/shard_map/cross_gram/pallas_call | solution.py:260
  16.3 0.4 %raw_parts.1 = (bf16[1024,256]{1,0:T(8,128)(2,1)S(1)}, bf16[1024,256]{1,0:T(8,128)(2,1)S(1)}, bf16[1024,256]{1,0:T(8,128)(2,1)S(1)}) custom-call(f32[1024,128]{1,0:T(8,128)S(1)} %collective-permute-done.left_ref.lower_ref, f32[1024,128]{1,0:T(8,128)S(1)} %copy-done), custom_call_target="tpu_custom_call" | custom-call | tf_op jit(solution)/shard_map/raw_parts/pallas_call | solution.py:263
  16.7 0.8 %collective-permute-done.1 = f32[64,128]{1,0:T(8,128)S(1)} collective-permute-done((f32[64,128]{1,0:T(8,128)S(1)}, f32[64,128]{1,0:T(8,128)S(1)}, u32[]{:S(2)}, u32[]{:S(2)}) %collective-permute-start.1) | collective-permute-done | bytes 32800 | tf_op jit(solution)/shard_map/ppermute | solution.py:220
  17.9 2.8 %collective-permute-start.2 = (f32[64,128]{1,0:T(8,128)S(1)}, f32[64,128]{1,0:T(8,128)S(1)}, u32[]{:S(2)}, u32[]{:S(2)}) collective-permute-start(f32[64,128]{1,0:T(8,128)S(1)} %add.30), channel_id=1, source_target_pairs={{0,8},{1,9},{2,10},{3,11},{4,12},{5,13},{6,14},{7,15},{8,0},{9,1},... | collective-permute-start | bytes 98312 | tf_op jit(solution)/shard_map/ppermute | solution.py:220
  20.7 1.5 %collective-permute-start.11 = (f32[128,128]{1,0:T(8,128)S(1)}, f32[128,128]{1,0:T(8,128)S(1)}, u32[]{:S(2)}, u32[]{:S(2)}) collective-permute-start(f32[128,128]{1,0:T(8,128)S(1)} %add.35.own_ref), channel_id=1, source_target_pairs={{16,0},{0,16},{17,1},{1,17},{18,2},{2,18},{19,3},{3,19},{20,4},{4,... | collective-permute-start | bytes 196616 | tf_op jit(solution)/shard_map/ppermute | solution.py:205
  22.2 0.5 %collective-permute-done.2 = f32[64,128]{1,0:T(8,128)S(1)} collective-permute-done((f32[64,128]{1,0:T(8,128)S(1)}, f32[64,128]{1,0:T(8,128)S(1)}, u32[]{:S(2)}, u32[]{:S(2)}) %collective-permute-start.2) | collective-permute-done | bytes 32800 | tf_op jit(solution)/shard_map/ppermute | solution.py:220
  22.7 2.7 %collective-permute-start.10 = (f32[64,128]{1,0:T(8,128)S(1)}, f32[64,128]{1,0:T(8,128)S(1)}, u32[]{:S(2)}, u32[]{:S(2)}) collective-permute-start(f32[64,128]{1,0:T(8,128)S(1)} %add.36), channel_id=1, source_target_pairs={{0,6},{1,7},{2,4},{3,5},{4,2},{5,3},{6,0},{7,1},{8,14},{9,15},{10,... | collective-permute-start | bytes 98312 | tf_op jit(solution)/shard_map/ppermute | solution.py:220
  25.4 0.4 %collective-permute-start.9 = (f32[64,128]{1,0:T(8,128)S(1)}, f32[64,128]{1,0:T(8,128)S(1)}, u32[]{:S(2)}, u32[]{:S(2)}) collective-permute-start(f32[64,128]{1,0:T(8,128)S(1)} %add.36), channel_id=1, source_target_pairs={{0,4},{1,5},{2,6},{3,7},{4,0},{5,1},{6,2},{7,3},{8,12},{9,13},{10,... | collective-permute-start | bytes 98312 | tf_op jit(solution)/shard_map/ppermute | solution.py:220
  25.9 0.4 %collective-permute-start.8 = (f32[64,128]{1,0:T(8,128)S(1)}, f32[64,128]{1,0:T(8,128)S(1)}, u32[]{:S(2)}, u32[]{:S(2)}) collective-permute-start(f32[64,128]{1,0:T(8,128)S(1)} %add.36), channel_id=1, source_target_pairs={{0,2},{1,3},{2,0},{3,1},{4,6},{5,7},{6,4},{7,5},{8,10},{9,11},{10,... | collective-permute-start | bytes 98312 | tf_op jit(solution)/shard_map/ppermute | solution.py:220
  26.2 2.4 %leaf_roots.1 = (f32[256,128]{1,0:T(8,128)S(1)}, bf16[2,256,512]{2,1,0:T(8,128)(2,1)S(1)}, bf16[2,256,256]{2,1,0:T(8,128)(2,1)S(1)}, bf16[2,2,256,256]{3,2,1,0:T(8,128)(2,1)S(1)}) custom-call(f32[128,128]{1,0:T(8,128)S(1)} %collective-permute-done.11.lower_ref, f32[128,128]{1,0:T(8,128)S(1)} %add.35.own_ref, f32[256,128]{1,0:T(8,128)S(1)} %bitcast.1), custom_call_target="tpu_custom_call" | custom-call | tf_op jit(solution)/shard_map/leaf_roots/pallas_call | solution.py:272
  28.7 0.6 %collective-permute-done.9 = f32[64,128]{1,0:T(8,128)S(1)} collective-permute-done((f32[64,128]{1,0:T(8,128)S(1)}, f32[64,128]{1,0:T(8,128)S(1)}, u32[]{:S(2)}, u32[]{:S(2)}) %collective-permute-start.9) | collective-permute-done | bytes 32800 | tf_op jit(solution)/shard_map/ppermute | solution.py:220
  29.3 0.4 %collective-permute-done.8 = f32[64,128]{1,0:T(8,128)S(1)} collective-permute-done((f32[64,128]{1,0:T(8,128)S(1)}, f32[64,128]{1,0:T(8,128)S(1)}, u32[]{:S(2)}, u32[]{:S(2)}) %collective-permute-start.8) | collective-permute-done | bytes 32800 | tf_op jit(solution)/shard_map/ppermute | solution.py:220
  29.9 1.2 %collective-permute-done.12.theirs_ref = f32[64,128]{1,0:T(8,128)S(1)} collective-permute-done((f32[64,128]{1,0:T(8,128)S(1)}, f32[64,128]{1,0:T(8,128)S(1)}, u32[]{:S(2)}, u32[]{:S(2)}) %collective-permute-start.12) | collective-permute-done | bytes 32800 | tf_op jit(solution)/shard_map/ppermute | solution.py:220
  31.1 4.3 %merge.1 = (f32[128,128]{1,0:T(8,128)}, f32[1024,128]{1,0:T(8,128)}) custom-call(f32[64,128]{1,0:T(8,128)S(1)} %add_add_fusion.1.mine_ref, f32[64,128]{1,0:T(8,128)S(1)} %collective-permute-done.12.theirs_ref, f32[256,128]{1,0:T(8,128)S(1)} %get-tuple-element.39.f_ref, bf16[2,256,512]{2,1,0:T(8,128)(2,1)S(1)} %get-tuple-element.40.wide_ref, ...), custom_call_target="tpu_custom_call" | custom-call | tf_op jit(solution)/shard_map/merge/pallas_call | solution.py:293
  (17 shorter events, 0.5 us)
Async XLA Ops:
  0.6 15.2 %copy-start = (f32[1024,128]{1,0:T(8,128)S(1)}, f32[1024,128]{1,0:T(8,128)}, u32[]{:S(2)}) copy-start(f32[1024,128]{1,0:T(8,128)} %own_ref.3) | copy-start | bytes 1572868
  0.6 15.1 %collective-permute-start = (f32[1024,128]{1,0:T(8,128)}, f32[1024,128]{1,0:T(8,128)S(1)}, u32[]{:S(2)}, u32[]{:S(2)}) collective-permute-start(f32[1024,128]{1,0:T(8,128)} %own_ref.3), channel_id=1, source_target_pairs={{16,0},{0,16},{17,1},{1,17},{18,2},{2,18},{19,3},{3,19},{20,4},{4,... | collective-permute-start | bytes 1572872 | tf_op jit(solution)/shard_map/ppermute | solution.py:205
  5.2 5.9 %collective-permute-start.5 = (f32[128,128]{1,0:T(8,128)S(1)}, f32[128,128]{1,0:T(8,128)S(1)}, u32[]{:S(2)}, u32[]{:S(2)}) collective-permute-start(f32[128,128]{1,0:T(8,128)S(1)} %own_gram.1), channel_id=1, source_target_pairs={{0,6},{1,7},{2,4},{3,5},{4,2},{5,3},{6,0},{7,1},{8,14},{9,15},{10,... | collective-permute-start | bytes 196616 | tf_op jit(solution)/shard_map/ppermute | solution.py:220
  7.8 4.3 %collective-permute-start.4 = (f32[128,128]{1,0:T(8,128)S(1)}, f32[128,128]{1,0:T(8,128)S(1)}, u32[]{:S(2)}, u32[]{:S(2)}) collective-permute-start(f32[128,128]{1,0:T(8,128)S(1)} %own_gram.1), channel_id=1, source_target_pairs={{0,4},{1,5},{2,6},{3,7},{4,0},{5,1},{6,2},{7,3},{8,12},{9,13},{10,... | collective-permute-start | bytes 196616 | tf_op jit(solution)/shard_map/ppermute | solution.py:220
  8.2 4.3 %collective-permute-start.3 = (f32[128,128]{1,0:T(8,128)S(1)}, f32[128,128]{1,0:T(8,128)S(1)}, u32[]{:S(2)}, u32[]{:S(2)}) collective-permute-start(f32[128,128]{1,0:T(8,128)S(1)} %own_gram.1), channel_id=1, source_target_pairs={{0,2},{1,3},{2,0},{3,1},{4,6},{5,7},{6,4},{7,5},{8,10},{9,11},{10,... | collective-permute-start | bytes 196616 | tf_op jit(solution)/shard_map/ppermute | solution.py:220
  12.5 5.2 %collective-permute-start.6 = (f32[128,128]{1,0:T(8,128)S(1)}, f32[128,128]{1,0:T(8,128)S(1)}, u32[]{:S(2)}, u32[]{:S(2)}) collective-permute-start(f32[128,128]{1,0:T(8,128)S(1)} %add_add_fusion), channel_id=1, source_target_pairs={{0,8},{1,9},{2,10},{3,11},{4,12},{5,13},{6,14},{7,15},{8,0},{9,1},... | collective-permute-start | bytes 196616 | tf_op jit(solution)/shard_map/ppermute | solution.py:220
  16.3 1.3 %collective-permute-start.1 = (f32[64,128]{1,0:T(8,128)S(1)}, f32[64,128]{1,0:T(8,128)S(1)}, u32[]{:S(2)}, u32[]{:S(2)}) collective-permute-start(f32[64,128]{1,0:T(8,128)S(1)} %get-tuple-element.25), channel_id=1, source_target_pairs={{0,1},{1,0},{2,3},{3,2},{4,5},{5,4},{6,7},{7,6},{8,9},{9,8},{10,11... | collective-permute-start | bytes 98312 | tf_op jit(solution)/shard_map/ppermute | solution.py:220
  17.8 8.5 %copy-start.1 = (f32[1,256,128]{2,1,0:T(8,128)S(1)}, f32[1,256,128]{2,1,0:T(8,128)}, u32[]{:S(2)}) copy-start(f32[1,256,128]{2,1,0:T(8,128)} %param.3) | copy-start | bytes 393220
  17.8 2.9 %collective-permute-start.7 = (f32[128,128]{1,0:T(8,128)S(1)}, f32[128,128]{1,0:T(8,128)S(1)}, u32[]{:S(2)}, u32[]{:S(2)}) collective-permute-start(f32[128,128]{1,0:T(8,128)S(1)} %add.34), channel_id=1, source_target_pairs={{0,1},{1,0},{2,3},{3,2},{4,5},{5,4},{6,7},{7,6},{8,9},{9,8},{10,11... | collective-permute-start | bytes 196616 | tf_op jit(solution)/shard_map/ppermute | solution.py:220
  17.9 4.9 %collective-permute-start.2 = (f32[64,128]{1,0:T(8,128)S(1)}, f32[64,128]{1,0:T(8,128)S(1)}, u32[]{:S(2)}, u32[]{:S(2)}) collective-permute-start(f32[64,128]{1,0:T(8,128)S(1)} %add.30), channel_id=1, source_target_pairs={{0,8},{1,9},{2,10},{3,11},{4,12},{5,13},{6,14},{7,15},{8,0},{9,1},... | collective-permute-start | bytes 98312 | tf_op jit(solution)/shard_map/ppermute | solution.py:220
  20.7 5.6 %collective-permute-start.11 = (f32[128,128]{1,0:T(8,128)S(1)}, f32[128,128]{1,0:T(8,128)S(1)}, u32[]{:S(2)}, u32[]{:S(2)}) collective-permute-start(f32[128,128]{1,0:T(8,128)S(1)} %add.35.own_ref), channel_id=1, source_target_pairs={{16,0},{0,16},{17,1},{1,17},{18,2},{2,18},{19,3},{3,19},{20,4},{4,... | collective-permute-start | bytes 196616 | tf_op jit(solution)/shard_map/ppermute | solution.py:205
  22.7 5.9 %collective-permute-start.10 = (f32[64,128]{1,0:T(8,128)S(1)}, f32[64,128]{1,0:T(8,128)S(1)}, u32[]{:S(2)}, u32[]{:S(2)}) collective-permute-start(f32[64,128]{1,0:T(8,128)S(1)} %add.36), channel_id=1, source_target_pairs={{0,6},{1,7},{2,4},{3,5},{4,2},{5,3},{6,0},{7,1},{8,14},{9,15},{10,... | collective-permute-start | bytes 98312 | tf_op jit(solution)/shard_map/ppermute | solution.py:220
  25.4 3.9 %collective-permute-start.9 = (f32[64,128]{1,0:T(8,128)S(1)}, f32[64,128]{1,0:T(8,128)S(1)}, u32[]{:S(2)}, u32[]{:S(2)}) collective-permute-start(f32[64,128]{1,0:T(8,128)S(1)} %add.36), channel_id=1, source_target_pairs={{0,4},{1,5},{2,6},{3,7},{4,0},{5,1},{6,2},{7,3},{8,12},{9,13},{10,... | collective-permute-start | bytes 98312 | tf_op jit(solution)/shard_map/ppermute | solution.py:220
  25.9 3.9 %collective-permute-start.8 = (f32[64,128]{1,0:T(8,128)S(1)}, f32[64,128]{1,0:T(8,128)S(1)}, u32[]{:S(2)}, u32[]{:S(2)}) collective-permute-start(f32[64,128]{1,0:T(8,128)S(1)} %add.36), channel_id=1, source_target_pairs={{0,2},{1,3},{2,0},{3,1},{4,6},{5,7},{6,4},{7,5},{8,10},{9,11},{10,... | collective-permute-start | bytes 98312 | tf_op jit(solution)/shard_map/ppermute | solution.py:220
  29.8 1.3 %collective-permute-start.12 = (f32[64,128]{1,0:T(8,128)S(1)}, f32[64,128]{1,0:T(8,128)S(1)}, u32[]{:S(2)}, u32[]{:S(2)}) collective-permute-start(f32[64,128]{1,0:T(8,128)S(1)} %add_add_fusion.1.mine_ref), channel_id=1, source_target_pairs={{0,1},{1,0},{2,3},{3,2},{4,5},{5,4},{6,7},{7,6},{8,9},{9,8},{10,11... | collective-permute-start | bytes 98312 | tf_op jit(solution)/shard_map/ppermute | solution.py:220

commit v5 on v4

--- a/solution.py
+++ b/solution.py
@@ -28,6 +28,10 @@
 
 def dot_t(left, right):
     return lax.dot_general(left, right, (((0,), (0,)), ((), ())), preferred_element_type=F32)
+
+
+def dot_nt(left, right):
+    return lax.dot_general(left, right, (((1,), (1,)), ((), ())), preferred_element_type=F32)
 
 
 def mul(left, right):
@@ -49,18 +53,26 @@
     return wide[:k, :n] + ((wide[:k, n:] + wide[k : 2 * k, :n]) + (wide[k : 2 * k, n:] + (wide[2 * k :, :n] + small)))
 
 
+def mul_nt(left, right):
+    k, n = left[0].shape[0], right[0].shape[0]
+    wide = dot_nt(jnp.concatenate(left, 0), jnp.concatenate(right[:2], 0))
+    small = dot_nt(left[0], right[2])
+    return wide[:k, :n] + ((wide[:k, n:] + wide[k : 2 * k, :n]) + (wide[k : 2 * k, n:] + (wide[2 * k :, :n] + small)))
+
+
 def identity(size):
     return (
         lax.broadcasted_iota(jnp.int32, (size, size), 0) == lax.broadcasted_iota(jnp.int32, (size, size), 1)
     ).astype(F32)
 
 
-def root_iteration(matrices):
+def root_iteration(matrices, beside=lambda step: None):
     eye = identity(matrices[0].shape[0])
     squares = []
     for a in matrices:
         parts = split(a)
         squares.append(mul(parts, parts))
+    beside(0)
     scales = [jnp.sqrt(jnp.sum(a * a, keepdims=True) + 1e-06) for a in matrices]
     ys, zs = [], []
     for a, square, scale in zip(matrices, squares, scales):
@@ -73,25 +85,17 @@
         middles = [1.5 * eye - 0.5 * mul(z, y) for z, y in zip(z_parts, y_parts)]
         if repeat == NS_STEPS - 1:
             return zs, middles, scales
+        beside(2 * repeat - 1)
         m_parts = [split(m) for m in middles]
         ys = [mul(y, m) for y, m in zip(y_parts, m_parts)]
         zs = [mul(m, z) for z, m in zip(z_parts, m_parts)]
-
-
-def gram_kernel(x_ref, out_ref, buffer_ref, sems):
+        beside(2 * repeat)
+
+
+def gram_kernel(x_ref, out_ref):
     k = x_ref.shape[1]
-    chunks = sems.shape[0]
-    step = x_ref.shape[0] // chunks
-    slices = [slice(at * step, (at + 1) * step) for at in range(chunks)]
-    copies = [pltpu.make_async_copy(x_ref.at[s], buffer_ref.at[s], sems.at[at]) for at, s in enumerate(slices)]
-    for copy in copies:
-        copy.start()
-    wide = None
-    for s, copy in zip(slices, copies):
-        copy.wait()
-        h, m, l = split(buffer_ref[s, :])
-        piece = dot_t(jnp.concatenate([h, m, l], 1), jnp.concatenate([h, m], 1))
-        wide = piece if wide is None else wide + piece
+    h, m, l = split(x_ref[...])
+    wide = dot_t(jnp.concatenate([h, m, l], 1), jnp.concatenate([h, m], 1))
     cross = wide[:k, k:] + wide[2 * k :, :k]
     out_ref[...] = (wide[:k, :k] + wide[k : 2 * k, k:]) + (cross + cross.T)
 
@@ -132,61 +136,70 @@
         high_ref[:, columns], middle_ref[:, columns], low_ref[:, columns] = split(ref[...])
 
 
-def leaf_kernel(lower_ref, own_ref, sketch_ref, f_ref, wide_ref, small_ref, left_ref):
+def leaf_kernel(lower_ref, own_ref, sketch_ref, f_ref, left_ref, wide_ref, small_ref):
     n = own_ref.shape[0]
     grams = [lower_ref[...], own_ref[...]]
     zs, middles, scales = root_iteration(grams)
     roots = [mul(split(m), split(z)) * lax.rsqrt(c) for z, m, c in zip(zs, middles, scales)]
     for at, (gram, root) in enumerate(zip(grams, roots)):
-        rows = slice(at * n, (at + 1) * n)
         root_parts, gram_parts = split(root), split(gram)
-        e = split(mul(root_parts, split(sketch_ref[rows, :])))
-        m = split(mul(root_parts, split(root.T)))
-        wide_ref[at], small_ref[at] = weights([jnp.concatenate([a, b], 1) for a, b in zip(e, m)])
-        f_ref[rows, :] = mul(gram_parts, e)
-        left_ref[at, 0, :n], left_ref[at, 1, :n] = packed(m)
-        left_ref[at, 0, n:], left_ref[at, 1, n:] = packed(split(mul(gram_parts, m)))
+        e = mul(root_parts, split(sketch_ref[at * n : (at + 1) * n, :]))
+        m = mul(root_parts, split(root.T))
+        lefts = packed(split(jnp.concatenate([e.T, m], 0)))
+        products = mul_packed(lefts, weights(gram_parts))
+        f_ref[at] = products[:n]
+        left_ref[at, 0], left_ref[at, 1] = lefts
+        wide_ref[at], small_ref[at] = weights(split(jnp.concatenate([m, products[n:]], 1)))
 
 
 def merge_kernel(
-    mine_ref, theirs_ref, f_ref, wide_ref, small_ref, left_ref, high_ref, middle_ref, low_ref, own_ref,
-    coef_ref, out_ref, coef_stage_ref, stage_ref, coef_sem, sems,
+    mine_ref, theirs_ref, f_ref, left_ref, wide_ref, small_ref, high_ref, middle_ref, low_ref, own_ref,
+    coef_ref, out_ref, coef_stage_ref, stage_ref, wide_modes_ref, small_modes_ref, coef_sem, sems,
 ):
     n = mine_ref.shape[1]
     upper = upper_half()
     mine, theirs = mine_ref[...], theirs_ref[...]
     cross = jnp.concatenate([jnp.where(upper, theirs, mine), jnp.where(upper, mine, theirs)], 0)
-    right = mul_packed(packed(split(cross)), (wide_ref[1], small_ref[1]))
-    left = mul_packed(packed(split(cross.T)), (wide_ref[0], small_ref[0]))
-    results = []
-    for at, part, other in ((0, right, left), (1, left, right)):
-        f = weights(split(f_ref[at * n : (at + 1) * n, :] + part[:, :n]))
-        extra = packed(split(other[:, n:]))
-        lefts = [jnp.concatenate([left_ref[at, k], extra[k]], 0) for k in range(2)]
-        results.append(mul_packed(lefts, f))
-    lower, own = results
-    v = jnp.concatenate([lower[:n], own[:n]], 0)
-    p = jnp.concatenate([lower[n : 2 * n] + own[2 * n :], lower[2 * n :] + own[n : 2 * n]], 0)
-    (z,), (middle,), (scale,) = root_iteration([mul_t(split(v), split(p))])
-    both = mul(split(jnp.concatenate([v, p[n:]], 0)), split(z))
-    both = mul(split(both), split(middle)) * lax.rsqrt(scale)
-    coefficients = both[2 * n :].T
+    from_lower = mul_packed((left_ref[0, 0], left_ref[0, 1]), weights(split(cross)))
+    from_own = mul_packed((left_ref[1, 0], left_ref[1, 1]), weights(split(cross.T)))
+    lower_f, own_f = split(f_ref[0] + from_own[:n]), split(f_ref[1] + from_lower[:n])
+    lower = mul_packed(packed(lower_f), (wide_ref[0], small_ref[0]))
+    own = mul_packed(packed(own_f), (wide_ref[1], small_ref[1]))
+    lower_p = lower[:, n:] + mul(own_f, split(from_own[n:]))
+    own_p = own[:, n:] + mul(lower_f, split(from_lower[n:]))
+    v = jnp.concatenate([lower[:, :n], own[:, :n]], 1)
+    p = jnp.concatenate([lower_p, own_p], 1)
+    rows, chunks = own_ref.shape[0], sems.shape[0]
+    step = rows // chunks
+    slices = [slice(at * step, (at + 1) * step) for at in range(chunks)]
+    v_high, v_middle, v_low = split(v.T)
+    v_both = jnp.concatenate([v_high, v_middle], 1)
+    pieces = 4
+
+    def one_piece(at):
+        if at >= pieces:
+            return
+        here = slice(at * rows // pieces, (at + 1) * rows // pieces)
+        high = high_ref[here, :]
+        first, second = dot(high, v_both), dot(middle_ref[here, :], v_both)
+        third = dot(low_ref[here, :], v_high) + dot(high, v_low)
+        modes = first[:, :n] + ((first[:, n:] + second[:, :n]) + (second[:, n:] + third))
+        wide_modes_ref[here, :], small_modes_ref[here, :] = packed(split(modes))
+
+    (z,), (middle,), (scale,) = root_iteration([mul_nt(split(v), split(p))], one_piece)
+    z_parts, middle_parts = split(z), split(middle)
+    zp = split(mul(z_parts, split(own_p)))
+    coefficients = mul(middle_parts, zp) * lax.rsqrt(scale)
     coef_stage_ref[...] = coefficients
     coef_copy = pltpu.make_async_copy(coef_stage_ref, coef_ref, coef_sem)
     coef_copy.start()
-    mixed = split(mul(split(both[: 2 * n]), split(coefficients)))
-    mixed_both = jnp.concatenate(mixed[:2], 1)
-    rows, chunks = own_ref.shape[0], sems.shape[0]
-    step = rows // chunks
+    mixed = mul(split(mul(middle_parts, middle_parts)), split(mul(z_parts, zp))) / scale
+    mixed_wide, mixed_small = weights(split(mixed))
     copies = []
-    for at in range(chunks):
-        here = slice(at * step, (at + 1) * step)
-        high = high_ref[here, :]
-        first, second = dot(high, mixed_both), dot(middle_ref[here, :], mixed_both)
-        third = dot(low_ref[here, :], mixed[0]) + dot(high, mixed[2])
-        stage_ref[here, :] = own_ref[here, :] - (
-            first[:, :n] + ((first[:, n:] + second[:, :n]) + (second[:, n:] + third))
-        )
+    for at, here in enumerate(slices):
+        wide = dot(wide_modes_ref[here, :], mixed_wide)
+        small = dot(small_modes_ref[here, :], mixed_small)
+        stage_ref[here, :] = own_ref[here, :] - (wide[:, :n] + (wide[:, n:] + small))
         copy = pltpu.make_async_copy(stage_ref.at[here], out_ref.at[here], sems.at[at])
         copy.start()
         copies.append(copy)
@@ -247,14 +260,7 @@
     rows, n = snapshots.shape
     lower = passed_along(snapshots, "tm", 1)
     stages = stages_of(lax.axis_size("row"))
-    gram = call(
-        gram_kernel,
-        "own_gram",
-        shape(n, n),
-        in_specs=[pl.BlockSpec(memory_space=pltpu.HBM)],
-        out_specs=IN_VMEM,
-        scratch_shapes=[pltpu.VMEM((rows, n), F32), pltpu.SemaphoreType.DMA((2,))],
-    )(pltpu.with_memory_space_constraint(snapshots, pltpu.HBM))
+    gram = call(gram_kernel, "own_gram", shape(n, n), in_specs=[IN_VMEM], out_specs=IN_VMEM)(snapshots)
     for bits in stages[1:-1]:
         gram = summed_over(gram, "row", bits)
     mine, theirs = call(
@@ -273,10 +279,10 @@
         leaf_kernel,
         "leaf_roots",
         [
-            shape(2 * n, n),
+            shape(2, n, n),
+            shape(2, 2, 2 * n, 2 * n, kind=BF16),
             shape(2, 2 * n, 4 * n, kind=BF16),
             shape(2, 2 * n, 2 * n, kind=BF16),
-            shape(2, 2, 2 * n, 2 * n, kind=BF16),
         ],
         in_specs=[IN_VMEM] * 3,
         out_specs=[IN_VMEM] * 4,
@@ -299,6 +305,8 @@
             scratch_shapes=[
                 pltpu.VMEM((n, n), F32),
                 pltpu.VMEM((rows, n), F32),
+                pltpu.VMEM((rows, 2 * n), BF16),
+                pltpu.VMEM((rows, 2 * n), BF16),
                 pltpu.SemaphoreType.DMA,
                 pltpu.SemaphoreType.DMA((chunks,)),
             ],
@@ -351,7 +359,8 @@
 
 def body(snapshots, sketches):
     tree_depth = lax.axis_size("tm").bit_length() - 1
-    if tree_depth == 1:
+    row_count = lax.axis_size("row")
+    if tree_depth == 1 and row_count >= 4 and row_count & (row_count - 1) == 0:
         return one_merge(snapshots, sketches[0])
     return many_merges(snapshots, sketches, tree_depth)
 

time: 35.5 us -> 35.2 us (level)
  Pallas kernels: 9.1 us -> 7.77 us
  local copies, waits for them, and re-layouts: 0.01 us -> 1.08 us
    unnamed x4 -> x6, local copies, waits for them, and re-layouts: 0.01 us -> 1.08 us
    pallas_call x2, Pallas kernels: 3.99 us -> 2.93 us  [the longest x1 2.45 us: one_merge(): call(leaf_kernel, 'leaf_roots', [shape(2, n, n), shape(2, 2, 2 * n, 2 * n...]
  transfers between devices with their start and end apart: 13 -> 13, of which waited for: 10 -> 10; matrix products, arithmetic and copies ran while one was open for 0% -> 0% of each run, Pallas kernels for 14% -> 11%
where the time goes in v5:
time: 35.2 us; the launch traced here: 35 us
  starting transfers between devices  17.2 us (49%)
  waiting for transfers between devices  8.16 us (23%)
  Pallas kernels  7.77 us (22%)
  local copies, waits for them, and re-layouts  1.08 us (3%)
  between operations  0.73 us (2%)
    ppermute x11, starting transfers between devices, received(): lax.ppermute(part, axis, [(i, i ^ flip) for i in range(size)])  12.7 us
    ppermute x11, waiting for transfers between devices, received(): lax.ppermute(part, axis, [(i, i ^ flip) for i in range(size)])  7.58 us
    ppermute x2, starting transfers between devices, passed_along(): return lax.ppermute(block, axis, route)  4.55 us
    pallas_call x1, Pallas kernels, one_merge(): call(merge_kernel, 'merge', [shape(n, n), shape(rows, n)], in_specs=[IN_V...  3.98 us
    pallas_call x1, Pallas kernels, one_merge(): call(leaf_kernel, 'leaf_roots', [shape(2, n, n), shape(2, 2, 2 * n, 2 * n...  2.45 us
    unnamed x6, local copies, waits for them, and re-layouts  1.08 us
  transfers between devices with their start and end apart: 13, of which 10 were waited for; matrix products, arithmetic and copies ran while one was open for 0% of the time, Pallas kernels for 11%

profile of v5, /device:TPU:0, one launch (start us, length us, event | category | flops | bytes accessed | tf_op | source)
XLA Modules:
  0.0 35.0 jit_solution(11797884674136573680)
XLA Ops:
  0.6 3.0 %collective-permute-start = (f32[1024,128]{1,0:T(8,128)}, f32[1024,128]{1,0:T(8,128)S(1)}, u32[]{:S(2)}, u32[]{:S(2)}) collective-permute-start(f32[1024,128]{1,0:T(8,128)} %own_ref.3), channel_id=1, source_target_pairs={{16,0},{0,16},{17,1},{1,17},{18,2},{2,18},{19,3},{3,19},{20,4},{4,... | collective-permute-start | bytes 1572872 | tf_op jit(solution)/shard_map/ppermute | solution.py:218
  3.6 1.1 %copy-done = f32[1024,128]{1,0:T(8,128)S(1)} copy-done((f32[1024,128]{1,0:T(8,128)S(1)}, f32[1024,128]{1,0:T(8,128)}, u32[]{:S(2)}) %copy-start) | copy-done | bytes 524312
  4.7 0.5 %own_gram.1 = f32[128,128]{1,0:T(8,128)S(1)} custom-call(f32[1024,128]{1,0:T(8,128)S(1)} %copy-done), custom_call_target="tpu_custom_call" | custom-call | tf_op jit(solution)/shard_map/own_gram/pallas_call | solution.py:263
  5.2 2.6 %collective-permute-start.5 = (f32[128,128]{1,0:T(8,128)S(1)}, f32[128,128]{1,0:T(8,128)S(1)}, u32[]{:S(2)}, u32[]{:S(2)}) collective-permute-start(f32[128,128]{1,0:T(8,128)S(1)} %own_gram.1), channel_id=1, source_target_pairs={{0,6},{1,7},{2,4},{3,5},{4,2},{5,3},{6,0},{7,1},{8,14},{9,15},{10,... | collective-permute-start | bytes 196616 | tf_op jit(solution)/shard_map/ppermute | solution.py:233
  7.8 0.4 %collective-permute-start.4 = (f32[128,128]{1,0:T(8,128)S(1)}, f32[128,128]{1,0:T(8,128)S(1)}, u32[]{:S(2)}, u32[]{:S(2)}) collective-permute-start(f32[128,128]{1,0:T(8,128)S(1)} %own_gram.1), channel_id=1, source_target_pairs={{0,4},{1,5},{2,6},{3,7},{4,0},{5,1},{6,2},{7,3},{8,12},{9,13},{10,... | collective-permute-start | bytes 196616 | tf_op jit(solution)/shard_map/ppermute | solution.py:233
  8.3 0.5 %collective-permute-start.3 = (f32[128,128]{1,0:T(8,128)S(1)}, f32[128,128]{1,0:T(8,128)S(1)}, u32[]{:S(2)}, u32[]{:S(2)}) collective-permute-start(f32[128,128]{1,0:T(8,128)S(1)} %own_gram.1), channel_id=1, source_target_pairs={{0,2},{1,3},{2,0},{3,1},{4,6},{5,7},{6,4},{7,5},{8,10},{9,11},{10,... | collective-permute-start | bytes 196616 | tf_op jit(solution)/shard_map/ppermute | solution.py:233
  8.8 2.4 %collective-permute-done.5 = f32[128,128]{1,0:T(8,128)S(1)} collective-permute-done((f32[128,128]{1,0:T(8,128)S(1)}, f32[128,128]{1,0:T(8,128)S(1)}, u32[]{:S(2)}, u32[]{:S(2)}) %collective-permute-start.5) | collective-permute-done | bytes 65568 | tf_op jit(solution)/shard_map/ppermute | solution.py:233
  11.1 0.9 %collective-permute-done.4 = f32[128,128]{1,0:T(8,128)S(1)} collective-permute-done((f32[128,128]{1,0:T(8,128)S(1)}, f32[128,128]{1,0:T(8,128)S(1)}, u32[]{:S(2)}, u32[]{:S(2)}) %collective-permute-start.4) | collective-permute-done | bytes 65568 | tf_op jit(solution)/shard_map/ppermute | solution.py:233
  12.1 0.4 %collective-permute-done.3 = f32[128,128]{1,0:T(8,128)S(1)} collective-permute-done((f32[128,128]{1,0:T(8,128)S(1)}, f32[128,128]{1,0:T(8,128)S(1)}, u32[]{:S(2)}, u32[]{:S(2)}) %collective-permute-start.3) | collective-permute-done | bytes 65568 | tf_op jit(solution)/shard_map/ppermute | solution.py:233
  12.5 2.7 %collective-permute-start.6 = (f32[128,128]{1,0:T(8,128)S(1)}, f32[128,128]{1,0:T(8,128)S(1)}, u32[]{:S(2)}, u32[]{:S(2)}) collective-permute-start(f32[128,128]{1,0:T(8,128)S(1)} %add_add_fusion), channel_id=1, source_target_pairs={{0,8},{1,9},{2,10},{3,11},{4,12},{5,13},{6,14},{7,15},{8,0},{9,1},... | collective-permute-start | bytes 196616 | tf_op jit(solution)/shard_map/ppermute | solution.py:233
  15.2 0.6 %collective-permute-done.left_ref.lower_ref = f32[1024,128]{1,0:T(8,128)S(1)} collective-permute-done((f32[1024,128]{1,0:T(8,128)}, f32[1024,128]{1,0:T(8,128)S(1)}, u32[]{:S(2)}, u32[]{:S(2)}) %collective-permute-start) | collective-permute-done | bytes 524320 | tf_op jit(solution)/shard_map/ppermute | solution.py:218
  15.8 0.5 %cross_gram.1 = (f32[64,128]{1,0:T(8,128)S(1)}, f32[64,128]{1,0:T(8,128)S(1)}) custom-call(f32[1024,128]{1,0:T(8,128)S(1)} %collective-permute-done.left_ref.lower_ref, f32[1024,128]{1,0:T(8,128)S(1)} %copy-done.1), custom_call_target="tpu_custom_call" | custom-call | tf_op jit(solution)/shard_map/cross_gram/pallas_call | solution.py:266
  16.7 0.8 %collective-permute-done.1 = f32[64,128]{1,0:T(8,128)S(1)} collective-permute-done((f32[64,128]{1,0:T(8,128)S(1)}, f32[64,128]{1,0:T(8,128)S(1)}, u32[]{:S(2)}, u32[]{:S(2)}) %collective-permute-start.1) | collective-permute-done | bytes 32800 | tf_op jit(solution)/shard_map/ppermute | solution.py:233
  17.9 2.8 %collective-permute-start.2 = (f32[64,128]{1,0:T(8,128)S(1)}, f32[64,128]{1,0:T(8,128)S(1)}, u32[]{:S(2)}, u32[]{:S(2)}) collective-permute-start(f32[64,128]{1,0:T(8,128)S(1)} %add.30), channel_id=1, source_target_pairs={{0,8},{1,9},{2,10},{3,11},{4,12},{5,13},{6,14},{7,15},{8,0},{9,1},... | collective-permute-start | bytes 98312 | tf_op jit(solution)/shard_map/ppermute | solution.py:233
  20.7 1.5 %collective-permute-start.11 = (f32[128,128]{1,0:T(8,128)S(1)}, f32[128,128]{1,0:T(8,128)S(1)}, u32[]{:S(2)}, u32[]{:S(2)}) collective-permute-start(f32[128,128]{1,0:T(8,128)S(1)} %add.35.own_ref), channel_id=1, source_target_pairs={{16,0},{0,16},{17,1},{1,17},{18,2},{2,18},{19,3},{3,19},{20,4},{4,... | collective-permute-start | bytes 196616 | tf_op jit(solution)/shard_map/ppermute | solution.py:218
  22.2 0.5 %collective-permute-done.2 = f32[64,128]{1,0:T(8,128)S(1)} collective-permute-done((f32[64,128]{1,0:T(8,128)S(1)}, f32[64,128]{1,0:T(8,128)S(1)}, u32[]{:S(2)}, u32[]{:S(2)}) %collective-permute-start.2) | collective-permute-done | bytes 32800 | tf_op jit(solution)/shard_map/ppermute | solution.py:233
  22.8 2.6 %collective-permute-start.10 = (f32[64,128]{1,0:T(8,128)S(1)}, f32[64,128]{1,0:T(8,128)S(1)}, u32[]{:S(2)}, u32[]{:S(2)}) collective-permute-start(f32[64,128]{1,0:T(8,128)S(1)} %add.36), channel_id=1, source_target_pairs={{0,6},{1,7},{2,4},{3,5},{4,2},{5,3},{6,0},{7,1},{8,14},{9,15},{10,... | collective-permute-start | bytes 98312 | tf_op jit(solution)/shard_map/ppermute | solution.py:233
  25.4 0.4 %collective-permute-start.9 = (f32[64,128]{1,0:T(8,128)S(1)}, f32[64,128]{1,0:T(8,128)S(1)}, u32[]{:S(2)}, u32[]{:S(2)}) collective-permute-start(f32[64,128]{1,0:T(8,128)S(1)} %add.36), channel_id=1, source_target_pairs={{0,4},{1,5},{2,6},{3,7},{4,0},{5,1},{6,2},{7,3},{8,12},{9,13},{10,... | collective-permute-start | bytes 98312 | tf_op jit(solution)/shard_map/ppermute | solution.py:233
  25.9 0.4 %collective-permute-start.8 = (f32[64,128]{1,0:T(8,128)S(1)}, f32[64,128]{1,0:T(8,128)S(1)}, u32[]{:S(2)}, u32[]{:S(2)}) collective-permute-start(f32[64,128]{1,0:T(8,128)S(1)} %add.36), channel_id=1, source_target_pairs={{0,2},{1,3},{2,0},{3,1},{4,6},{5,7},{6,4},{7,5},{8,10},{9,11},{10,... | collective-permute-start | bytes 98312 | tf_op jit(solution)/shard_map/ppermute | solution.py:233
  26.3 2.4 %leaf_roots.1 = (f32[2,128,128]{2,1,0:T(8,128)S(1)}, bf16[2,2,256,256]{3,2,1,0:T(8,128)(2,1)S(1)}, bf16[2,256,512]{2,1,0:T(8,128)(2,1)S(1)}, bf16[2,256,256]{2,1,0:T(8,128)(2,1)S(1)}) custom-call(f32[128,128]{1,0:T(8,128)S(1)} %collective-permute-done.11.lower_ref, f32[128,128]{1,0:T(8,128)S(1)} %add.35.own_ref, f32[256,128]{1,0:T(8,128)S(1)} %bitcast.1), custom_call_target="tpu_custom_call" | custom-call | tf_op jit(solution)/shard_map/leaf_roots/pallas_call | solution.py:278
  28.7 0.6 %collective-permute-done.9 = f32[64,128]{1,0:T(8,128)S(1)} collective-permute-done((f32[64,128]{1,0:T(8,128)S(1)}, f32[64,128]{1,0:T(8,128)S(1)}, u32[]{:S(2)}, u32[]{:S(2)}) %collective-permute-start.9) | collective-permute-done | bytes 32800 | tf_op jit(solution)/shard_map/ppermute | solution.py:233
  29.3 0.4 %collective-permute-done.8 = f32[64,128]{1,0:T(8,128)S(1)} collective-permute-done((f32[64,128]{1,0:T(8,128)S(1)}, f32[64,128]{1,0:T(8,128)S(1)}, u32[]{:S(2)}, u32[]{:S(2)}) %collective-permute-start.8) | collective-permute-done | bytes 32800 | tf_op jit(solution)/shard_map/ppermute | solution.py:233
  29.9 1.2 %collective-permute-done.12.theirs_ref = f32[64,128]{1,0:T(8,128)S(1)} collective-permute-done((f32[64,128]{1,0:T(8,128)S(1)}, f32[64,128]{1,0:T(8,128)S(1)}, u32[]{:S(2)}, u32[]{:S(2)}) %collective-permute-start.12) | collective-permute-done | bytes 32800 | tf_op jit(solution)/shard_map/ppermute | solution.py:233
  31.1 4.0 %merge.1 = (f32[128,128]{1,0:T(8,128)}, f32[1024,128]{1,0:T(8,128)}) custom-call(f32[64,128]{1,0:T(8,128)S(1)} %add_add_fusion.1.mine_ref, f32[64,128]{1,0:T(8,128)S(1)} %collective-permute-done.12.theirs_ref, f32[2,128,128]{2,1,0:T(8,128)S(1)} %get-tuple-element.39.f_ref, bf16[2,2,256,256]{3,2,1,0:T(8,128)(2,1)S(1)} %get-tuple-element.40.left_ref, ...), custom_call_target="tpu_custom_call" | custom-call | tf_op jit(solution)/shard_map/merge/pallas_call | solution.py:299
  (19 shorter events, 0.9 us)
Async XLA Ops:
  0.6 15.1 %collective-permute-start = (f32[1024,128]{1,0:T(8,128)}, f32[1024,128]{1,0:T(8,128)S(1)}, u32[]{:S(2)}, u32[]{:S(2)}) collective-permute-start(f32[1024,128]{1,0:T(8,128)} %own_ref.3), channel_id=1, source_target_pairs={{16,0},{0,16},{17,1},{1,17},{18,2},{2,18},{19,3},{3,19},{20,4},{4,... | collective-permute-start | bytes 1572872 | tf_op jit(solution)/shard_map/ppermute | solution.py:218
  3.6 1.1 %copy-start = (f32[1024,128]{1,0:T(8,128)S(1)}, f32[1024,128]{1,0:T(8,128)}, u32[]{:S(2)}) copy-start(f32[1024,128]{1,0:T(8,128)} %own_ref.3) | copy-start | bytes 1572868
  4.7 11.1 %copy-start.1 = (f32[1024,128]{1,0:T(8,128)S(1)}, f32[1024,128]{1,0:T(8,128)}, u32[]{:S(2)}) copy-start(f32[1024,128]{1,0:T(8,128)} %own_ref.3) | copy-start | bytes 1572868
  5.2 5.9 %collective-permute-start.5 = (f32[128,128]{1,0:T(8,128)S(1)}, f32[128,128]{1,0:T(8,128)S(1)}, u32[]{:S(2)}, u32[]{:S(2)}) collective-permute-start(f32[128,128]{1,0:T(8,128)S(1)} %own_gram.1), channel_id=1, source_target_pairs={{0,6},{1,7},{2,4},{3,5},{4,2},{5,3},{6,0},{7,1},{8,14},{9,15},{10,... | collective-permute-start | bytes 196616 | tf_op jit(solution)/shard_map/ppermute | solution.py:233
  7.8 4.3 %collective-permute-start.4 = (f32[128,128]{1,0:T(8,128)S(1)}, f32[128,128]{1,0:T(8,128)S(1)}, u32[]{:S(2)}, u32[]{:S(2)}) collective-permute-start(f32[128,128]{1,0:T(8,128)S(1)} %own_gram.1), channel_id=1, source_target_pairs={{0,4},{1,5},{2,6},{3,7},{4,0},{5,1},{6,2},{7,3},{8,12},{9,13},{10,... | collective-permute-start | bytes 196616 | tf_op jit(solution)/shard_map/ppermute | solution.py:233
  8.3 4.3 %collective-permute-start.3 = (f32[128,128]{1,0:T(8,128)S(1)}, f32[128,128]{1,0:T(8,128)S(1)}, u32[]{:S(2)}, u32[]{:S(2)}) collective-permute-start(f32[128,128]{1,0:T(8,128)S(1)} %own_gram.1), channel_id=1, source_target_pairs={{0,2},{1,3},{2,0},{3,1},{4,6},{5,7},{6,4},{7,5},{8,10},{9,11},{10,... | collective-permute-start | bytes 196616 | tf_op jit(solution)/shard_map/ppermute | solution.py:233
  12.5 5.2 %collective-permute-start.6 = (f32[128,128]{1,0:T(8,128)S(1)}, f32[128,128]{1,0:T(8,128)S(1)}, u32[]{:S(2)}, u32[]{:S(2)}) collective-permute-start(f32[128,128]{1,0:T(8,128)S(1)} %add_add_fusion), channel_id=1, source_target_pairs={{0,8},{1,9},{2,10},{3,11},{4,12},{5,13},{6,14},{7,15},{8,0},{9,1},... | collective-permute-start | bytes 196616 | tf_op jit(solution)/shard_map/ppermute | solution.py:233
  16.3 1.3 %collective-permute-start.1 = (f32[64,128]{1,0:T(8,128)S(1)}, f32[64,128]{1,0:T(8,128)S(1)}, u32[]{:S(2)}, u32[]{:S(2)}) collective-permute-start(f32[64,128]{1,0:T(8,128)S(1)} %get-tuple-element.25), channel_id=1, source_target_pairs={{0,1},{1,0},{2,3},{3,2},{4,5},{5,4},{6,7},{7,6},{8,9},{9,8},{10,11... | collective-permute-start | bytes 98312 | tf_op jit(solution)/shard_map/ppermute | solution.py:233
  17.8 8.5 %copy-start.2 = (f32[1,256,128]{2,1,0:T(8,128)S(1)}, f32[1,256,128]{2,1,0:T(8,128)}, u32[]{:S(2)}) copy-start(f32[1,256,128]{2,1,0:T(8,128)} %param.3) | copy-start | bytes 393220
  17.8 2.9 %collective-permute-start.7 = (f32[128,128]{1,0:T(8,128)S(1)}, f32[128,128]{1,0:T(8,128)S(1)}, u32[]{:S(2)}, u32[]{:S(2)}) collective-permute-start(f32[128,128]{1,0:T(8,128)S(1)} %add.34), channel_id=1, source_target_pairs={{0,1},{1,0},{2,3},{3,2},{4,5},{5,4},{6,7},{7,6},{8,9},{9,8},{10,11... | collective-permute-start | bytes 196616 | tf_op jit(solution)/shard_map/ppermute | solution.py:233
  17.9 4.9 %collective-permute-start.2 = (f32[64,128]{1,0:T(8,128)S(1)}, f32[64,128]{1,0:T(8,128)S(1)}, u32[]{:S(2)}, u32[]{:S(2)}) collective-permute-start(f32[64,128]{1,0:T(8,128)S(1)} %add.30), channel_id=1, source_target_pairs={{0,8},{1,9},{2,10},{3,11},{4,12},{5,13},{6,14},{7,15},{8,0},{9,1},... | collective-permute-start | bytes 98312 | tf_op jit(solution)/shard_map/ppermute | solution.py:233
  20.7 5.6 %collective-permute-start.11 = (f32[128,128]{1,0:T(8,128)S(1)}, f32[128,128]{1,0:T(8,128)S(1)}, u32[]{:S(2)}, u32[]{:S(2)}) collective-permute-start(f32[128,128]{1,0:T(8,128)S(1)} %add.35.own_ref), channel_id=1, source_target_pairs={{16,0},{0,16},{17,1},{1,17},{18,2},{2,18},{19,3},{3,19},{20,4},{4,... | collective-permute-start | bytes 196616 | tf_op jit(solution)/shard_map/ppermute | solution.py:218
  22.8 6.0 %collective-permute-start.10 = (f32[64,128]{1,0:T(8,128)S(1)}, f32[64,128]{1,0:T(8,128)S(1)}, u32[]{:S(2)}, u32[]{:S(2)}) collective-permute-start(f32[64,128]{1,0:T(8,128)S(1)} %add.36), channel_id=1, source_target_pairs={{0,6},{1,7},{2,4},{3,5},{4,2},{5,3},{6,0},{7,1},{8,14},{9,15},{10,... | collective-permute-start | bytes 98312 | tf_op jit(solution)/shard_map/ppermute | solution.py:233
  25.4 3.9 %collective-permute-start.9 = (f32[64,128]{1,0:T(8,128)S(1)}, f32[64,128]{1,0:T(8,128)S(1)}, u32[]{:S(2)}, u32[]{:S(2)}) collective-permute-start(f32[64,128]{1,0:T(8,128)S(1)} %add.36), channel_id=1, source_target_pairs={{0,4},{1,5},{2,6},{3,7},{4,0},{5,1},{6,2},{7,3},{8,12},{9,13},{10,... | collective-permute-start | bytes 98312 | tf_op jit(solution)/shard_map/ppermute | solution.py:233
  25.9 3.9 %collective-permute-start.8 = (f32[64,128]{1,0:T(8,128)S(1)}, f32[64,128]{1,0:T(8,128)S(1)}, u32[]{:S(2)}, u32[]{:S(2)}) collective-permute-start(f32[64,128]{1,0:T(8,128)S(1)} %add.36), channel_id=1, source_target_pairs={{0,2},{1,3},{2,0},{3,1},{4,6},{5,7},{6,4},{7,5},{8,10},{9,11},{10,... | collective-permute-start | bytes 98312 | tf_op jit(solution)/shard_map/ppermute | solution.py:233
  29.8 1.3 %collective-permute-start.12 = (f32[64,128]{1,0:T(8,128)S(1)}, f32[64,128]{1,0:T(8,128)S(1)}, u32[]{:S(2)}, u32[]{:S(2)}) collective-permute-start(f32[64,128]{1,0:T(8,128)S(1)} %add_add_fusion.1.mine_ref), channel_id=1, source_target_pairs={{0,1},{1,0},{2,3},{3,2},{4,5},{5,4},{6,7},{7,6},{8,9},{9,8},{10,11... | collective-permute-start | bytes 98312 | tf_op jit(solution)/shard_map/ppermute | solution.py:233

commit v6 on v5

--- a/solution.py
+++ b/solution.py
@@ -39,8 +39,8 @@
     rh, rm, rl = right
     n = rh.shape[1]
     both = jnp.concatenate([jnp.concatenate([rh, rm], 1), jnp.concatenate([rm, rh], 1)], 0)
+    small = dot(jnp.concatenate([ll, lh], 1), jnp.concatenate([rh, rl], 0))
     wide = dot(jnp.concatenate([lh, lm], 1), both)
-    small = dot(jnp.concatenate([ll, lh], 1), jnp.concatenate([rh, rl], 0))
     return wide[:, :n] + (wide[:, n:] + small)
 
 

time: 35.2 us -> 35.2 us (level)
  no operation moved by 1% of the time
where the time goes in v6:
time: 35.2 us; the launch traced here: 35 us
  starting transfers between devices  17.2 us (49%)
  waiting for transfers between devices  8.16 us (23%)
  Pallas kernels  7.77 us (22%)
  local copies, waits for them, and re-layouts  1.08 us (3%)
  between operations  0.73 us (2%)
    ppermute x11, starting transfers between devices, received(): lax.ppermute(part, axis, [(i, i ^ flip) for i in range(size)])  12.7 us
    ppermute x11, waiting for transfers between devices, received(): lax.ppermute(part, axis, [(i, i ^ flip) for i in range(size)])  7.58 us
    ppermute x2, starting transfers between devices, passed_along(): return lax.ppermute(block, axis, route)  4.55 us
    pallas_call x1, Pallas kernels, one_merge(): call(merge_kernel, 'merge', [shape(n, n), shape(rows, n)], in_specs=[IN_V...  3.97 us
    pallas_call x1, Pallas kernels, one_merge(): call(leaf_kernel, 'leaf_roots', [shape(2, n, n), shape(2, 2, 2 * n, 2 * n...  2.46 us
    unnamed x6, local copies, waits for them, and re-layouts  1.08 us
  transfers between devices with their start and end apart: 13, of which 10 were waited for; matrix products, arithmetic and copies ran while one was open for 0% of the time, Pallas kernels for 11%

profile of v6, /device:TPU:0, one launch (start us, length us, event | category | flops | bytes accessed | tf_op | source)
XLA Modules:
  0.0 35.0 jit_solution(4788629838375233497)
XLA Ops:
  0.6 3.0 %collective-permute-start = (f32[1024,128]{1,0:T(8,128)}, f32[1024,128]{1,0:T(8,128)S(1)}, u32[]{:S(2)}, u32[]{:S(2)}) collective-permute-start(f32[1024,128]{1,0:T(8,128)} %own_ref.3), channel_id=1, source_target_pairs={{16,0},{0,16},{17,1},{1,17},{18,2},{2,18},{19,3},{3,19},{20,4},{4,... | collective-permute-start | bytes 1572872 | tf_op jit(solution)/shard_map/ppermute | solution.py:218
  3.6 1.1 %copy-done = f32[1024,128]{1,0:T(8,128)S(1)} copy-done((f32[1024,128]{1,0:T(8,128)S(1)}, f32[1024,128]{1,0:T(8,128)}, u32[]{:S(2)}) %copy-start) | copy-done | bytes 524312
  4.7 0.5 %own_gram.1 = f32[128,128]{1,0:T(8,128)S(1)} custom-call(f32[1024,128]{1,0:T(8,128)S(1)} %copy-done), custom_call_target="tpu_custom_call" | custom-call | tf_op jit(solution)/shard_map/own_gram/pallas_call | solution.py:263
  5.2 2.6 %collective-permute-start.5 = (f32[128,128]{1,0:T(8,128)S(1)}, f32[128,128]{1,0:T(8,128)S(1)}, u32[]{:S(2)}, u32[]{:S(2)}) collective-permute-start(f32[128,128]{1,0:T(8,128)S(1)} %own_gram.1), channel_id=1, source_target_pairs={{0,6},{1,7},{2,4},{3,5},{4,2},{5,3},{6,0},{7,1},{8,14},{9,15},{10,... | collective-permute-start | bytes 196616 | tf_op jit(solution)/shard_map/ppermute | solution.py:233
  7.8 0.4 %collective-permute-start.4 = (f32[128,128]{1,0:T(8,128)S(1)}, f32[128,128]{1,0:T(8,128)S(1)}, u32[]{:S(2)}, u32[]{:S(2)}) collective-permute-start(f32[128,128]{1,0:T(8,128)S(1)} %own_gram.1), channel_id=1, source_target_pairs={{0,4},{1,5},{2,6},{3,7},{4,0},{5,1},{6,2},{7,3},{8,12},{9,13},{10,... | collective-permute-start | bytes 196616 | tf_op jit(solution)/shard_map/ppermute | solution.py:233
  8.3 0.5 %collective-permute-start.3 = (f32[128,128]{1,0:T(8,128)S(1)}, f32[128,128]{1,0:T(8,128)S(1)}, u32[]{:S(2)}, u32[]{:S(2)}) collective-permute-start(f32[128,128]{1,0:T(8,128)S(1)} %own_gram.1), channel_id=1, source_target_pairs={{0,2},{1,3},{2,0},{3,1},{4,6},{5,7},{6,4},{7,5},{8,10},{9,11},{10,... | collective-permute-start | bytes 196616 | tf_op jit(solution)/shard_map/ppermute | solution.py:233
  8.8 2.4 %collective-permute-done.5 = f32[128,128]{1,0:T(8,128)S(1)} collective-permute-done((f32[128,128]{1,0:T(8,128)S(1)}, f32[128,128]{1,0:T(8,128)S(1)}, u32[]{:S(2)}, u32[]{:S(2)}) %collective-permute-start.5) | collective-permute-done | bytes 65568 | tf_op jit(solution)/shard_map/ppermute | solution.py:233
  11.1 0.9 %collective-permute-done.4 = f32[128,128]{1,0:T(8,128)S(1)} collective-permute-done((f32[128,128]{1,0:T(8,128)S(1)}, f32[128,128]{1,0:T(8,128)S(1)}, u32[]{:S(2)}, u32[]{:S(2)}) %collective-permute-start.4) | collective-permute-done | bytes 65568 | tf_op jit(solution)/shard_map/ppermute | solution.py:233
  12.1 0.4 %collective-permute-done.3 = f32[128,128]{1,0:T(8,128)S(1)} collective-permute-done((f32[128,128]{1,0:T(8,128)S(1)}, f32[128,128]{1,0:T(8,128)S(1)}, u32[]{:S(2)}, u32[]{:S(2)}) %collective-permute-start.3) | collective-permute-done | bytes 65568 | tf_op jit(solution)/shard_map/ppermute | solution.py:233
  12.5 2.7 %collective-permute-start.6 = (f32[128,128]{1,0:T(8,128)S(1)}, f32[128,128]{1,0:T(8,128)S(1)}, u32[]{:S(2)}, u32[]{:S(2)}) collective-permute-start(f32[128,128]{1,0:T(8,128)S(1)} %add_add_fusion), channel_id=1, source_target_pairs={{0,8},{1,9},{2,10},{3,11},{4,12},{5,13},{6,14},{7,15},{8,0},{9,1},... | collective-permute-start | bytes 196616 | tf_op jit(solution)/shard_map/ppermute | solution.py:233
  15.2 0.6 %collective-permute-done.left_ref.lower_ref = f32[1024,128]{1,0:T(8,128)S(1)} collective-permute-done((f32[1024,128]{1,0:T(8,128)}, f32[1024,128]{1,0:T(8,128)S(1)}, u32[]{:S(2)}, u32[]{:S(2)}) %collective-permute-start) | collective-permute-done | bytes 524320 | tf_op jit(solution)/shard_map/ppermute | solution.py:218
  15.8 0.5 %cross_gram.1 = (f32[64,128]{1,0:T(8,128)S(1)}, f32[64,128]{1,0:T(8,128)S(1)}) custom-call(f32[1024,128]{1,0:T(8,128)S(1)} %collective-permute-done.left_ref.lower_ref, f32[1024,128]{1,0:T(8,128)S(1)} %copy-done.1), custom_call_target="tpu_custom_call" | custom-call | tf_op jit(solution)/shard_map/cross_gram/pallas_call | solution.py:266
  16.7 0.8 %collective-permute-done.1 = f32[64,128]{1,0:T(8,128)S(1)} collective-permute-done((f32[64,128]{1,0:T(8,128)S(1)}, f32[64,128]{1,0:T(8,128)S(1)}, u32[]{:S(2)}, u32[]{:S(2)}) %collective-permute-start.1) | collective-permute-done | bytes 32800 | tf_op jit(solution)/shard_map/ppermute | solution.py:233
  17.9 2.8 %collective-permute-start.2 = (f32[64,128]{1,0:T(8,128)S(1)}, f32[64,128]{1,0:T(8,128)S(1)}, u32[]{:S(2)}, u32[]{:S(2)}) collective-permute-start(f32[64,128]{1,0:T(8,128)S(1)} %add.30), channel_id=1, source_target_pairs={{0,8},{1,9},{2,10},{3,11},{4,12},{5,13},{6,14},{7,15},{8,0},{9,1},... | collective-permute-start | bytes 98312 | tf_op jit(solution)/shard_map/ppermute | solution.py:233
  20.7 1.5 %collective-permute-start.11 = (f32[128,128]{1,0:T(8,128)S(1)}, f32[128,128]{1,0:T(8,128)S(1)}, u32[]{:S(2)}, u32[]{:S(2)}) collective-permute-start(f32[128,128]{1,0:T(8,128)S(1)} %add.35.own_ref), channel_id=1, source_target_pairs={{16,0},{0,16},{17,1},{1,17},{18,2},{2,18},{19,3},{3,19},{20,4},{4,... | collective-permute-start | bytes 196616 | tf_op jit(solution)/shard_map/ppermute | solution.py:218
  22.2 0.5 %collective-permute-done.2 = f32[64,128]{1,0:T(8,128)S(1)} collective-permute-done((f32[64,128]{1,0:T(8,128)S(1)}, f32[64,128]{1,0:T(8,128)S(1)}, u32[]{:S(2)}, u32[]{:S(2)}) %collective-permute-start.2) | collective-permute-done | bytes 32800 | tf_op jit(solution)/shard_map/ppermute | solution.py:233
  22.8 2.6 %collective-permute-start.10 = (f32[64,128]{1,0:T(8,128)S(1)}, f32[64,128]{1,0:T(8,128)S(1)}, u32[]{:S(2)}, u32[]{:S(2)}) collective-permute-start(f32[64,128]{1,0:T(8,128)S(1)} %add.36), channel_id=1, source_target_pairs={{0,6},{1,7},{2,4},{3,5},{4,2},{5,3},{6,0},{7,1},{8,14},{9,15},{10,... | collective-permute-start | bytes 98312 | tf_op jit(solution)/shard_map/ppermute | solution.py:233
  25.4 0.4 %collective-permute-start.9 = (f32[64,128]{1,0:T(8,128)S(1)}, f32[64,128]{1,0:T(8,128)S(1)}, u32[]{:S(2)}, u32[]{:S(2)}) collective-permute-start(f32[64,128]{1,0:T(8,128)S(1)} %add.36), channel_id=1, source_target_pairs={{0,4},{1,5},{2,6},{3,7},{4,0},{5,1},{6,2},{7,3},{8,12},{9,13},{10,... | collective-permute-start | bytes 98312 | tf_op jit(solution)/shard_map/ppermute | solution.py:233
  25.9 0.4 %collective-permute-start.8 = (f32[64,128]{1,0:T(8,128)S(1)}, f32[64,128]{1,0:T(8,128)S(1)}, u32[]{:S(2)}, u32[]{:S(2)}) collective-permute-start(f32[64,128]{1,0:T(8,128)S(1)} %add.36), channel_id=1, source_target_pairs={{0,2},{1,3},{2,0},{3,1},{4,6},{5,7},{6,4},{7,5},{8,10},{9,11},{10,... | collective-permute-start | bytes 98312 | tf_op jit(solution)/shard_map/ppermute | solution.py:233
  26.3 2.5 %leaf_roots.1 = (f32[2,128,128]{2,1,0:T(8,128)S(1)}, bf16[2,2,256,256]{3,2,1,0:T(8,128)(2,1)S(1)}, bf16[2,256,512]{2,1,0:T(8,128)(2,1)S(1)}, bf16[2,256,256]{2,1,0:T(8,128)(2,1)S(1)}) custom-call(f32[128,128]{1,0:T(8,128)S(1)} %collective-permute-done.11.lower_ref, f32[128,128]{1,0:T(8,128)S(1)} %add.35.own_ref, f32[256,128]{1,0:T(8,128)S(1)} %bitcast.1), custom_call_target="tpu_custom_call" | custom-call | tf_op jit(solution)/shard_map/leaf_roots/pallas_call | solution.py:278
  28.7 0.6 %collective-permute-done.9 = f32[64,128]{1,0:T(8,128)S(1)} collective-permute-done((f32[64,128]{1,0:T(8,128)S(1)}, f32[64,128]{1,0:T(8,128)S(1)}, u32[]{:S(2)}, u32[]{:S(2)}) %collective-permute-start.9) | collective-permute-done | bytes 32800 | tf_op jit(solution)/shard_map/ppermute | solution.py:233
  29.3 0.4 %collective-permute-done.8 = f32[64,128]{1,0:T(8,128)S(1)} collective-permute-done((f32[64,128]{1,0:T(8,128)S(1)}, f32[64,128]{1,0:T(8,128)S(1)}, u32[]{:S(2)}, u32[]{:S(2)}) %collective-permute-start.8) | collective-permute-done | bytes 32800 | tf_op jit(solution)/shard_map/ppermute | solution.py:233
  29.9 1.2 %collective-permute-done.12.theirs_ref = f32[64,128]{1,0:T(8,128)S(1)} collective-permute-done((f32[64,128]{1,0:T(8,128)S(1)}, f32[64,128]{1,0:T(8,128)S(1)}, u32[]{:S(2)}, u32[]{:S(2)}) %collective-permute-start.12) | collective-permute-done | bytes 32800 | tf_op jit(solution)/shard_map/ppermute | solution.py:233
  31.1 4.0 %merge.1 = (f32[128,128]{1,0:T(8,128)}, f32[1024,128]{1,0:T(8,128)}) custom-call(f32[64,128]{1,0:T(8,128)S(1)} %add_add_fusion.1.mine_ref, f32[64,128]{1,0:T(8,128)S(1)} %collective-permute-done.12.theirs_ref, f32[2,128,128]{2,1,0:T(8,128)S(1)} %get-tuple-element.39.f_ref, bf16[2,2,256,256]{3,2,1,0:T(8,128)(2,1)S(1)} %get-tuple-element.40.left_ref, ...), custom_call_target="tpu_custom_call" | custom-call | tf_op jit(solution)/shard_map/merge/pallas_call | solution.py:299
  (19 shorter events, 0.9 us)
Async XLA Ops:
  0.6 15.1 %collective-permute-start = (f32[1024,128]{1,0:T(8,128)}, f32[1024,128]{1,0:T(8,128)S(1)}, u32[]{:S(2)}, u32[]{:S(2)}) collective-permute-start(f32[1024,128]{1,0:T(8,128)} %own_ref.3), channel_id=1, source_target_pairs={{16,0},{0,16},{17,1},{1,17},{18,2},{2,18},{19,3},{3,19},{20,4},{4,... | collective-permute-start | bytes 1572872 | tf_op jit(solution)/shard_map/ppermute | solution.py:218
  3.6 1.1 %copy-start = (f32[1024,128]{1,0:T(8,128)S(1)}, f32[1024,128]{1,0:T(8,128)}, u32[]{:S(2)}) copy-start(f32[1024,128]{1,0:T(8,128)} %own_ref.3) | copy-start | bytes 1572868
  4.7 11.1 %copy-start.1 = (f32[1024,128]{1,0:T(8,128)S(1)}, f32[1024,128]{1,0:T(8,128)}, u32[]{:S(2)}) copy-start(f32[1024,128]{1,0:T(8,128)} %own_ref.3) | copy-start | bytes 1572868
  5.2 5.9 %collective-permute-start.5 = (f32[128,128]{1,0:T(8,128)S(1)}, f32[128,128]{1,0:T(8,128)S(1)}, u32[]{:S(2)}, u32[]{:S(2)}) collective-permute-start(f32[128,128]{1,0:T(8,128)S(1)} %own_gram.1), channel_id=1, source_target_pairs={{0,6},{1,7},{2,4},{3,5},{4,2},{5,3},{6,0},{7,1},{8,14},{9,15},{10,... | collective-permute-start | bytes 196616 | tf_op jit(solution)/shard_map/ppermute | solution.py:233
  7.8 4.3 %collective-permute-start.4 = (f32[128,128]{1,0:T(8,128)S(1)}, f32[128,128]{1,0:T(8,128)S(1)}, u32[]{:S(2)}, u32[]{:S(2)}) collective-permute-start(f32[128,128]{1,0:T(8,128)S(1)} %own_gram.1), channel_id=1, source_target_pairs={{0,4},{1,5},{2,6},{3,7},{4,0},{5,1},{6,2},{7,3},{8,12},{9,13},{10,... | collective-permute-start | bytes 196616 | tf_op jit(solution)/shard_map/ppermute | solution.py:233
  8.3 4.3 %collective-permute-start.3 = (f32[128,128]{1,0:T(8,128)S(1)}, f32[128,128]{1,0:T(8,128)S(1)}, u32[]{:S(2)}, u32[]{:S(2)}) collective-permute-start(f32[128,128]{1,0:T(8,128)S(1)} %own_gram.1), channel_id=1, source_target_pairs={{0,2},{1,3},{2,0},{3,1},{4,6},{5,7},{6,4},{7,5},{8,10},{9,11},{10,... | collective-permute-start | bytes 196616 | tf_op jit(solution)/shard_map/ppermute | solution.py:233
  12.5 5.2 %collective-permute-start.6 = (f32[128,128]{1,0:T(8,128)S(1)}, f32[128,128]{1,0:T(8,128)S(1)}, u32[]{:S(2)}, u32[]{:S(2)}) collective-permute-start(f32[128,128]{1,0:T(8,128)S(1)} %add_add_fusion), channel_id=1, source_target_pairs={{0,8},{1,9},{2,10},{3,11},{4,12},{5,13},{6,14},{7,15},{8,0},{9,1},... | collective-permute-start | bytes 196616 | tf_op jit(solution)/shard_map/ppermute | solution.py:233
  16.3 1.3 %collective-permute-start.1 = (f32[64,128]{1,0:T(8,128)S(1)}, f32[64,128]{1,0:T(8,128)S(1)}, u32[]{:S(2)}, u32[]{:S(2)}) collective-permute-start(f32[64,128]{1,0:T(8,128)S(1)} %get-tuple-element.25), channel_id=1, source_target_pairs={{0,1},{1,0},{2,3},{3,2},{4,5},{5,4},{6,7},{7,6},{8,9},{9,8},{10,11... | collective-permute-start | bytes 98312 | tf_op jit(solution)/shard_map/ppermute | solution.py:233
  17.8 8.5 %copy-start.2 = (f32[1,256,128]{2,1,0:T(8,128)S(1)}, f32[1,256,128]{2,1,0:T(8,128)}, u32[]{:S(2)}) copy-start(f32[1,256,128]{2,1,0:T(8,128)} %param.3) | copy-start | bytes 393220
  17.8 2.9 %collective-permute-start.7 = (f32[128,128]{1,0:T(8,128)S(1)}, f32[128,128]{1,0:T(8,128)S(1)}, u32[]{:S(2)}, u32[]{:S(2)}) collective-permute-start(f32[128,128]{1,0:T(8,128)S(1)} %add.34), channel_id=1, source_target_pairs={{0,1},{1,0},{2,3},{3,2},{4,5},{5,4},{6,7},{7,6},{8,9},{9,8},{10,11... | collective-permute-start | bytes 196616 | tf_op jit(solution)/shard_map/ppermute | solution.py:233
  17.9 4.9 %collective-permute-start.2 = (f32[64,128]{1,0:T(8,128)S(1)}, f32[64,128]{1,0:T(8,128)S(1)}, u32[]{:S(2)}, u32[]{:S(2)}) collective-permute-start(f32[64,128]{1,0:T(8,128)S(1)} %add.30), channel_id=1, source_target_pairs={{0,8},{1,9},{2,10},{3,11},{4,12},{5,13},{6,14},{7,15},{8,0},{9,1},... | collective-permute-start | bytes 98312 | tf_op jit(solution)/shard_map/ppermute | solution.py:233
  20.7 5.6 %collective-permute-start.11 = (f32[128,128]{1,0:T(8,128)S(1)}, f32[128,128]{1,0:T(8,128)S(1)}, u32[]{:S(2)}, u32[]{:S(2)}) collective-permute-start(f32[128,128]{1,0:T(8,128)S(1)} %add.35.own_ref), channel_id=1, source_target_pairs={{16,0},{0,16},{17,1},{1,17},{18,2},{2,18},{19,3},{3,19},{20,4},{4,... | collective-permute-start | bytes 196616 | tf_op jit(solution)/shard_map/ppermute | solution.py:218
  22.8 6.0 %collective-permute-start.10 = (f32[64,128]{1,0:T(8,128)S(1)}, f32[64,128]{1,0:T(8,128)S(1)}, u32[]{:S(2)}, u32[]{:S(2)}) collective-permute-start(f32[64,128]{1,0:T(8,128)S(1)} %add.36), channel_id=1, source_target_pairs={{0,6},{1,7},{2,4},{3,5},{4,2},{5,3},{6,0},{7,1},{8,14},{9,15},{10,... | collective-permute-start | bytes 98312 | tf_op jit(solution)/shard_map/ppermute | solution.py:233
  25.4 3.9 %collective-permute-start.9 = (f32[64,128]{1,0:T(8,128)S(1)}, f32[64,128]{1,0:T(8,128)S(1)}, u32[]{:S(2)}, u32[]{:S(2)}) collective-permute-start(f32[64,128]{1,0:T(8,128)S(1)} %add.36), channel_id=1, source_target_pairs={{0,4},{1,5},{2,6},{3,7},{4,0},{5,1},{6,2},{7,3},{8,12},{9,13},{10,... | collective-permute-start | bytes 98312 | tf_op jit(solution)/shard_map/ppermute | solution.py:233
  25.9 3.9 %collective-permute-start.8 = (f32[64,128]{1,0:T(8,128)S(1)}, f32[64,128]{1,0:T(8,128)S(1)}, u32[]{:S(2)}, u32[]{:S(2)}) collective-permute-start(f32[64,128]{1,0:T(8,128)S(1)} %add.36), channel_id=1, source_target_pairs={{0,2},{1,3},{2,0},{3,1},{4,6},{5,7},{6,4},{7,5},{8,10},{9,11},{10,... | collective-permute-start | bytes 98312 | tf_op jit(solution)/shard_map/ppermute | solution.py:233
  29.8 1.3 %collective-permute-start.12 = (f32[64,128]{1,0:T(8,128)S(1)}, f32[64,128]{1,0:T(8,128)S(1)}, u32[]{:S(2)}, u32[]{:S(2)}) collective-permute-start(f32[64,128]{1,0:T(8,128)S(1)} %add_add_fusion.1.mine_ref), channel_id=1, source_target_pairs={{0,1},{1,0},{2,3},{3,2},{4,5},{5,4},{6,7},{7,6},{8,9},{9,8},{10,11... | collective-permute-start | bytes 98312 | tf_op jit(solution)/shard_map/ppermute | solution.py:233

commit v7 on v5

--- a/solution.py
+++ b/solution.py
@@ -230,7 +230,9 @@
 def received(part, axis, bits):
     flips = [bits[0]] if len(bits) == 1 else [bits[0], bits[1], bits[0] | bits[1]]
     size = lax.axis_size(axis)
-    return [lax.ppermute(part, axis, [(i, i ^ flip) for i in range(size)]) for flip in flips]
+    order = [2, 1, 0] if len(flips) == 3 else [0]
+    moved = {at: lax.ppermute(part, axis, [(i, i ^ flips[at]) for i in range(size)]) for at in order}
+    return [moved[at] for at in range(len(flips))]
 
 
 def total(part, others):

time: 35.2 us -> 35.2 us (level)
  no operation moved by 1% of the time
where the time goes in v7:
time: 35.2 us; the launch traced here: 35 us
  starting transfers between devices  17.2 us (49%)
  waiting for transfers between devices  8.16 us (23%)
  Pallas kernels  7.77 us (22%)
  local copies, waits for them, and re-layouts  1.08 us (3%)
  between operations  0.73 us (2%)
    ppermute x11, starting transfers between devices, received(): lax.ppermute(part, axis, [(i, i ^ flips[at]) for i in range(size)])  12.7 us
    ppermute x11, waiting for transfers between devices, received(): lax.ppermute(part, axis, [(i, i ^ flips[at]) for i in range(size)])  7.58 us
    ppermute x2, starting transfers between devices, passed_along(): return lax.ppermute(block, axis, route)  4.55 us
    pallas_call x1, Pallas kernels, one_merge(): call(merge_kernel, 'merge', [shape(n, n), shape(rows, n)], in_specs=[IN_V...  3.98 us
    pallas_call x1, Pallas kernels, one_merge(): call(leaf_kernel, 'leaf_roots', [shape(2, n, n), shape(2, 2, 2 * n, 2 * n...  2.45 us
    unnamed x6, local copies, waits for them, and re-layouts  1.08 us
  transfers between devices with their start and end apart: 13, of which 10 were waited for; matrix products, arithmetic and copies ran while one was open for 0% of the time, Pallas kernels for 11%

profile of v7, /device:TPU:0, one launch (start us, length us, event | category | flops | bytes accessed | tf_op | source)
XLA Modules:
  0.0 35.0 jit_solution(11797884674136573680)
XLA Ops:
  0.6 3.0 %collective-permute-start = (f32[1024,128]{1,0:T(8,128)}, f32[1024,128]{1,0:T(8,128)S(1)}, u32[]{:S(2)}, u32[]{:S(2)}) collective-permute-start(f32[1024,128]{1,0:T(8,128)} %own_ref.3), channel_id=1, source_target_pairs={{16,0},{0,16},{17,1},{1,17},{18,2},{2,18},{19,3},{3,19},{20,4},{4,... | collective-permute-start | bytes 1572872 | tf_op jit(solution)/shard_map/ppermute | solution.py:218
  3.6 1.1 %copy-done = f32[1024,128]{1,0:T(8,128)S(1)} copy-done((f32[1024,128]{1,0:T(8,128)S(1)}, f32[1024,128]{1,0:T(8,128)}, u32[]{:S(2)}) %copy-start) | copy-done | bytes 524312
  4.7 0.5 %own_gram.1 = f32[128,128]{1,0:T(8,128)S(1)} custom-call(f32[1024,128]{1,0:T(8,128)S(1)} %copy-done), custom_call_target="tpu_custom_call" | custom-call | tf_op jit(solution)/shard_map/own_gram/pallas_call | solution.py:265
  5.2 2.6 %collective-permute-start.5 = (f32[128,128]{1,0:T(8,128)S(1)}, f32[128,128]{1,0:T(8,128)S(1)}, u32[]{:S(2)}, u32[]{:S(2)}) collective-permute-start(f32[128,128]{1,0:T(8,128)S(1)} %own_gram.1), channel_id=1, source_target_pairs={{0,6},{1,7},{2,4},{3,5},{4,2},{5,3},{6,0},{7,1},{8,14},{9,15},{10,... | collective-permute-start | bytes 196616 | tf_op jit(solution)/shard_map/ppermute | solution.py:234
  7.8 0.4 %collective-permute-start.4 = (f32[128,128]{1,0:T(8,128)S(1)}, f32[128,128]{1,0:T(8,128)S(1)}, u32[]{:S(2)}, u32[]{:S(2)}) collective-permute-start(f32[128,128]{1,0:T(8,128)S(1)} %own_gram.1), channel_id=1, source_target_pairs={{0,4},{1,5},{2,6},{3,7},{4,0},{5,1},{6,2},{7,3},{8,12},{9,13},{10,... | collective-permute-start | bytes 196616 | tf_op jit(solution)/shard_map/ppermute | solution.py:234
  8.3 0.5 %collective-permute-start.3 = (f32[128,128]{1,0:T(8,128)S(1)}, f32[128,128]{1,0:T(8,128)S(1)}, u32[]{:S(2)}, u32[]{:S(2)}) collective-permute-start(f32[128,128]{1,0:T(8,128)S(1)} %own_gram.1), channel_id=1, source_target_pairs={{0,2},{1,3},{2,0},{3,1},{4,6},{5,7},{6,4},{7,5},{8,10},{9,11},{10,... | collective-permute-start | bytes 196616 | tf_op jit(solution)/shard_map/ppermute | solution.py:234
  8.8 2.4 %collective-permute-done.5 = f32[128,128]{1,0:T(8,128)S(1)} collective-permute-done((f32[128,128]{1,0:T(8,128)S(1)}, f32[128,128]{1,0:T(8,128)S(1)}, u32[]{:S(2)}, u32[]{:S(2)}) %collective-permute-start.5) | collective-permute-done | bytes 65568 | tf_op jit(solution)/shard_map/ppermute | solution.py:234
  11.1 0.9 %collective-permute-done.4 = f32[128,128]{1,0:T(8,128)S(1)} collective-permute-done((f32[128,128]{1,0:T(8,128)S(1)}, f32[128,128]{1,0:T(8,128)S(1)}, u32[]{:S(2)}, u32[]{:S(2)}) %collective-permute-start.4) | collective-permute-done | bytes 65568 | tf_op jit(solution)/shard_map/ppermute | solution.py:234
  12.1 0.4 %collective-permute-done.3 = f32[128,128]{1,0:T(8,128)S(1)} collective-permute-done((f32[128,128]{1,0:T(8,128)S(1)}, f32[128,128]{1,0:T(8,128)S(1)}, u32[]{:S(2)}, u32[]{:S(2)}) %collective-permute-start.3) | collective-permute-done | bytes 65568 | tf_op jit(solution)/shard_map/ppermute | solution.py:234
  12.5 2.7 %collective-permute-start.6 = (f32[128,128]{1,0:T(8,128)S(1)}, f32[128,128]{1,0:T(8,128)S(1)}, u32[]{:S(2)}, u32[]{:S(2)}) collective-permute-start(f32[128,128]{1,0:T(8,128)S(1)} %add_add_fusion), channel_id=1, source_target_pairs={{0,8},{1,9},{2,10},{3,11},{4,12},{5,13},{6,14},{7,15},{8,0},{9,1},... | collective-permute-start | bytes 196616 | tf_op jit(solution)/shard_map/ppermute | solution.py:234
  15.2 0.6 %collective-permute-done.left_ref.lower_ref = f32[1024,128]{1,0:T(8,128)S(1)} collective-permute-done((f32[1024,128]{1,0:T(8,128)}, f32[1024,128]{1,0:T(8,128)S(1)}, u32[]{:S(2)}, u32[]{:S(2)}) %collective-permute-start) | collective-permute-done | bytes 524320 | tf_op jit(solution)/shard_map/ppermute | solution.py:218
  15.8 0.5 %cross_gram.1 = (f32[64,128]{1,0:T(8,128)S(1)}, f32[64,128]{1,0:T(8,128)S(1)}) custom-call(f32[1024,128]{1,0:T(8,128)S(1)} %collective-permute-done.left_ref.lower_ref, f32[1024,128]{1,0:T(8,128)S(1)} %copy-done.1), custom_call_target="tpu_custom_call" | custom-call | tf_op jit(solution)/shard_map/cross_gram/pallas_call | solution.py:268
  16.7 0.8 %collective-permute-done.1 = f32[64,128]{1,0:T(8,128)S(1)} collective-permute-done((f32[64,128]{1,0:T(8,128)S(1)}, f32[64,128]{1,0:T(8,128)S(1)}, u32[]{:S(2)}, u32[]{:S(2)}) %collective-permute-start.1) | collective-permute-done | bytes 32800 | tf_op jit(solution)/shard_map/ppermute | solution.py:234
  17.9 2.8 %collective-permute-start.2 = (f32[64,128]{1,0:T(8,128)S(1)}, f32[64,128]{1,0:T(8,128)S(1)}, u32[]{:S(2)}, u32[]{:S(2)}) collective-permute-start(f32[64,128]{1,0:T(8,128)S(1)} %add.30), channel_id=1, source_target_pairs={{0,8},{1,9},{2,10},{3,11},{4,12},{5,13},{6,14},{7,15},{8,0},{9,1},... | collective-permute-start | bytes 98312 | tf_op jit(solution)/shard_map/ppermute | solution.py:234
  20.7 1.5 %collective-permute-start.11 = (f32[128,128]{1,0:T(8,128)S(1)}, f32[128,128]{1,0:T(8,128)S(1)}, u32[]{:S(2)}, u32[]{:S(2)}) collective-permute-start(f32[128,128]{1,0:T(8,128)S(1)} %add.35.own_ref), channel_id=1, source_target_pairs={{16,0},{0,16},{17,1},{1,17},{18,2},{2,18},{19,3},{3,19},{20,4},{4,... | collective-permute-start | bytes 196616 | tf_op jit(solution)/shard_map/ppermute | solution.py:218
  22.2 0.5 %collective-permute-done.2 = f32[64,128]{1,0:T(8,128)S(1)} collective-permute-done((f32[64,128]{1,0:T(8,128)S(1)}, f32[64,128]{1,0:T(8,128)S(1)}, u32[]{:S(2)}, u32[]{:S(2)}) %collective-permute-start.2) | collective-permute-done | bytes 32800 | tf_op jit(solution)/shard_map/ppermute | solution.py:234
  22.8 2.6 %collective-permute-start.10 = (f32[64,128]{1,0:T(8,128)S(1)}, f32[64,128]{1,0:T(8,128)S(1)}, u32[]{:S(2)}, u32[]{:S(2)}) collective-permute-start(f32[64,128]{1,0:T(8,128)S(1)} %add.36), channel_id=1, source_target_pairs={{0,6},{1,7},{2,4},{3,5},{4,2},{5,3},{6,0},{7,1},{8,14},{9,15},{10,... | collective-permute-start | bytes 98312 | tf_op jit(solution)/shard_map/ppermute | solution.py:234
  25.4 0.4 %collective-permute-start.9 = (f32[64,128]{1,0:T(8,128)S(1)}, f32[64,128]{1,0:T(8,128)S(1)}, u32[]{:S(2)}, u32[]{:S(2)}) collective-permute-start(f32[64,128]{1,0:T(8,128)S(1)} %add.36), channel_id=1, source_target_pairs={{0,4},{1,5},{2,6},{3,7},{4,0},{5,1},{6,2},{7,3},{8,12},{9,13},{10,... | collective-permute-start | bytes 98312 | tf_op jit(solution)/shard_map/ppermute | solution.py:234
  25.9 0.4 %collective-permute-start.8 = (f32[64,128]{1,0:T(8,128)S(1)}, f32[64,128]{1,0:T(8,128)S(1)}, u32[]{:S(2)}, u32[]{:S(2)}) collective-permute-start(f32[64,128]{1,0:T(8,128)S(1)} %add.36), channel_id=1, source_target_pairs={{0,2},{1,3},{2,0},{3,1},{4,6},{5,7},{6,4},{7,5},{8,10},{9,11},{10,... | collective-permute-start | bytes 98312 | tf_op jit(solution)/shard_map/ppermute | solution.py:234
  26.3 2.4 %leaf_roots.1 = (f32[2,128,128]{2,1,0:T(8,128)S(1)}, bf16[2,2,256,256]{3,2,1,0:T(8,128)(2,1)S(1)}, bf16[2,256,512]{2,1,0:T(8,128)(2,1)S(1)}, bf16[2,256,256]{2,1,0:T(8,128)(2,1)S(1)}) custom-call(f32[128,128]{1,0:T(8,128)S(1)} %collective-permute-done.11.lower_ref, f32[128,128]{1,0:T(8,128)S(1)} %add.35.own_ref, f32[256,128]{1,0:T(8,128)S(1)} %bitcast.1), custom_call_target="tpu_custom_call" | custom-call | tf_op jit(solution)/shard_map/leaf_roots/pallas_call | solution.py:280
  28.7 0.6 %collective-permute-done.9 = f32[64,128]{1,0:T(8,128)S(1)} collective-permute-done((f32[64,128]{1,0:T(8,128)S(1)}, f32[64,128]{1,0:T(8,128)S(1)}, u32[]{:S(2)}, u32[]{:S(2)}) %collective-permute-start.9) | collective-permute-done | bytes 32800 | tf_op jit(solution)/shard_map/ppermute | solution.py:234
  29.3 0.4 %collective-permute-done.8 = f32[64,128]{1,0:T(8,128)S(1)} collective-permute-done((f32[64,128]{1,0:T(8,128)S(1)}, f32[64,128]{1,0:T(8,128)S(1)}, u32[]{:S(2)}, u32[]{:S(2)}) %collective-permute-start.8) | collective-permute-done | bytes 32800 | tf_op jit(solution)/shard_map/ppermute | solution.py:234
  29.9 1.2 %collective-permute-done.12.theirs_ref = f32[64,128]{1,0:T(8,128)S(1)} collective-permute-done((f32[64,128]{1,0:T(8,128)S(1)}, f32[64,128]{1,0:T(8,128)S(1)}, u32[]{:S(2)}, u32[]{:S(2)}) %collective-permute-start.12) | collective-permute-done | bytes 32800 | tf_op jit(solution)/shard_map/ppermute | solution.py:234
  31.1 4.0 %merge.1 = (f32[128,128]{1,0:T(8,128)}, f32[1024,128]{1,0:T(8,128)}) custom-call(f32[64,128]{1,0:T(8,128)S(1)} %add_add_fusion.1.mine_ref, f32[64,128]{1,0:T(8,128)S(1)} %collective-permute-done.12.theirs_ref, f32[2,128,128]{2,1,0:T(8,128)S(1)} %get-tuple-element.39.f_ref, bf16[2,2,256,256]{3,2,1,0:T(8,128)(2,1)S(1)} %get-tuple-element.40.left_ref, ...), custom_call_target="tpu_custom_call" | custom-call | tf_op jit(solution)/shard_map/merge/pallas_call | solution.py:301
  (19 shorter events, 0.9 us)
Async XLA Ops:
  0.6 15.1 %collective-permute-start = (f32[1024,128]{1,0:T(8,128)}, f32[1024,128]{1,0:T(8,128)S(1)}, u32[]{:S(2)}, u32[]{:S(2)}) collective-permute-start(f32[1024,128]{1,0:T(8,128)} %own_ref.3), channel_id=1, source_target_pairs={{16,0},{0,16},{17,1},{1,17},{18,2},{2,18},{19,3},{3,19},{20,4},{4,... | collective-permute-start | bytes 1572872 | tf_op jit(solution)/shard_map/ppermute | solution.py:218
  3.6 1.1 %copy-start = (f32[1024,128]{1,0:T(8,128)S(1)}, f32[1024,128]{1,0:T(8,128)}, u32[]{:S(2)}) copy-start(f32[1024,128]{1,0:T(8,128)} %own_ref.3) | copy-start | bytes 1572868
  4.7 11.1 %copy-start.1 = (f32[1024,128]{1,0:T(8,128)S(1)}, f32[1024,128]{1,0:T(8,128)}, u32[]{:S(2)}) copy-start(f32[1024,128]{1,0:T(8,128)} %own_ref.3) | copy-start | bytes 1572868
  5.2 5.9 %collective-permute-start.5 = (f32[128,128]{1,0:T(8,128)S(1)}, f32[128,128]{1,0:T(8,128)S(1)}, u32[]{:S(2)}, u32[]{:S(2)}) collective-permute-start(f32[128,128]{1,0:T(8,128)S(1)} %own_gram.1), channel_id=1, source_target_pairs={{0,6},{1,7},{2,4},{3,5},{4,2},{5,3},{6,0},{7,1},{8,14},{9,15},{10,... | collective-permute-start | bytes 196616 | tf_op jit(solution)/shard_map/ppermute | solution.py:234
  7.8 4.3 %collective-permute-start.4 = (f32[128,128]{1,0:T(8,128)S(1)}, f32[128,128]{1,0:T(8,128)S(1)}, u32[]{:S(2)}, u32[]{:S(2)}) collective-permute-start(f32[128,128]{1,0:T(8,128)S(1)} %own_gram.1), channel_id=1, source_target_pairs={{0,4},{1,5},{2,6},{3,7},{4,0},{5,1},{6,2},{7,3},{8,12},{9,13},{10,... | collective-permute-start | bytes 196616 | tf_op jit(solution)/shard_map/ppermute | solution.py:234
  8.3 4.3 %collective-permute-start.3 = (f32[128,128]{1,0:T(8,128)S(1)}, f32[128,128]{1,0:T(8,128)S(1)}, u32[]{:S(2)}, u32[]{:S(2)}) collective-permute-start(f32[128,128]{1,0:T(8,128)S(1)} %own_gram.1), channel_id=1, source_target_pairs={{0,2},{1,3},{2,0},{3,1},{4,6},{5,7},{6,4},{7,5},{8,10},{9,11},{10,... | collective-permute-start | bytes 196616 | tf_op jit(solution)/shard_map/ppermute | solution.py:234
  12.5 5.2 %collective-permute-start.6 = (f32[128,128]{1,0:T(8,128)S(1)}, f32[128,128]{1,0:T(8,128)S(1)}, u32[]{:S(2)}, u32[]{:S(2)}) collective-permute-start(f32[128,128]{1,0:T(8,128)S(1)} %add_add_fusion), channel_id=1, source_target_pairs={{0,8},{1,9},{2,10},{3,11},{4,12},{5,13},{6,14},{7,15},{8,0},{9,1},... | collective-permute-start | bytes 196616 | tf_op jit(solution)/shard_map/ppermute | solution.py:234
  16.3 1.3 %collective-permute-start.1 = (f32[64,128]{1,0:T(8,128)S(1)}, f32[64,128]{1,0:T(8,128)S(1)}, u32[]{:S(2)}, u32[]{:S(2)}) collective-permute-start(f32[64,128]{1,0:T(8,128)S(1)} %get-tuple-element.25), channel_id=1, source_target_pairs={{0,1},{1,0},{2,3},{3,2},{4,5},{5,4},{6,7},{7,6},{8,9},{9,8},{10,11... | collective-permute-start | bytes 98312 | tf_op jit(solution)/shard_map/ppermute | solution.py:234
  17.8 8.5 %copy-start.2 = (f32[1,256,128]{2,1,0:T(8,128)S(1)}, f32[1,256,128]{2,1,0:T(8,128)}, u32[]{:S(2)}) copy-start(f32[1,256,128]{2,1,0:T(8,128)} %param.3) | copy-start | bytes 393220
  17.8 2.9 %collective-permute-start.7 = (f32[128,128]{1,0:T(8,128)S(1)}, f32[128,128]{1,0:T(8,128)S(1)}, u32[]{:S(2)}, u32[]{:S(2)}) collective-permute-start(f32[128,128]{1,0:T(8,128)S(1)} %add.34), channel_id=1, source_target_pairs={{0,1},{1,0},{2,3},{3,2},{4,5},{5,4},{6,7},{7,6},{8,9},{9,8},{10,11... | collective-permute-start | bytes 196616 | tf_op jit(solution)/shard_map/ppermute | solution.py:234
  17.9 4.9 %collective-permute-start.2 = (f32[64,128]{1,0:T(8,128)S(1)}, f32[64,128]{1,0:T(8,128)S(1)}, u32[]{:S(2)}, u32[]{:S(2)}) collective-permute-start(f32[64,128]{1,0:T(8,128)S(1)} %add.30), channel_id=1, source_target_pairs={{0,8},{1,9},{2,10},{3,11},{4,12},{5,13},{6,14},{7,15},{8,0},{9,1},... | collective-permute-start | bytes 98312 | tf_op jit(solution)/shard_map/ppermute | solution.py:234
  20.7 5.6 %collective-permute-start.11 = (f32[128,128]{1,0:T(8,128)S(1)}, f32[128,128]{1,0:T(8,128)S(1)}, u32[]{:S(2)}, u32[]{:S(2)}) collective-permute-start(f32[128,128]{1,0:T(8,128)S(1)} %add.35.own_ref), channel_id=1, source_target_pairs={{16,0},{0,16},{17,1},{1,17},{18,2},{2,18},{19,3},{3,19},{20,4},{4,... | collective-permute-start | bytes 196616 | tf_op jit(solution)/shard_map/ppermute | solution.py:218
  22.8 6.0 %collective-permute-start.10 = (f32[64,128]{1,0:T(8,128)S(1)}, f32[64,128]{1,0:T(8,128)S(1)}, u32[]{:S(2)}, u32[]{:S(2)}) collective-permute-start(f32[64,128]{1,0:T(8,128)S(1)} %add.36), channel_id=1, source_target_pairs={{0,6},{1,7},{2,4},{3,5},{4,2},{5,3},{6,0},{7,1},{8,14},{9,15},{10,... | collective-permute-start | bytes 98312 | tf_op jit(solution)/shard_map/ppermute | solution.py:234
  25.4 3.9 %collective-permute-start.9 = (f32[64,128]{1,0:T(8,128)S(1)}, f32[64,128]{1,0:T(8,128)S(1)}, u32[]{:S(2)}, u32[]{:S(2)}) collective-permute-start(f32[64,128]{1,0:T(8,128)S(1)} %add.36), channel_id=1, source_target_pairs={{0,4},{1,5},{2,6},{3,7},{4,0},{5,1},{6,2},{7,3},{8,12},{9,13},{10,... | collective-permute-start | bytes 98312 | tf_op jit(solution)/shard_map/ppermute | solution.py:234
  25.9 3.9 %collective-permute-start.8 = (f32[64,128]{1,0:T(8,128)S(1)}, f32[64,128]{1,0:T(8,128)S(1)}, u32[]{:S(2)}, u32[]{:S(2)}) collective-permute-start(f32[64,128]{1,0:T(8,128)S(1)} %add.36), channel_id=1, source_target_pairs={{0,2},{1,3},{2,0},{3,1},{4,6},{5,7},{6,4},{7,5},{8,10},{9,11},{10,... | collective-permute-start | bytes 98312 | tf_op jit(solution)/shard_map/ppermute | solution.py:234
  29.8 1.3 %collective-permute-start.12 = (f32[64,128]{1,0:T(8,128)S(1)}, f32[64,128]{1,0:T(8,128)S(1)}, u32[]{:S(2)}, u32[]{:S(2)}) collective-permute-start(f32[64,128]{1,0:T(8,128)S(1)} %add_add_fusion.1.mine_ref), channel_id=1, source_target_pairs={{0,1},{1,0},{2,3},{3,2},{4,5},{5,4},{6,7},{7,6},{8,9},{9,8},{10,11... | collective-permute-start | bytes 98312 | tf_op jit(solution)/shard_map/ppermute | solution.py:234
